TPU v7x, 128 devices: a whole 4x4x4 slice. The times are simulated.
128 devices in a mesh: shot: 16 (over y_hi, x, core), slab: 8 (over y_lo, z).
Axes of the slice: x: 4, y: 4 (y_hi: 2, y_lo: 2; y = y_hi * 2 + y_lo), z: 4, core: 2. Of those that a mesh axis runs over, the one named last changes fastest.
Arguments:
- gradient: float32 [16, 128, 64, 256], P('shot', 'slab'), may hold values from -6 to 6
- illumination: float32 [16, 128, 64, 256], P('shot', 'slab'), may hold values from 0.5 to 4
- u_prev: float32 [16, 128, 64, 256], P('shot', 'slab'), may hold values from -6 to 6
- u_cur: float32 [16, 128, 64, 256], P('shot', 'slab'), may hold values from -6 to 6
- velocity: float32 [4, 128, 64, 256], P(None, 'slab'), may hold values from 2.5 to 4
- offsets: int32 [16], P('shot'), may hold values from 0 to 24
Outputs:
- new_model: float32 [4, 128, 64, 256], P(None, 'slab')
- wavefield: float32 [16, 128, 64, 256], P('shot', 'slab')
Inputs may be any that keep to these rules, and one draw needn't show every extreme that they name: Shot s's aperture covers model slabs offsets[s] to offsets[s] + 128 / 16 - 1.
All inputs are finite; a program needn't handle non-finite values.
Results may differ from a plain program's by a relative error of at most 0.0003.
Values sent between devices are 32-bit elements; how exact they have to be, the bound alone decides.
No kernel may reach another device: no remote copies, remote signals or barrier semaphores. Data moves between devices by JAX's collectives and lax.ppermute only.
A program may use at most 128 MiB of HBM per device.

v0:
```python
import jax
import jax.numpy as jnp
from jax import lax
from jax.sharding import PartitionSpec as P

SPAN = 4


STENCIL = (-205.0 / 72.0, 8.0 / 5.0, -1.0 / 5.0, 8.0 / 315.0, -1.0 / 560.0)
RATE = 0.2
COURANT = 0.11


def from_behind(value, axis, steps):
    count = lax.axis_size(axis)
    pairs = [(source, (source + steps) % count) for source in range(count)]
    return lax.ppermute(value, axis, pairs)


def with_halo(array, sides, width):
    for axis, dim in sides:
        count, length = (lax.axis_size(axis), array.shape[dim])
        up = [(i, (i + 1) % count) for i in range(count - 1)]
        down = [(j, i) for i, j in up]
        last = lax.slice_in_dim(array, length - width, length, axis=dim)
        leading = lax.slice_in_dim(array, 0, width, axis=dim)
        before = lax.ppermute(last, axis, up)
        after = lax.ppermute(leading, axis, down)
        array = jnp.concatenate([before, array, after], axis=dim)
    return array


def laplace_rows(extended):
    rows = extended.shape[1] - 8
    core = extended[:, 4 : 4 + rows]
    widths = core.shape[2]
    depths = core.shape[3]
    padded = jnp.pad(core, ((0, 0), (0, 0), (4, 4), (4, 4)))
    total = 3.0 * STENCIL[0] * core
    for reach in range(1, 5):
        along = (
            extended[:, 4 + reach : 4 + reach + rows] + extended[:, 4 - reach : 4 - reach + rows]
        )
        across = (
            padded[:, :, 4 + reach : 4 + reach + widths, 4 : 4 + depths]
            + padded[:, :, 4 - reach : 4 - reach + widths, 4 : 4 + depths]
        )
        downward = (
            padded[:, :, 4 : 4 + widths, 4 + reach : 4 + reach + depths]
            + padded[:, :, 4 : 4 + widths, 4 - reach : 4 - reach + depths]
        )
        total = total + STENCIL[reach] * (along + across + downward)
    return total


def rotate_forward(stacked, amount, bits):
    for level in range(bits):
        moved = from_behind(stacked, "slab", 1 << level)
        taken = amount >> level & 1 == 1
        stacked = jnp.where(taken[None, :, None, None, None], moved, stacked)
    return stacked


def rotate_back(field, amount, bits, count):
    for level in range(bits):
        moved = from_behind(field, "slab", count - (1 << level))
        taken = amount >> level & 1 == 1
        field = jnp.where(taken[:, None, None, None], moved, field)
    return field


def to_slots(selector, field):
    return jnp.einsum("sq,sxyz->qxyz", selector, field, precision=lax.Precision.HIGHEST)


def on_device(gradient, illumination, u_prev, u_cur, velocity, offsets):
    count = lax.axis_size("slab")
    bits = count.bit_length() - 1
    position = lax.axis_index("slab")
    levels = jnp.arange(SPAN, dtype=jnp.int32)
    remainder = offsets % count
    slot = offsets // count + (position < remainder).astype(jnp.int32)
    selector = (slot[:, None] == levels[None, :]).astype(jnp.float32)
    moved = rotate_forward(jnp.stack([gradient, illumination]), remainder, bits)
    grad_slots = to_slots(selector, moved[0])
    illum_slots = to_slots(selector, moved[1])
    summed_grad, summed_illum = lax.psum((grad_slots, illum_slots), "shot")
    new_model = velocity - RATE * summed_grad / (summed_illum + 1.0)
    local_model = jnp.einsum("sq,qxyz->sxyz", selector, new_model, precision=lax.Precision.HIGHEST)
    aperture_model = rotate_back(local_model, remainder, bits, count)
    squared = (aperture_model * COURANT) ** 2
    previous, current = (u_prev, u_cur)
    for step in range(2):
        extended = with_halo(current, (("slab", 1),), 4)
        following = 2.0 * current - previous + squared * laplace_rows(extended)
        previous, current = (current, following)
    return (new_model, current)


def solution(mesh):
    in_specs = (
        P("shot", "slab", None, None),
        P("shot", "slab", None, None),
        P("shot", "slab", None, None),
        P("shot", "slab", None, None),
        P(None, "slab", None, None),
        P("shot"),
    )
    out_specs = (P(None, "slab", None, None), P("shot", "slab", None, None))
    return jax.shard_map(
        on_device, mesh=mesh, in_specs=in_specs, out_specs=out_specs, check_vma=False
    )
```

profile of v0, /device:TPU:9, one launch (start us, length us, event | category | flops | bytes accessed | tf_op | source)
XLA Modules:
  0.0 438.3 jit_solution(13394094451721310355)
XLA Ops:
  7.2 0.0 all-reduce.5.cloned.1.call-start
  7.2 0.0 copy-start.2
  7.2 0.0 copy-start.3
  7.2 1.8 pad_maximum_fusion
  9.1 1.7 collective-permute-start
  11.4 46.5 %collective-permute-done = f32[2,1,16,64,256]{4,3,2,1,0:T(8,128)S(1)} collective-permute-done((f32[2,1,16,64,256]{4,3,2,1,0:T(8,128)S(1)}, f32[2,1,16,64,256]{4,3,2,1,0:T(8,128)S(1)}, u32[]{:S(2)}, u32[]{:S(2)}) %collective-permute-start) | collective-permute-done | bytes 2097184 | tf_op jit(solution)/shard_map/ppermute | solution.py:17
  57.9 0.0 copy-done.2
  57.9 0.0 copy-done.3
  57.9 0.3 broadcast_select_fusion
  58.2 1.4 collective-permute-start.1
  59.6 46.7 %collective-permute-done.1 = f32[2,1,16,64,256]{4,3,2,1,0:T(8,128)S(1)} collective-permute-done((f32[2,1,16,64,256]{4,3,2,1,0:T(8,128)S(1)}, f32[2,1,16,64,256]{4,3,2,1,0:T(8,128)S(1)}, u32[]{:S(2)}, u32[]{:S(2)}) %collective-permute-start.1) | collective-permute-done | bytes 2097184 | tf_op jit(solution)/shard_map/ppermute | solution.py:17
  106.4 0.6 broadcast_select_fusion.1
  107.0 1.8 collective-permute-start.2
  108.9 43.7 %collective-permute-done.2 = f32[2,1,16,64,256]{4,3,2,1,0:T(8,128)} collective-permute-done((f32[2,1,16,64,256]{4,3,2,1,0:T(8,128)S(1)}, f32[2,1,16,64,256]{4,3,2,1,0:T(8,128)}, u32[]{:S(2)}, u32[]{:S(2)}) %collective-permute-start.2) | collective-permute-done | bytes 2097184 | tf_op jit(solution)/shard_map/ppermute | solution.py:17
  152.5 1.9 broadcast_select_fusion.2
  154.4 0.2 slice_bitcast_fusion.1
  154.6 4.5 %broadcast_multiply_fusion.1 = (f32[4,16,64,256]{3,2,1,0:T(8,128)}, f32[4,16,64,256]{3,2,1,0:T(8,128)}) fusion(f32[16,64,256]{2,1,0:T(8,128)S(1)} %get-tuple-element.4, f32[4]{0:T(128)S(1)} %fusion.66, f32[16,64,256]{2,1,0:T(8,128)S(1)} %get-tuple-element.5), kind=kLoop, calls=%fused_computation.43 | loop fusion | flops 2097152 | bytes 10485776 | tf_op jit(solution)/shard_map/sq,sxyz->qxyz/dot_general | solution.py:73
  159.1 0.0 all-reduce.5.cloned.1.call-update
  159.1 163.9 %all-reduce.5.cloned.1.call-done = (f32[4,16,64,256]{3,2,1,0:T(8,128)}, f32[4,16,64,256]{3,2,1,0:T(8,128)}) async-done(((f32[4,16,64,256]{3,2,1,0:T(8,128)}, f32[4,16,64,256]{3,2,1,0:T(8,128)}), (f32[4,16,64,256]{3,2,1,0:T(8,128)}, f32[4,16,64,256]{3,2,1,0:T(8,128)})) %all-reduce.5.cloned.1.call-update) | async-done | bytes 8388624 | tf_op jit(solution)/shard_map/psum | solution.py:87
  323.0 6.0 %divide_subtract_fusion = f32[4,16,64,256]{3,2,1,0:T(8,128)S(1)} fusion(f32[4,16,64,256]{3,2,1,0:T(8,128)} %param.10, f32[4,16,64,256]{3,2,1,0:T(8,128)} %get-tuple-element.2, f32[4,16,64,256]{3,2,1,0:T(8,128)} %get-tuple-element.3), kind=kLoop, calls=%fused_computation.34 | loop fusion | flops 4194304 | bytes 16777216 | tf_op jit(solution)/shard_map/sub | solution.py:88
  329.1 0.0 copy-start
  329.1 5.4 %fusion = f32[1,16,64,256]{3,0,2,1:T(1,128)S(1)} fusion(f32[4,16,64,256]{3,2,1,0:T(8,128)S(1)} %divide_subtract_fusion, s32[]{:T(128)} %bitcast.1), kind=kOutput, calls=%fused_computation.32 | convolution fusion | flops 12582916 | bytes 5242884 | tf_op jit(solution)/shard_map/sq,qxyz->sxyz/dot_general | solution.py:89
  334.5 0.0 copy-done
  334.5 0.1 copy.10
  334.6 3.6 collective-permute-start.3
  338.2 20.3 %collective-permute-done.3 = f32[1,16,64,256]{3,2,1,0:T(8,128)S(1)} collective-permute-done((f32[1,16,64,256]{3,2,1,0:T(8,128)S(1)}, f32[1,16,64,256]{3,2,1,0:T(8,128)S(1)}, u32[]{:S(2)}, u32[]{:S(2)}) %collective-permute-start.3) | collective-permute-done | bytes 1048608 | tf_op jit(solution)/shard_map/ppermute | solution.py:17
  358.5 0.1 broadcast_select_fusion.3
  358.6 0.0 copy-start.1
  358.6 2.5 collective-permute-start.4
  361.1 20.7 %collective-permute-done.4 = f32[1,16,64,256]{3,2,1,0:T(8,128)S(1)} collective-permute-done((f32[1,16,64,256]{3,2,1,0:T(8,128)S(1)}, f32[1,16,64,256]{3,2,1,0:T(8,128)S(1)}, u32[]{:S(2)}, u32[]{:S(2)}) %collective-permute-start.4) | collective-permute-done | bytes 1048608 | tf_op jit(solution)/shard_map/ppermute | solution.py:17
  381.8 0.1 broadcast_select_fusion.4
  381.9 0.4 collective-permute-start.5
  382.3 0.0 copy-done.1
  382.3 4.1 collective-permute-start.7
  386.4 0.0 copy-start.4
  386.4 5.1 %collective-permute-start.6 = (f32[1,4,64,256]{3,2,1,0:T(8,128)S(1)}, f32[1,4,64,256]{3,2,1,0:T(8,128)S(1)}, u32[]{:S(2)}, u32[]{:S(2)}) collective-permute-start(f32[1,4,64,256]{3,2,1,0:T(8,128)S(1)} %get-tuple-element.8), channel_id=1, source_target_pairs={{1,0},{2,1},{3,2},{4,3},{5,4},{6,5},{7,6},{9,8},{10,9},{11,10},{12... | collective-permute-start | bytes 786440 | tf_op jit(solution)/shard_map/ppermute | solution.py:28
  391.5 18.9 %collective-permute-done.7 = f32[1,4,64,256]{3,2,1,0:T(8,128)S(1)} collective-permute-done((f32[1,4,64,256]{3,2,1,0:T(8,128)S(1)}, f32[1,4,64,256]{3,2,1,0:T(8,128)S(1)}, u32[]{:S(2)}, u32[]{:S(2)}) %collective-permute-start.7) | collective-permute-done | bytes 262176 | tf_op jit(solution)/shard_map/ppermute | solution.py:27
  410.5 0.2 constant_dynamic-update-slice_fusion.1
  410.7 0.0 collective-permute-done.6
  410.8 0.0 collective-permute-done.5
  410.8 0.0 copy-done.4
  410.8 2.5 fusion.35
  413.3 4.1 collective-permute-start.8
  417.4 1.9 collective-permute-start.9
  419.4 1.4 collective-permute-done.8
  420.7 5.9 %collective-permute-done.9 = f32[1,4,64,256]{3,2,1,0:T(8,128)S(1)} collective-permute-done((f32[1,4,64,256]{3,2,1,0:T(8,128)S(1)}, f32[1,4,64,256]{3,2,1,0:T(8,128)S(1)}, u32[]{:S(2)}, u32[]{:S(2)}) %collective-permute-start.9) | collective-permute-done | bytes 262176 | tf_op jit(solution)/shard_map/ppermute | solution.py:27
  426.7 4.8 %fusion.10 = f32[1,16,64,256]{3,2,1,0:T(8,128)} fusion(f32[1,16,64,256]{3,2,1,0:T(8,128)S(1)} %fusion.35, f32[1,4,64,256]{3,2,1,0:T(8,128)S(1)} %collective-permute-done.9, f32[1,4,64,256]{3,2,1,0:T(8,128)S(1)} %collective-permute-done.8, f32[1,16,64,256]{3,2,1,0:T(8,128)S(1)} %copy-done.1, f32[1,16,64,256]{3,2,1,0:T(8,128)S(1)} %collective-permute-done.5, ...), kind=kLoop, calls=%fused_computation.58 | loop fusion | flops 11534336 | bytes 5767169 | tf_op jit(solution)/shard_map/add | solution.py:95
  (5 shorter events, 0.1 us)
Async XLA Ops:
  7.2 315.9 %all-reduce.5.cloned.1.call-start = ((), (), s32[]{:S(2)}) async-start(), calls=%async_computation | async-start | bytes 16777216 | tf_op jit(solution)/shard_map/psum | solution.py:87
  7.2 50.7 %copy-start.2 = (f32[1,16,64,256]{3,2,1,0:T(8,128)S(1)}, f32[1,16,64,256]{3,2,1,0:T(8,128)}, u32[]{:S(2)}) copy-start(f32[1,16,64,256]{3,2,1,0:T(8,128)} %param.7) | copy-start | bytes 3145732
  7.2 50.7 %copy-start.3 = (f32[1,16,64,256]{3,2,1,0:T(8,128)S(1)}, f32[1,16,64,256]{3,2,1,0:T(8,128)}, u32[]{:S(2)}) copy-start(f32[1,16,64,256]{3,2,1,0:T(8,128)} %param.6) | copy-start | bytes 3145732
  9.1 48.8 %collective-permute-start = (f32[2,1,16,64,256]{4,3,2,1,0:T(8,128)S(1)}, f32[2,1,16,64,256]{4,3,2,1,0:T(8,128)S(1)}, u32[]{:S(2)}, u32[]{:S(2)}) collective-permute-start(f32[2,1,16,64,256]{4,3,2,1,0:T(8,128)S(1)} %pad_maximum_fusion), channel_id=1, source_target_pairs={{0,1},{1,2},{2,3},{3,4},{4,5},{5,6},{6,7},{7,0},{8,9},{9,10},{10,1... | collective-permute-start | bytes 6291464 | tf_op jit(solution)/shard_map/ppermute | solution.py:17
  58.2 48.1 %collective-permute-start.1 = (f32[2,1,16,64,256]{4,3,2,1,0:T(8,128)S(1)}, f32[2,1,16,64,256]{4,3,2,1,0:T(8,128)S(1)}, u32[]{:S(2)}, u32[]{:S(2)}) collective-permute-start(f32[2,1,16,64,256]{4,3,2,1,0:T(8,128)S(1)} %broadcast_select_fusion), channel_id=1, source_target_pairs={{0,2},{1,3},{2,4},{3,5},{4,6},{5,7},{6,0},{7,1},{8,10},{9,11},{10,... | collective-permute-start | bytes 6291464 | tf_op jit(solution)/shard_map/ppermute | solution.py:17
  107.0 45.5 %collective-permute-start.2 = (f32[2,1,16,64,256]{4,3,2,1,0:T(8,128)S(1)}, f32[2,1,16,64,256]{4,3,2,1,0:T(8,128)}, u32[]{:S(2)}, u32[]{:S(2)}) collective-permute-start(f32[2,1,16,64,256]{4,3,2,1,0:T(8,128)S(1)} %broadcast_select_fusion.1), channel_id=1, source_target_pairs={{0,4},{1,5},{2,6},{3,7},{4,0},{5,1},{6,2},{7,3},{8,12},{9,13},{10,... | collective-permute-start | bytes 6291464 | tf_op jit(solution)/shard_map/ppermute | solution.py:17
  329.1 5.4 %copy-start = (f32[4,16,64,256]{3,2,1,0:T(8,128)}, f32[4,16,64,256]{3,2,1,0:T(8,128)S(1)}, u32[]{:S(2)}) copy-start(f32[4,16,64,256]{3,2,1,0:T(8,128)S(1)} %divide_subtract_fusion) | copy-start | bytes 12582916
  334.6 23.9 %collective-permute-start.3 = (f32[1,16,64,256]{3,2,1,0:T(8,128)S(1)}, f32[1,16,64,256]{3,2,1,0:T(8,128)S(1)}, u32[]{:S(2)}, u32[]{:S(2)}) collective-permute-start(f32[1,16,64,256]{3,2,1,0:T(8,128)S(1)} %copy.10), channel_id=1, source_target_pairs={{0,7},{1,0},{2,1},{3,2},{4,3},{5,4},{6,5},{7,6},{8,15},{9,8},{10,9... | collective-permute-start | bytes 3145736 | tf_op jit(solution)/shard_map/ppermute | solution.py:17
  358.6 23.7 %copy-start.1 = (f32[1,16,64,256]{3,2,1,0:T(8,128)S(1)}, f32[1,16,64,256]{3,2,1,0:T(8,128)}, u32[]{:S(2)}) copy-start(f32[1,16,64,256]{3,2,1,0:T(8,128)} %param.9) | copy-start | bytes 3145732
  358.6 23.1 %collective-permute-start.4 = (f32[1,16,64,256]{3,2,1,0:T(8,128)S(1)}, f32[1,16,64,256]{3,2,1,0:T(8,128)S(1)}, u32[]{:S(2)}, u32[]{:S(2)}) collective-permute-start(f32[1,16,64,256]{3,2,1,0:T(8,128)S(1)} %broadcast_select_fusion.3), channel_id=1, source_target_pairs={{0,6},{1,7},{2,0},{3,1},{4,2},{5,3},{6,4},{7,5},{8,14},{9,15},{10,... | collective-permute-start | bytes 3145736 | tf_op jit(solution)/shard_map/ppermute | solution.py:17
  381.9 28.9 %collective-permute-start.5 = (f32[1,16,64,256]{3,2,1,0:T(8,128)S(1)}, f32[1,16,64,256]{3,2,1,0:T(8,128)S(1)}, u32[]{:S(2)}, u32[]{:S(2)}) collective-permute-start(f32[1,16,64,256]{3,2,1,0:T(8,128)S(1)} %broadcast_select_fusion.4), channel_id=1, source_target_pairs={{0,4},{1,5},{2,6},{3,7},{4,0},{5,1},{6,2},{7,3},{8,12},{9,13},{10,... | collective-permute-start | bytes 3145736 | tf_op jit(solution)/shard_map/ppermute | solution.py:17
  382.3 28.1 %collective-permute-start.7 = (f32[1,4,64,256]{3,2,1,0:T(8,128)S(1)}, f32[1,4,64,256]{3,2,1,0:T(8,128)S(1)}, u32[]{:S(2)}, u32[]{:S(2)}) collective-permute-start(f32[1,4,64,256]{3,2,1,0:T(8,128)S(1)} %get-tuple-element.9), channel_id=1, source_target_pairs={{0,1},{1,2},{2,3},{3,4},{4,5},{5,6},{6,7},{8,9},{9,10},{10,11},{11... | collective-permute-start | bytes 786440 | tf_op jit(solution)/shard_map/ppermute | solution.py:27
  386.4 24.4 %copy-start.4 = (f32[1,16,64,256]{3,2,1,0:T(8,128)S(1)}, f32[1,16,64,256]{3,2,1,0:T(8,128)}, u32[]{:S(2)}) copy-start(f32[1,16,64,256]{3,2,1,0:T(8,128)} %param.8) | copy-start | bytes 3145732
  386.4 24.3 %collective-permute-start.6 = (f32[1,4,64,256]{3,2,1,0:T(8,128)S(1)}, f32[1,4,64,256]{3,2,1,0:T(8,128)S(1)}, u32[]{:S(2)}, u32[]{:S(2)}) collective-permute-start(f32[1,4,64,256]{3,2,1,0:T(8,128)S(1)} %get-tuple-element.8), channel_id=1, source_target_pairs={{1,0},{2,1},{3,2},{4,3},{5,4},{6,5},{7,6},{9,8},{10,9},{11,10},{12... | collective-permute-start | bytes 786440 | tf_op jit(solution)/shard_map/ppermute | solution.py:28
  413.3 7.4 %collective-permute-start.8 = (f32[1,4,64,256]{3,2,1,0:T(8,128)S(1)}, f32[1,4,64,256]{3,2,1,0:T(8,128)S(1)}, u32[]{:S(2)}, u32[]{:S(2)}) collective-permute-start(f32[1,4,64,256]{3,2,1,0:T(8,128)S(1)} %get-tuple-element.6), channel_id=1, source_target_pairs={{1,0},{2,1},{3,2},{4,3},{5,4},{6,5},{7,6},{9,8},{10,9},{11,10},{12... | collective-permute-start | bytes 786440 | tf_op jit(solution)/shard_map/ppermute | solution.py:28
  417.4 9.2 %collective-permute-start.9 = (f32[1,4,64,256]{3,2,1,0:T(8,128)S(1)}, f32[1,4,64,256]{3,2,1,0:T(8,128)S(1)}, u32[]{:S(2)}, u32[]{:S(2)}) collective-permute-start(f32[1,4,64,256]{3,2,1,0:T(8,128)S(1)} %get-tuple-element.7), channel_id=1, source_target_pairs={{0,1},{1,2},{2,3},{3,4},{4,5},{5,6},{6,7},{8,9},{9,10},{10,11},{11... | collective-permute-start | bytes 786440 | tf_op jit(solution)/shard_map/ppermute | solution.py:27
Sparse Core Ops, SparseCore 0:
  159.3 163.7 all-reduce.4
where the time goes:
time: 447 us; the launch traced here: 438 us
  waiting for transfers between devices  368 us (82%)
  starting transfers between devices  26.6 us (6%)
  other arithmetic  22.8 us (5%)
  between operations  14.9 us (3%)
  matrix products  5.39 us (1%)
    ppermute x6, waiting for transfers between devices, from_behind(): return lax.ppermute(value, axis, pairs)  178 us
    psum x1, waiting for transfers between devices, on_device(): summed_grad, summed_illum = lax.psum((grad_slots, illum_slots), 'shot')  164 us
    ppermute x2, waiting for transfers between devices, with_halo(): before = lax.ppermute(last, axis, up)  24.9 us
    ppermute x6, starting transfers between devices, from_behind(): return lax.ppermute(value, axis, pairs)  11.4 us
    ppermute x2, starting transfers between devices, with_halo(): after = lax.ppermute(leading, axis, down)  9.17 us
  transfers between devices with their start and end apart: 11, of which 9 were waited for; matrix products, arithmetic and copies ran while one was open for 0% of the time, Pallas kernels for 0%

commit v1 on v0

v1 whole, which is shorter than its diff:
```python
import jax
import jax.numpy as jnp
from jax import lax
from jax.experimental import pallas as pl
from jax.experimental.pallas import tpu as pltpu
from jax.sharding import Mesh, PartitionSpec as P

STENCIL = (-205.0 / 72.0, 8.0 / 5.0, -1.0 / 5.0, 8.0 / 315.0, -1.0 / 560.0)
RATE = 0.2
COURANT = 0.11

AXES = ("yh", "x", "c", "yl", "z")
SIZES = {"yh": 2, "x": 4, "c": 2, "yl": 2, "z": 4}
SHOT = ("yh", "x", "c")
SLAB = ("yl", "z")
PLANE = ("yh", "x", "c", "yl")
PIECES = 32


def rotate(value, axis, steps):
    count = SIZES[axis]
    return lax.ppermute(value, axis, [(i, (i + steps) % count) for i in range(count)])


def halo(array, width):
    count, length = 8, array.shape[0]
    up = [(i, i + 1) for i in range(count - 1)]
    down = [(j, i) for i, j in up]
    before = lax.ppermute(array[length - width :], SLAB, up)
    after = lax.ppermute(array[:width], SLAB, down)
    return before, after


def laplace_rows(before, core, after):
    rows, widths, depths = core.shape
    extended = jnp.concatenate([before, core, after], axis=0)
    padded = jnp.pad(core, ((0, 0), (4, 4), (4, 4)))
    total = 3.0 * STENCIL[0] * core
    for reach in range(1, 5):
        along = extended[4 + reach : 4 + reach + rows] + extended[4 - reach : 4 - reach + rows]
        across = (
            padded[:, 4 + reach : 4 + reach + widths, 4 : 4 + depths]
            + padded[:, 4 - reach : 4 - reach + widths, 4 : 4 + depths]
        )
        downward = (
            padded[:, 4 : 4 + widths, 4 + reach : 4 + reach + depths]
            + padded[:, 4 : 4 + widths, 4 - reach : 4 - reach + depths]
        )
        total = total + STENCIL[reach] * (along + across + downward)
    return total


def gather_offsets(offsets):
    me = lax.axis_index(SHOT)
    value = jnp.where(jnp.arange(16, dtype=jnp.int32) == me, offsets[0], 0)
    value = value + rotate(value, "c", 1)
    value = value + rotate(value, "x", 1) + rotate(value, "x", 2) + rotate(value, "x", 3)
    return value + rotate(value, "yh", 1)


def bin_kernel(offs, items, own, one, two, three):
    outs = (own, one, two, three)
    for out in outs:
        out[...] = jnp.zeros_like(out)
    for item in range(PIECES):
        offset = offs[item // 2]
        place = lax.div(offset, 4) + item % 2
        shift = lax.rem(offset, 4)
        for k in range(4):

            @pl.when(shift == k)
            def _():
                outs[k][place] += items[item]


def put_in_bins(offs, items):
    shape = items.shape[1:]
    vmem = pl.BlockSpec(memory_space=pltpu.VMEM)
    return pl.pallas_call(
        bin_kernel,
        out_shape=[jax.ShapeDtypeStruct((8,) + shape, items.dtype)]
        + [jax.ShapeDtypeStruct((7,) + shape, items.dtype)] * 3,
        in_specs=[pl.BlockSpec(memory_space=pltpu.SMEM), vmem],
        out_specs=[vmem] * 4,
        cost_estimate=pl.CostEstimate(flops=1 << 18, bytes_accessed=1 << 21, transcendentals=0),
    )(offs, items)


def update_kernel(place, g0, g1, g2, g3, h0, h1, h2, h3, velocity, out, grad, illum):
    grad[...] = g0[...]
    illum[...] = h0[...]
    for k, g, h in ((1, g1, h1), (2, g2, h2), (3, g3, h3)):
        carry = (place[0] < k).astype(jnp.int32)
        grad[pl.ds(carry, 7)] += g[...]
        illum[pl.ds(carry, 7)] += h[...]
    out[...] = velocity[...] - RATE * grad[...] / (illum[...] + 1.0)


def update_model(place, grads, illums, velocity):
    vmem = pl.BlockSpec(memory_space=pltpu.VMEM)
    return pl.pallas_call(
        update_kernel,
        out_shape=jax.ShapeDtypeStruct(velocity.shape, velocity.dtype),
        in_specs=[pl.BlockSpec(memory_space=pltpu.SMEM)] + [vmem] * 9,
        out_specs=vmem,
        scratch_shapes=[pltpu.VMEM(velocity.shape, velocity.dtype)] * 2,
        cost_estimate=pl.CostEstimate(flops=1 << 19, bytes_accessed=1 << 22, transcendentals=0),
    )(place, *grads, *illums, velocity)


def pick_kernel(offs, place, n0, n1, n2, n3, out):
    refs = (n0, n1, n2, n3)
    for item in range(PIECES):
        offset = offs[item // 2]
        shift = lax.rem(offset, 4)
        slot = lax.div(offset, 4) + item % 2 + (place[0] + shift >= 4).astype(jnp.int32)
        for k in range(4):

            @pl.when(shift == k)
            def _():
                out[item] = refs[k][slot]


def pick(offs, place, news):
    shape = news[0].shape[1:]
    vmem = pl.BlockSpec(memory_space=pltpu.VMEM)
    smem = pl.BlockSpec(memory_space=pltpu.SMEM)
    return pl.pallas_call(
        pick_kernel,
        out_shape=jax.ShapeDtypeStruct((PIECES,) + shape, news[0].dtype),
        in_specs=[smem, smem] + [vmem] * 4,
        out_specs=vmem,
        cost_estimate=pl.CostEstimate(flops=1 << 18, bytes_accessed=1 << 21, transcendentals=0),
    )(offs, place, *news)


def on_device(gradient, illumination, u_prev, u_cur, velocity, offsets):
    shape = u_cur.shape[1:]
    u_prev, u_cur = u_prev[0], u_cur[0]
    yl, z = lax.axis_index("yl"), lax.axis_index("z")
    row = lax.axis_index(SHOT)
    place = z.astype(jnp.int32).reshape(1)
    offs = gather_offsets(offsets)

    halves = velocity.reshape(4, 16, 2, 32, 256)
    mine = lax.dynamic_slice(halves, (0, row, yl, 0, 0), (4, 1, 1, 32, 256)).reshape(4, 32, 256)
    send = lax.dynamic_slice(halves, (0, row, 1 - yl, 0, 0), (4, 1, 1, 32, 256)).reshape(4, 32, 256)
    other = rotate(send, "yl", 1)
    share = jnp.where(
        yl == 0, jnp.stack([mine, other], axis=1), jnp.stack([other, mine], axis=1)
    ).reshape(8, 32, 256)

    before, after = halo(u_cur, 4)
    first_lap = laplace_rows(before, u_cur, after)
    base = 2.0 * u_cur - u_prev

    grads = lax.all_to_all(gradient.reshape(PIECES, 32, 256), PLANE, 0, 0)
    illums = lax.all_to_all(illumination.reshape(PIECES, 32, 256), PLANE, 0, 0)
    grads = put_in_bins(offs, grads)
    illums = put_in_bins(offs, illums)
    grads = [grads[0]] + [rotate(grads[k], "z", k) for k in (1, 2, 3)]
    illums = [illums[0]] + [rotate(illums[k], "z", k) for k in (1, 2, 3)]
    new = update_model(place, grads, illums, share)

    news = [new] + [rotate(new, "z", -k) for k in (1, 2, 3)]
    items = pick(offs, place, news)
    local = lax.all_to_all(items, PLANE, 0, 0).reshape(shape)

    pairs = new.reshape(4, 2, 32, 256)
    keep = lax.dynamic_slice(pairs, (0, yl, 0, 0), (4, 1, 32, 256))
    give = lax.dynamic_slice(pairs, (0, 1 - yl, 0, 0), (4, 1, 32, 256))
    got = rotate(give, "yl", 1)
    whole = jnp.where(
        yl == 0, jnp.concatenate([keep, got], axis=1), jnp.concatenate([got, keep], axis=1)
    ).reshape(4, 1, 64, 256)
    new_model = lax.all_gather(whole, SHOT, axis=1, tiled=True)

    squared = (local * COURANT) ** 2
    one = base + squared * first_lap
    before, after = halo(one, 4)
    final = 2.0 * one - u_cur + squared * laplace_rows(before, one, after)
    return new_model, final[None]


def solution(mesh):
    fine = Mesh(mesh.devices.reshape(tuple(SIZES[a] for a in AXES)), AXES)
    field = P(SHOT, SLAB, None, None)
    model = P(None, SLAB, None, None)
    return jax.shard_map(
        on_device,
        mesh=fine,
        in_specs=(field, field, field, field, model, P(SHOT)),
        out_specs=(model, field),
        check_vma=False,
    )
```

time: 447 us -> 186 us (0.42)
  the two profiles are of different devices: /device:TPU:9 before, /device:TPU:12 now
where the time goes in v1:
time: 186 us; the launch traced here: 185 us
  waiting for transfers between devices  61.5 us (33%)
  starting transfers between devices  52.5 us (28%)
  blocking collectives  22.1 us (12%)
  between operations  14.8 us (8%)
  Pallas kernels  11.8 us (6%)
  other arithmetic  11.7 us (6%)
  local copies, waits for them, and re-layouts  10.7 us (6%)
    ppermute x16, waiting for transfers between devices, rotate(): lax.ppermute(value, axis, [(i, (i + steps) % count) for i in range(count)])  32.7 us
    ppermute x16, starting transfers between devices, rotate(): lax.ppermute(value, axis, [(i, (i + steps) % count) for i in range(count)])  23.7 us
    all_to_all x1, blocking collectives, on_device(): illums = lax.all_to_all(illumination.reshape(PIECES, 32, 256), PLANE, 0, 0)  22.1 us
    ppermute x2, waiting for transfers between devices, halo(): after = lax.ppermute(array[:width], SLAB, down)  11.3 us
    all_to_all x1, waiting for transfers between devices, on_device(): local = lax.all_to_all(items, PLANE, 0, 0).reshape(shape)  10.1 us
    ppermute x2, starting transfers between devices, halo(): after = lax.ppermute(array[:width], SLAB, down)  8.76 us
    all_to_all x1, starting transfers between devices, on_device(): local = lax.all_to_all(items, PLANE, 0, 0).reshape(shape)  8.14 us
    unnamed x27, local copies, waits for them, and re-layouts  7.77 us
  transfers between devices with their start and end apart: 23, of which 15 were waited for; matrix products, arithmetic and copies ran while one was open for 7% of the time, Pallas kernels for 5%

profile of v1, /device:TPU:12, one launch (start us, length us, event | category | flops | bytes accessed | tf_op | source)
XLA Modules:
  0.0 185.1 jit_solution(3731012481704615053)
XLA Ops:
  7.2 22.1 %all_to_all.15.items = f32[32,32,256]{2,1,0:T(8,128)} all-to-all(f32[32,32,256]{2,1,0:T(8,128)} %bitcast.37), channel_id=1, replica_groups=mesh['yh'=2,'x'=4,'c'=2,'yl'=2,'z'=4] {'yh','x','c','yl'}, dimensions={0} | all-to-all | bytes 2097152 | tf_op jit(solution)/shard_map/all_to_all | solution.py:158
  29.3 7.2 %all-to-all-start = ((f32[32,32,256]{2,1,0:T(8,128)}), f32[32,32,256]{2,1,0:T(8,128)S(1)}, u32[]{:S(2)}, u32[]{:S(2)}) async-start(f32[32,32,256]{2,1,0:T(8,128)} %bitcast.2), calls=%async_computation | async-start | bytes 2097152 | tf_op jit(solution)/shard_map/all_to_all | solution.py:157
  36.5 0.0 all-gather.2.cloned.1.call-start
  37.2 0.2 collective-permute-start
  37.5 1.0 collective-permute-done
  38.4 0.5 collective-permute-start.3
  39.0 2.7 %collective-permute-start.2 = (s32[16]{0:T(128)S(1)}, s32[16]{0:T(128)S(1)}, u32[]{:S(2)}, u32[]{:S(2)}) collective-permute-start(s32[16]{0:T(128)S(1)} %fusion.74), channel_id=1, source_target_pairs={{0,32},{16,48},{32,0},{48,16},{1,33},{17,49},{33,1},{49,17},{2,34}... | collective-permute-start | bytes 200 | tf_op jit(solution)/shard_map/ppermute | solution.py:22
  41.7 0.0 collective-permute-start.1
  41.7 8.3 %collective-permute-done.3 = s32[16]{0:T(128)S(1)} collective-permute-done((s32[16]{0:T(128)S(1)}, s32[16]{0:T(128)S(1)}, u32[]{:S(2)}, u32[]{:S(2)}) %collective-permute-start.3) | collective-permute-done | bytes 96 | tf_op jit(solution)/shard_map/ppermute | solution.py:22
  50.0 0.0 collective-permute-done.2
  50.0 0.0 collective-permute-done.1
  50.0 2.3 %collective-permute-start.4 = (s32[16]{0:T(128)S(1)}, s32[16]{0:T(128)S(1)}, u32[]{:S(2)}, u32[]{:S(2)}) collective-permute-start(s32[16]{0:T(128)S(1)} %add_add_fusion), channel_id=1, source_target_pairs={{0,64},{64,0},{1,65},{65,1},{2,66},{66,2},{3,67},{67,3},{4,68},{68... | collective-permute-start | bytes 200 | tf_op jit(solution)/shard_map/ppermute | solution.py:22
  52.3 2.9 %collective-permute-done.4 = s32[16]{0:T(128)S(1)} collective-permute-done((s32[16]{0:T(128)S(1)}, s32[16]{0:T(128)S(1)}, u32[]{:S(2)}, u32[]{:S(2)}) %collective-permute-start.4) | collective-permute-done | bytes 96 | tf_op jit(solution)/shard_map/ppermute | solution.py:22
  55.2 0.5 add.196.offs
  55.7 3.1 %shard_map.78 = (f32[8,32,256]{2,1,0:T(8,128)}, f32[7,32,256]{2,1,0:T(8,128)}, f32[7,32,256]{2,1,0:T(8,128)}, f32[7,32,256]{2,1,0:T(8,128)}) custom-call(s32[16]{0:T(128)} %add.196.offs, f32[32,32,256]{2,1,0:T(8,128)} %all_to_all.15.items), custom_call_target="tpu_custom_call" | custom-call | flops 262144 | bytes 2097152 | tf_op jit(solution)/shard_map/pallas_call | solution.py:79
  58.8 1.9 %collective-permute-start.8 = (f32[7,32,256]{2,1,0:T(8,128)}, f32[7,32,256]{2,1,0:T(8,128)S(1)}, u32[]{:S(2)}, u32[]{:S(2)}) collective-permute-start(f32[7,32,256]{2,1,0:T(8,128)} %get-tuple-element.15), channel_id=1, source_target_pairs={{0,1},{1,2},{2,3},{3,0},{4,5},{5,6},{6,7},{7,4},{8,9},{9,10},{10,1... | collective-permute-start | bytes 688136 | tf_op jit(solution)/shard_map/ppermute | solution.py:22
  60.7 1.0 dynamic-slice_bitcast_fusion.1
  61.7 0.7 collective-permute-start.11
  62.4 3.6 %collective-permute-start.9 = (f32[7,32,256]{2,1,0:T(8,128)}, f32[7,32,256]{2,1,0:T(8,128)S(1)}, u32[]{:S(2)}, u32[]{:S(2)}) collective-permute-start(f32[7,32,256]{2,1,0:T(8,128)} %get-tuple-element.16), channel_id=1, source_target_pairs={{0,2},{1,3},{2,0},{3,1},{4,6},{5,7},{6,4},{7,5},{8,10},{9,11},{10,... | collective-permute-start | bytes 688136 | tf_op jit(solution)/shard_map/ppermute | solution.py:22
  66.0 1.0 collective-permute-start.10
  67.0 1.0 copy-done.1
  68.0 3.1 %shard_map.77 = (f32[8,32,256]{2,1,0:T(8,128)}, f32[7,32,256]{2,1,0:T(8,128)}, f32[7,32,256]{2,1,0:T(8,128)}, f32[7,32,256]{2,1,0:T(8,128)}) custom-call(s32[16]{0:T(128)} %add.196.offs, f32[32,32,256]{2,1,0:T(8,128)} %copy-done.1), custom_call_target="tpu_custom_call" | custom-call | flops 262144 | bytes 2097152 | tf_op jit(solution)/shard_map/pallas_call | solution.py:79
  71.1 1.0 collective-permute-start.5
  72.1 0.0 collective-permute-done.11
  72.1 0.4 collective-permute-start.6
  72.6 0.0 collective-permute-done.8.h1
  72.6 2.3 %collective-permute-start.7 = (f32[7,32,256]{2,1,0:T(8,128)}, f32[7,32,256]{2,1,0:T(8,128)S(1)}, u32[]{:S(2)}, u32[]{:S(2)}) collective-permute-start(f32[7,32,256]{2,1,0:T(8,128)} %get-tuple-element.13), channel_id=1, source_target_pairs={{0,3},{1,0},{2,1},{3,2},{4,7},{5,4},{6,5},{7,6},{8,11},{9,8},{10,9... | collective-permute-start | bytes 688136 | tf_op jit(solution)/shard_map/ppermute | solution.py:22
  74.9 0.7 maximum_select_fusion
  75.6 0.1 collective-permute-done.9.h2
  75.7 1.1 collective-permute-done.10.h3
  76.9 7.0 %collective-permute-done.5.g1 = f32[7,32,256]{2,1,0:T(8,128)S(1)} collective-permute-done((f32[7,32,256]{2,1,0:T(8,128)}, f32[7,32,256]{2,1,0:T(8,128)S(1)}, u32[]{:S(2)}, u32[]{:S(2)}) %collective-permute-start.5) | collective-permute-done | bytes 229408 | tf_op jit(solution)/shard_map/ppermute | solution.py:22
  83.9 0.2 collective-permute-done.7.g3
  84.1 0.5 copy-done.10
  84.6 0.1 copy-done.11
  84.7 0.1 copy-done.12
  84.8 2.6 %shard_map.79.n0 = f32[8,32,256]{2,1,0:T(8,128)} custom-call(s32[1]{0:T(128)} %bitcast.place, f32[8,32,256]{2,1,0:T(8,128)} %get-tuple-element.10.g0, f32[7,32,256]{2,1,0:T(8,128)} %copy-done.10, f32[7,32,256]{2,1,0:T(8,128)} %copy-done.11, f32[7,32,256]{2,1,0:T(8,128)} %copy-done.12, f32[8,32,256]{2,1,0:T(8,128)} %get-tuple-element.14.h0, ...), custom_call_target="tpu_custom_call" | custom-call | flops 524288 | bytes 4194304 | tf_op jit(solution)/shard_map/pallas_call | solution.py:101
  87.4 1.0 constant_dynamic-slice_fusion.1
  88.4 1.5 collective-permute-start.12
  89.9 3.6 %collective-permute-done.12 = f32[4,1,32,256]{3,2,1,0:T(8,128)S(1)} collective-permute-done((f32[4,1,32,256]{3,2,1,0:T(8,128)S(1)}, f32[4,1,32,256]{3,2,1,0:T(8,128)S(1)}, u32[]{:S(2)}, u32[]{:S(2)}) %collective-permute-start.12) | collective-permute-done | bytes 131104 | tf_op jit(solution)/shard_map/ppermute | solution.py:22
  93.5 0.7 maximum_select_fusion.1
  94.2 0.0 all-gather.2.cloned.1.call-update
  94.2 1.8 collective-permute-start.15
  96.0 2.4 %collective-permute-start.14 = (f32[8,32,256]{2,1,0:T(8,128)S(1)}, f32[8,32,256]{2,1,0:T(8,128)S(1)}, u32[]{:S(2)}, u32[]{:S(2)}) collective-permute-start(f32[8,32,256]{2,1,0:T(8,128)S(1)} %copy-done.2), channel_id=1, source_target_pairs={{0,2},{1,3},{2,0},{3,1},{4,6},{5,7},{6,4},{7,5},{8,10},{9,11},{10,... | collective-permute-start | bytes 786440 | tf_op jit(solution)/shard_map/ppermute | solution.py:22
  98.4 1.3 collective-permute-start.13
  99.7 4.5 %collective-permute-done.15.n3 = f32[8,32,256]{2,1,0:T(8,128)S(1)} collective-permute-done((f32[8,32,256]{2,1,0:T(8,128)S(1)}, f32[8,32,256]{2,1,0:T(8,128)S(1)}, u32[]{:S(2)}, u32[]{:S(2)}) %collective-permute-start.15) | collective-permute-done | bytes 262176 | tf_op jit(solution)/shard_map/ppermute | solution.py:22
  104.2 4.0 %collective-permute-done.14.n2 = f32[8,32,256]{2,1,0:T(8,128)S(1)} collective-permute-done((f32[8,32,256]{2,1,0:T(8,128)S(1)}, f32[8,32,256]{2,1,0:T(8,128)S(1)}, u32[]{:S(2)}, u32[]{:S(2)}) %collective-permute-start.14) | collective-permute-done | bytes 262176 | tf_op jit(solution)/shard_map/ppermute | solution.py:22
  108.2 0.7 copy-done.5
  108.9 0.7 copy-done.6
  109.6 3.0 %shard_map.80 = f32[32,32,256]{2,1,0:T(8,128)} custom-call(s32[16]{0:T(128)} %add.196.offs, s32[1]{0:T(128)} %bitcast.place, f32[8,32,256]{2,1,0:T(8,128)} %shard_map.79.n0, f32[8,32,256]{2,1,0:T(8,128)} %copy-done.6, f32[8,32,256]{2,1,0:T(8,128)} %copy-done.5, f32[8,32,256]{2,1,0:T(8,128)} %copy-done.4), custom_call_target="tpu_custom_call" | custom-call | flops 262144 | bytes 2097152 | tf_op jit(solution)/shard_map/pallas_call | solution.py:128
  112.6 8.1 %all-to-all-start.2 = ((f32[32,32,256]{2,1,0:T(8,128)}), f32[32,32,256]{2,1,0:T(8,128)S(1)}, u32[]{:S(2)}, u32[]{:S(2)}) async-start(f32[32,32,256]{2,1,0:T(8,128)} %shard_map.80), calls=%async_computation.2 | async-start | bytes 2097152 | tf_op jit(solution)/shard_map/all_to_all | solution.py:167
  120.8 0.8 slice_bitcast_fusion.1
  121.6 3.5 %collective-permute-start.16 = (f32[4,64,256]{2,1,0:T(8,128)}, f32[4,64,256]{2,1,0:T(8,128)S(1)}, u32[]{:S(2)}, u32[]{:S(2)}) collective-permute-start(f32[4,64,256]{2,1,0:T(8,128)} %get-tuple-element.22), channel_id=1, source_target_pairs={{1,0},{2,1},{3,2},{4,3},{5,4},{6,5},{7,6},{9,8},{10,9},{11,10},{12... | collective-permute-start | bytes 786440 | tf_op jit(solution)/shard_map/ppermute | solution.py:30
  125.1 2.7 %collective-permute-start.17 = (f32[4,64,256]{2,1,0:T(8,128)}, f32[4,64,256]{2,1,0:T(8,128)}, u32[]{:S(2)}, u32[]{:S(2)}) collective-permute-start(f32[4,64,256]{2,1,0:T(8,128)} %get-tuple-element.23), channel_id=1, source_target_pairs={{0,1},{1,2},{2,3},{3,4},{4,5},{5,6},{6,7},{8,9},{9,10},{10,11},{11... | collective-permute-start | bytes 786440 | tf_op jit(solution)/shard_map/ppermute | solution.py:29
  127.8 10.1 %all-to-all-done.2 = f32[32,32,256]{2,1,0:T(8,128)S(1)} async-done(((f32[32,32,256]{2,1,0:T(8,128)}), f32[32,32,256]{2,1,0:T(8,128)S(1)}, u32[]{:S(2)}, u32[]{:S(2)}) %all-to-all-start.2) | async-done | bytes 1048608 | tf_op jit(solution)/shard_map/all_to_all | solution.py:167
  137.9 0.1 multiply_multiply_fusion
  138.0 7.9 %collective-permute-done.16 = f32[4,64,256]{2,1,0:T(8,128)S(1)} collective-permute-done((f32[4,64,256]{2,1,0:T(8,128)}, f32[4,64,256]{2,1,0:T(8,128)S(1)}, u32[]{:S(2)}, u32[]{:S(2)}) %collective-permute-start.16) | collective-permute-done | bytes 262176 | tf_op jit(solution)/shard_map/ppermute | solution.py:30
  145.9 1.1 collective-permute-done.17
  147.0 4.9 %fusion.33 = f32[16,64,256]{2,1,0:T(8,128)S(1)} fusion(f32[16,64,256]{2,1,0:T(8,128)S(1)} %bitcast.34, f32[4,64,256]{2,1,0:T(8,128)} %collective-permute-done.17, f32[4,64,256]{2,1,0:T(8,128)S(1)} %collective-permute-done.16, f32[1,16,64,256]{3,2,1,0:T(8,128)S(1)} %copy-done.3, f32[16,64,256]{2,1,0:T(8,128)S(1)} %bitcast.32), kind=kLoop, calls=%fused_computation.89 | loop fusion | flops 10747904 | bytes 4718592 | tf_op jit(solution)/shard_map/add | solution.py:179
  152.0 5.3 %collective-permute-start.18 = (f32[4,64,256]{2,1,0:T(8,128)S(1)}, f32[4,64,256]{2,1,0:T(8,128)S(1)}, u32[]{:S(2)}, u32[]{:S(2)}) collective-permute-start(f32[4,64,256]{2,1,0:T(8,128)S(1)} %get-tuple-element.20), channel_id=1, source_target_pairs={{1,0},{2,1},{3,2},{4,3},{5,4},{6,5},{7,6},{9,8},{10,9},{11,10},{12... | collective-permute-start | bytes 786440 | tf_op jit(solution)/shard_map/ppermute | solution.py:30
  157.3 1.9 %collective-permute-start.19 = (f32[4,64,256]{2,1,0:T(8,128)S(1)}, f32[4,64,256]{2,1,0:T(8,128)S(1)}, u32[]{:S(2)}, u32[]{:S(2)}) collective-permute-start(f32[4,64,256]{2,1,0:T(8,128)S(1)} %get-tuple-element.21), channel_id=1, source_target_pairs={{0,1},{1,2},{2,3},{3,4},{4,5},{5,6},{6,7},{8,9},{9,10},{10,11},{11... | collective-permute-start | bytes 786440 | tf_op jit(solution)/shard_map/ppermute | solution.py:29
  159.2 3.4 %collective-permute-done.18 = f32[4,64,256]{2,1,0:T(8,128)S(1)} collective-permute-done((f32[4,64,256]{2,1,0:T(8,128)S(1)}, f32[4,64,256]{2,1,0:T(8,128)S(1)}, u32[]{:S(2)}, u32[]{:S(2)}) %collective-permute-start.18) | collective-permute-done | bytes 262176 | tf_op jit(solution)/shard_map/ppermute | solution.py:30
  162.6 6.2 %collective-permute-done.19 = f32[4,64,256]{2,1,0:T(8,128)S(1)} collective-permute-done((f32[4,64,256]{2,1,0:T(8,128)S(1)}, f32[4,64,256]{2,1,0:T(8,128)S(1)}, u32[]{:S(2)}, u32[]{:S(2)}) %collective-permute-start.19) | collective-permute-done | bytes 262176 | tf_op jit(solution)/shard_map/ppermute | solution.py:29
  168.9 4.6 %fusion.9 = f32[1,16,64,256]{3,2,1,0:T(8,128)} fusion(f32[16,64,256]{2,1,0:T(8,128)S(1)} %fusion.33, f32[4,64,256]{2,1,0:T(8,128)S(1)} %collective-permute-done.19, f32[4,64,256]{2,1,0:T(8,128)S(1)} %collective-permute-done.18, f32[1,16,64,256]{3,2,1,0:T(8,128)S(1)} %copy-done, f32[16,64,256]{2,1,0:T(8,128)S(1)} %bitcast.33), kind=kLoop, calls=%fused_computation.65 | loop fusion | flops 10747904 | bytes 4718592 | tf_op jit(solution)/shard_map/broadcast_in_dim | solution.py:182
  173.5 4.7 %copy.10 = f32[4,16,64,256]{3,2,1,0:T(8,128)} copy(f32[4,16,64,256]{3,2,1,0:T(8,128)} %all-gather.2.cloned.1.call-done) | data formatting | bytes 8388608
  (28 shorter events, 0.1 us)
Async XLA Ops:
  29.3 37.8 %all-to-all-start = ((f32[32,32,256]{2,1,0:T(8,128)}), f32[32,32,256]{2,1,0:T(8,128)S(1)}, u32[]{:S(2)}, u32[]{:S(2)}) async-start(f32[32,32,256]{2,1,0:T(8,128)} %bitcast.2), calls=%async_computation | async-start | bytes 2097152 | tf_op jit(solution)/shard_map/all_to_all | solution.py:157
  36.5 137.0 %all-gather.2.cloned.1.call-start = ((), (), s32[]{:S(2)}) async-start(), calls=%async_computation.3 | async-start | bytes 4456448 | tf_op jit(solution)/shard_map/all_gather | solution.py:176
  37.2 1.2 collective-permute-start
  38.4 11.6 %collective-permute-start.3 = (s32[16]{0:T(128)S(1)}, s32[16]{0:T(128)S(1)}, u32[]{:S(2)}, u32[]{:S(2)}) collective-permute-start(s32[16]{0:T(128)S(1)} %fusion.74), channel_id=1, source_target_pairs={{0,48},{16,0},{32,16},{48,32},{1,49},{17,1},{33,17},{49,33},{2,50}... | collective-permute-start | bytes 200 | tf_op jit(solution)/shard_map/ppermute | solution.py:22
  39.0 11.1 %collective-permute-start.2 = (s32[16]{0:T(128)S(1)}, s32[16]{0:T(128)S(1)}, u32[]{:S(2)}, u32[]{:S(2)}) collective-permute-start(s32[16]{0:T(128)S(1)} %fusion.74), channel_id=1, source_target_pairs={{0,32},{16,48},{32,0},{48,16},{1,33},{17,49},{33,1},{49,17},{2,34}... | collective-permute-start | bytes 200 | tf_op jit(solution)/shard_map/ppermute | solution.py:22
  41.7 8.3 %collective-permute-start.1 = (s32[16]{0:T(128)S(1)}, s32[16]{0:T(128)S(1)}, u32[]{:S(2)}, u32[]{:S(2)}) collective-permute-start(s32[16]{0:T(128)S(1)} %fusion.74), channel_id=1, source_target_pairs={{0,16},{16,32},{32,48},{48,0},{1,17},{17,33},{33,49},{49,1},{2,18}... | collective-permute-start | bytes 200 | tf_op jit(solution)/shard_map/ppermute | solution.py:22
  50.0 5.1 %collective-permute-start.4 = (s32[16]{0:T(128)S(1)}, s32[16]{0:T(128)S(1)}, u32[]{:S(2)}, u32[]{:S(2)}) collective-permute-start(s32[16]{0:T(128)S(1)} %add_add_fusion), channel_id=1, source_target_pairs={{0,64},{64,0},{1,65},{65,1},{2,66},{66,2},{3,67},{67,3},{4,68},{68... | collective-permute-start | bytes 200 | tf_op jit(solution)/shard_map/ppermute | solution.py:22
  58.8 13.8 %collective-permute-start.8 = (f32[7,32,256]{2,1,0:T(8,128)}, f32[7,32,256]{2,1,0:T(8,128)S(1)}, u32[]{:S(2)}, u32[]{:S(2)}) collective-permute-start(f32[7,32,256]{2,1,0:T(8,128)} %get-tuple-element.15), channel_id=1, source_target_pairs={{0,1},{1,2},{2,3},{3,0},{4,5},{5,6},{6,7},{7,4},{8,9},{9,10},{10,1... | collective-permute-start | bytes 688136 | tf_op jit(solution)/shard_map/ppermute | solution.py:22
  61.7 10.4 %collective-permute-start.11 = (f32[4,32,256]{2,1,0:T(8,128)S(1)}, f32[4,32,256]{2,1,0:T(8,128)S(1)}, u32[]{:S(2)}, u32[]{:S(2)}) collective-permute-start(f32[4,32,256]{2,1,0:T(8,128)S(1)} %get-tuple-element.19), channel_id=1, source_target_pairs={{0,4},{4,0},{1,5},{5,1},{2,6},{6,2},{3,7},{7,3},{8,12},{12,8},{9,1... | collective-permute-start | bytes 393224 | tf_op jit(solution)/shard_map/ppermute | solution.py:22
  62.4 13.3 %collective-permute-start.9 = (f32[7,32,256]{2,1,0:T(8,128)}, f32[7,32,256]{2,1,0:T(8,128)S(1)}, u32[]{:S(2)}, u32[]{:S(2)}) collective-permute-start(f32[7,32,256]{2,1,0:T(8,128)} %get-tuple-element.16), channel_id=1, source_target_pairs={{0,2},{1,3},{2,0},{3,1},{4,6},{5,7},{6,4},{7,5},{8,10},{9,11},{10,... | collective-permute-start | bytes 688136 | tf_op jit(solution)/shard_map/ppermute | solution.py:22
  66.0 10.9 %collective-permute-start.10 = (f32[7,32,256]{2,1,0:T(8,128)}, f32[7,32,256]{2,1,0:T(8,128)S(1)}, u32[]{:S(2)}, u32[]{:S(2)}) collective-permute-start(f32[7,32,256]{2,1,0:T(8,128)} %get-tuple-element.17), channel_id=1, source_target_pairs={{0,3},{1,0},{2,1},{3,2},{4,7},{5,4},{6,5},{7,6},{8,11},{9,8},{10,9... | collective-permute-start | bytes 688136 | tf_op jit(solution)/shard_map/ppermute | solution.py:22
  67.0 1.0 copy-start.1
  71.1 12.9 %collective-permute-start.5 = (f32[7,32,256]{2,1,0:T(8,128)}, f32[7,32,256]{2,1,0:T(8,128)S(1)}, u32[]{:S(2)}, u32[]{:S(2)}) collective-permute-start(f32[7,32,256]{2,1,0:T(8,128)} %get-tuple-element.11), channel_id=1, source_target_pairs={{0,1},{1,2},{2,3},{3,0},{4,5},{5,6},{6,7},{7,4},{8,9},{9,10},{10,1... | collective-permute-start | bytes 688136 | tf_op jit(solution)/shard_map/ppermute | solution.py:22
  72.1 11.8 %collective-permute-start.6 = (f32[7,32,256]{2,1,0:T(8,128)}, f32[7,32,256]{2,1,0:T(8,128)S(1)}, u32[]{:S(2)}, u32[]{:S(2)}) collective-permute-start(f32[7,32,256]{2,1,0:T(8,128)} %get-tuple-element.12), channel_id=1, source_target_pairs={{0,2},{1,3},{2,0},{3,1},{4,6},{5,7},{6,4},{7,5},{8,10},{9,11},{10,... | collective-permute-start | bytes 688136 | tf_op jit(solution)/shard_map/ppermute | solution.py:22
  72.6 11.6 %copy-start.7 = (f32[7,32,256]{2,1,0:T(8,128)}, f32[7,32,256]{2,1,0:T(8,128)S(1)}, u32[]{:S(2)}) copy-start(f32[7,32,256]{2,1,0:T(8,128)S(1)} %collective-permute-done.8.h1) | copy-start | bytes 688132
  72.6 11.5 %collective-permute-start.7 = (f32[7,32,256]{2,1,0:T(8,128)}, f32[7,32,256]{2,1,0:T(8,128)S(1)}, u32[]{:S(2)}, u32[]{:S(2)}) collective-permute-start(f32[7,32,256]{2,1,0:T(8,128)} %get-tuple-element.13), channel_id=1, source_target_pairs={{0,3},{1,0},{2,1},{3,2},{4,7},{5,4},{6,5},{7,6},{8,11},{9,8},{10,9... | collective-permute-start | bytes 688136 | tf_op jit(solution)/shard_map/ppermute | solution.py:22
  75.7 8.4 %copy-start.8 = (f32[7,32,256]{2,1,0:T(8,128)}, f32[7,32,256]{2,1,0:T(8,128)S(1)}, u32[]{:S(2)}) copy-start(f32[7,32,256]{2,1,0:T(8,128)S(1)} %collective-permute-done.9.h2) | copy-start | bytes 688132
  76.9 7.2 %copy-start.9 = (f32[7,32,256]{2,1,0:T(8,128)}, f32[7,32,256]{2,1,0:T(8,128)S(1)}, u32[]{:S(2)}) copy-start(f32[7,32,256]{2,1,0:T(8,128)S(1)} %collective-permute-done.10.h3) | copy-start | bytes 688132
  83.9 0.7 copy-start.10
  83.9 0.8 copy-start.11
  84.1 0.7 copy-start.12
  87.4 6.8 %copy-start.2 = (f32[8,32,256]{2,1,0:T(8,128)S(1)}, f32[8,32,256]{2,1,0:T(8,128)}, u32[]{:S(2)}) copy-start(f32[8,32,256]{2,1,0:T(8,128)} %shard_map.79.n0) | copy-start | bytes 786436
  88.4 5.0 %collective-permute-start.12 = (f32[4,1,32,256]{3,2,1,0:T(8,128)S(1)}, f32[4,1,32,256]{3,2,1,0:T(8,128)S(1)}, u32[]{:S(2)}, u32[]{:S(2)}) collective-permute-start(f32[4,1,32,256]{3,2,1,0:T(8,128)S(1)} %get-tuple-element.25), channel_id=1, source_target_pairs={{0,4},{4,0},{1,5},{5,1},{2,6},{6,2},{3,7},{7,3},{8,12},{12,8},{9,1... | collective-permute-start | bytes 393224 | tf_op jit(solution)/shard_map/ppermute | solution.py:22
  94.2 10.0 %collective-permute-start.15 = (f32[8,32,256]{2,1,0:T(8,128)S(1)}, f32[8,32,256]{2,1,0:T(8,128)S(1)}, u32[]{:S(2)}, u32[]{:S(2)}) collective-permute-start(f32[8,32,256]{2,1,0:T(8,128)S(1)} %copy-done.2), channel_id=1, source_target_pairs={{0,1},{1,2},{2,3},{3,0},{4,5},{5,6},{6,7},{7,4},{8,9},{9,10},{10,1... | collective-permute-start | bytes 786440 | tf_op jit(solution)/shard_map/ppermute | solution.py:22
  96.0 12.2 %collective-permute-start.14 = (f32[8,32,256]{2,1,0:T(8,128)S(1)}, f32[8,32,256]{2,1,0:T(8,128)S(1)}, u32[]{:S(2)}, u32[]{:S(2)}) collective-permute-start(f32[8,32,256]{2,1,0:T(8,128)S(1)} %copy-done.2), channel_id=1, source_target_pairs={{0,2},{1,3},{2,0},{3,1},{4,6},{5,7},{6,4},{7,5},{8,10},{9,11},{10,... | collective-permute-start | bytes 786440 | tf_op jit(solution)/shard_map/ppermute | solution.py:22
  98.4 9.8 %collective-permute-start.13 = (f32[8,32,256]{2,1,0:T(8,128)S(1)}, f32[8,32,256]{2,1,0:T(8,128)S(1)}, u32[]{:S(2)}, u32[]{:S(2)}) collective-permute-start(f32[8,32,256]{2,1,0:T(8,128)S(1)} %copy-done.2), channel_id=1, source_target_pairs={{0,3},{1,0},{2,1},{3,2},{4,7},{5,4},{6,5},{7,6},{8,11},{9,8},{10,9... | collective-permute-start | bytes 786440 | tf_op jit(solution)/shard_map/ppermute | solution.py:22
  104.2 4.0 %copy-start.4 = (f32[8,32,256]{2,1,0:T(8,128)}, f32[8,32,256]{2,1,0:T(8,128)S(1)}, u32[]{:S(2)}) copy-start(f32[8,32,256]{2,1,0:T(8,128)S(1)} %collective-permute-done.15.n3) | copy-start | bytes 786436
  108.2 0.7 copy-start.5
  108.9 0.7 copy-start.6
  112.6 8.1 %copy-start = (f32[1,16,64,256]{3,2,1,0:T(8,128)S(1)}, f32[1,16,64,256]{3,2,1,0:T(8,128)}, u32[]{:S(2)}) copy-start(f32[1,16,64,256]{3,2,1,0:T(8,128)} %param.9) | copy-start | bytes 3145732
  112.6 25.3 %all-to-all-start.2 = ((f32[32,32,256]{2,1,0:T(8,128)}), f32[32,32,256]{2,1,0:T(8,128)S(1)}, u32[]{:S(2)}, u32[]{:S(2)}) async-start(f32[32,32,256]{2,1,0:T(8,128)} %shard_map.80), calls=%async_computation.2 | async-start | bytes 2097152 | tf_op jit(solution)/shard_map/all_to_all | solution.py:167
  121.6 25.4 %copy-start.3 = (f32[1,16,64,256]{3,2,1,0:T(8,128)S(1)}, f32[1,16,64,256]{3,2,1,0:T(8,128)}, u32[]{:S(2)}) copy-start(f32[1,16,64,256]{3,2,1,0:T(8,128)} %param.8) | copy-start | bytes 3145732
  121.6 24.3 %collective-permute-start.16 = (f32[4,64,256]{2,1,0:T(8,128)}, f32[4,64,256]{2,1,0:T(8,128)S(1)}, u32[]{:S(2)}, u32[]{:S(2)}) collective-permute-start(f32[4,64,256]{2,1,0:T(8,128)} %get-tuple-element.22), channel_id=1, source_target_pairs={{1,0},{2,1},{3,2},{4,3},{5,4},{6,5},{7,6},{9,8},{10,9},{11,10},{12... | collective-permute-start | bytes 786440 | tf_op jit(solution)/shard_map/ppermute | solution.py:30
  125.1 21.9 %collective-permute-start.17 = (f32[4,64,256]{2,1,0:T(8,128)}, f32[4,64,256]{2,1,0:T(8,128)}, u32[]{:S(2)}, u32[]{:S(2)}) collective-permute-start(f32[4,64,256]{2,1,0:T(8,128)} %get-tuple-element.23), channel_id=1, source_target_pairs={{0,1},{1,2},{2,3},{3,4},{4,5},{5,6},{6,7},{8,9},{9,10},{10,11},{11... | collective-permute-start | bytes 786440 | tf_op jit(solution)/shard_map/ppermute | solution.py:29
  152.0 10.6 %collective-permute-start.18 = (f32[4,64,256]{2,1,0:T(8,128)S(1)}, f32[4,64,256]{2,1,0:T(8,128)S(1)}, u32[]{:S(2)}, u32[]{:S(2)}) collective-permute-start(f32[4,64,256]{2,1,0:T(8,128)S(1)} %get-tuple-element.20), channel_id=1, source_target_pairs={{1,0},{2,1},{3,2},{4,3},{5,4},{6,5},{7,6},{9,8},{10,9},{11,10},{12... | collective-permute-start | bytes 786440 | tf_op jit(solution)/shard_map/ppermute | solution.py:30
  157.3 11.6 %collective-permute-start.19 = (f32[4,64,256]{2,1,0:T(8,128)S(1)}, f32[4,64,256]{2,1,0:T(8,128)S(1)}, u32[]{:S(2)}, u32[]{:S(2)}) collective-permute-start(f32[4,64,256]{2,1,0:T(8,128)S(1)} %get-tuple-element.21), channel_id=1, source_target_pairs={{0,1},{1,2},{2,3},{3,4},{4,5},{5,6},{6,7},{8,9},{9,10},{10,11},{11... | collective-permute-start | bytes 786440 | tf_op jit(solution)/shard_map/ppermute | solution.py:29
Sparse Core Ops, SparseCore 0:
  94.3 65.9 all-gather.1

commit v2 on v1

v2 whole, which is shorter than its diff:
```python
import jax
import jax.numpy as jnp
from jax import lax
from jax.experimental import pallas as pl
from jax.experimental.pallas import tpu as pltpu
from jax.sharding import Mesh, PartitionSpec as P

STENCIL = (-205.0 / 72.0, 8.0 / 5.0, -1.0 / 5.0, 8.0 / 315.0, -1.0 / 560.0)
RATE = 0.2
COURANT = 0.11

AXES = ("yh", "x", "c", "yl", "z")
SIZES = {"yh": 2, "x": 4, "c": 2, "yl": 2, "z": 4}
SHOT = ("yh", "x", "c")
SLAB = ("yl", "z")


def rotate(value, axis, steps):
    count = SIZES[axis]
    return lax.ppermute(value, axis, [(i, (i + steps) % count) for i in range(count)])


def halo(array, width):
    count, length = 8, array.shape[0]
    up = [(i, i + 1) for i in range(count - 1)]
    down = [(j, i) for i, j in up]
    before = lax.ppermute(array[length - width :], SLAB, up)
    after = lax.ppermute(array[:width], SLAB, down)
    return before, after


def laplace_rows(before, core, after):
    rows, widths, depths = core.shape
    extended = jnp.concatenate([before, core, after], axis=0)
    padded = jnp.pad(core, ((0, 0), (4, 4), (4, 4)))
    total = 3.0 * STENCIL[0] * core
    for reach in range(1, 5):
        along = extended[4 + reach : 4 + reach + rows] + extended[4 - reach : 4 - reach + rows]
        across = (
            padded[:, 4 + reach : 4 + reach + widths, 4 : 4 + depths]
            + padded[:, 4 - reach : 4 - reach + widths, 4 : 4 + depths]
        )
        downward = (
            padded[:, 4 : 4 + widths, 4 + reach : 4 + reach + depths]
            + padded[:, 4 : 4 + widths, 4 - reach : 4 - reach + depths]
        )
        total = total + STENCIL[reach] * (along + across + downward)
    return total


def gather_offsets(offsets):
    me = lax.axis_index(SHOT)
    value = jnp.where(jnp.arange(16, dtype=jnp.int32) == me, offsets[0], 0)
    value = value + rotate(value, "c", 1)
    value = value + rotate(value, "x", 1) + rotate(value, "x", 2) + rotate(value, "x", 3)
    return value + rotate(value, "yh", 1)


def model_kernel(offs, place, sent, near, far, items, z0, z1, z2, z3, grad, illum):
    z, yl = place[0], place[1]
    grad[...] = jnp.zeros_like(grad)
    illum[...] = jnp.zeros_like(illum)
    for shot in range(16):
        first = offs[shot]
        grad[pl.ds(first, 8)] += sent[8 * shot : 8 * shot + 8, :8]
        illum[pl.ds(first, 8)] += sent[8 * shot : 8 * shot + 8, 8:]
    for velocity, half in ((near, yl), (far, 1 - yl)):
        for k in range(4):
            for q in range(4):
                slab = 8 * q + 4 * half + lax.rem(z + 4 - k, 4)
                grad[slab] = velocity[k, q] - RATE * grad[slab] / (illum[slab] + 1.0)
    for shot in range(16):
        items[8 * shot : 8 * shot + 8] = grad[pl.ds(offs[shot], 8)]
    for k, out in enumerate((z0, z1, z2, z3)):
        there = lax.rem(z + k, 4)
        for q in range(4):
            for half in range(2):
                out[q, half] = grad[8 * q + 4 * half + there]


def update_model(offs, place, sent, near, far):
    vmem = pl.BlockSpec(memory_space=pltpu.VMEM)
    smem = pl.BlockSpec(memory_space=pltpu.SMEM)
    dtype = sent.dtype
    return pl.pallas_call(
        model_kernel,
        out_shape=[jax.ShapeDtypeStruct((128, 8, 256), dtype)]
        + [jax.ShapeDtypeStruct((4, 2, 8, 256), dtype)] * 4,
        in_specs=[smem, smem, vmem, vmem, vmem],
        out_specs=[vmem] * 5,
        scratch_shapes=[pltpu.VMEM((32, 8, 256), dtype)] * 2,
        cost_estimate=pl.CostEstimate(flops=1 << 20, bytes_accessed=1 << 22, transcendentals=0),
    )(offs, place, sent, near, far)


def row_kernel(place, near, far, out):
    z, yl = place[0], place[1]
    for parts, half in ((near, yl), (far, 1 - yl)):
        for k in range(4):
            block = 4 * half + lax.rem(z + 4 - k, 4)
            for q in range(4):
                out[q, block] = parts[k, q]


def order_row(place, near, far):
    vmem = pl.BlockSpec(memory_space=pltpu.VMEM)
    return pl.pallas_call(
        row_kernel,
        out_shape=jax.ShapeDtypeStruct((4, 8, 8, 256), near.dtype),
        in_specs=[pl.BlockSpec(memory_space=pltpu.SMEM), vmem, vmem],
        out_specs=vmem,
        cost_estimate=pl.CostEstimate(flops=0, bytes_accessed=1 << 19, transcendentals=0),
    )(place, near, far).reshape(4, 64, 256)


def place_kernel(rows, *refs):
    pieces, out, sems = refs[:16], refs[16], refs[17]
    copies = [
        pltpu.make_async_copy(piece, out.at[:, rows[i]], sems.at[i])
        for i, piece in enumerate(pieces)
    ]
    for copy in copies:
        copy.start()
    for copy in copies:
        copy.wait()


def place_rows(rows, pieces):
    hbm = pl.BlockSpec(memory_space=pl.ANY)
    return pl.pallas_call(
        place_kernel,
        out_shape=jax.ShapeDtypeStruct((4, 16) + pieces[0].shape[1:], pieces[0].dtype),
        in_specs=[pl.BlockSpec(memory_space=pltpu.SMEM)] + [hbm] * 16,
        out_specs=hbm,
        scratch_shapes=[pltpu.SemaphoreType.DMA((16,))],
        cost_estimate=pl.CostEstimate(flops=0, bytes_accessed=1 << 23, transcendentals=0),
    )(rows, *pieces)


def exchange(parts):
    yl = lax.axis_index("yl")
    parts = jnp.stack([parts[0]] + [rotate(parts[k], "z", k) for k in (1, 2, 3)])
    near = lax.dynamic_index_in_dim(parts, yl, 2, keepdims=False)
    far = lax.dynamic_index_in_dim(parts, 1 - yl, 2, keepdims=False)
    return near, rotate(far, "yl", 1)


def velocity_pieces(velocity):
    z = lax.axis_index("z")
    rows = lax.dynamic_index_in_dim(velocity, lax.axis_index(SHOT), 1, keepdims=False)
    rows = rows.reshape(4, 2, 4, 8, 256)
    return exchange([lax.dynamic_index_in_dim(rows, (z + k) % 4, 2, keepdims=False) for k in range(4)])


def gather_rows(own):
    yh, x, c = (lax.axis_index(a) for a in SHOT)
    found = [(own, 0, 0)] + [(rotate(own, "x", k), 0, k) for k in (1, 2, 3)]
    flipped = rotate(own, "yh", 1)
    found.append((flipped, 1, 0))
    found += [(rotate(flipped, "x", k), 1, k) for k in (1, 3)]
    found.append((rotate(found[2][0], "yh", 1), 1, 2))
    pieces, rows = [], []
    for value, dy, dx in found:
        base = ((yh + dy) % 2) * 8 + ((x - dx) % 4) * 2
        pieces += [value, rotate(value, "c", 1)]
        rows += [base + c, base + 1 - c]
    return place_rows(jnp.stack(rows).astype(jnp.int32), pieces)


def on_device(gradient, illumination, u_prev, u_cur, velocity, offsets):
    shape = u_cur.shape[1:]
    u_prev, u_cur = u_prev[0], u_cur[0]
    place = jnp.stack([lax.axis_index("z"), lax.axis_index("yl")]).astype(jnp.int32)

    sent = jnp.concatenate(
        [gradient.reshape(128, 8, 256), illumination.reshape(128, 8, 256)], axis=1
    )
    sent = lax.all_to_all(sent, AXES, 0, 0)

    offs = gather_offsets(offsets)
    near, far = velocity_pieces(velocity)
    before, after = halo(u_cur, 4)
    first_lap = laplace_rows(before, u_cur, after)
    base = 2.0 * u_cur - u_prev

    items, *parts = update_model(offs, place, sent, near, far)
    local = lax.all_to_all(items, AXES, 0, 0).reshape(shape)
    new_model = gather_rows(order_row(place, *exchange(parts)))

    squared = (local * COURANT) ** 2
    one = base + squared * first_lap
    before, after = halo(one, 4)
    final = 2.0 * one - u_cur + squared * laplace_rows(before, one, after)
    return new_model, final[None]


def solution(mesh):
    fine = Mesh(mesh.devices.reshape(tuple(SIZES[a] for a in AXES)), AXES)
    field = P(SHOT, SLAB, None, None)
    model = P(None, SLAB, None, None)
    return jax.shard_map(
        on_device,
        mesh=fine,
        in_specs=(field, field, field, field, model, P(SHOT)),
        out_specs=(model, field),
        check_vma=False,
    )
```

time: 186 us -> 265 us (1.42)
  the two profiles are of different devices: /device:TPU:12 before, /device:TPU:9 now
where the time goes in v2:
time: 265 us; the launch traced here: 264 us
  Pallas kernels  134 us (51%)
  starting transfers between devices  72.4 us (27%)
  waiting for transfers between devices  34.9 us (13%)
  other arithmetic  13.8 us (5%)
  local copies, waits for them, and re-layouts  7.42 us (3%)
    pallas_call x1, Pallas kernels, place_rows(): pl.pallas_call(place_kernel, out_shape=jax.ShapeDtypeStruct((4, 16) + pie...  129 us
    ppermute x28, starting transfers between devices, rotate(): lax.ppermute(value, axis, [(i, (i + steps) % count) for i in range(count)])  39.8 us
    ppermute x28, waiting for transfers between devices, rotate(): lax.ppermute(value, axis, [(i, (i + steps) % count) for i in range(count)])  34.8 us
    all_to_all x1, starting transfers between devices, on_device(): sent = lax.all_to_all(sent, AXES, 0, 0)  10.8 us
    all_to_all x1, starting transfers between devices, on_device(): local = lax.all_to_all(items, AXES, 0, 0).reshape(shape)  9.49 us
    ppermute x2, starting transfers between devices, halo(): after = lax.ppermute(array[:width], SLAB, down)  8.51 us
  transfers between devices with their start and end apart: 34, of which 8 were waited for; matrix products, arithmetic and copies ran while one was open for 4% of the time, Pallas kernels for 49%

profile of v2, /device:TPU:9, one launch (start us, length us, event | category | flops | bytes accessed | tf_op | source)
XLA Modules:
  0.0 264.1 jit_solution(12286694789821167342)
XLA Ops:
  0.6 3.0 %pad_maximum_fusion = f32[128,16,256]{2,1,0:T(8,128)} fusion(f32[128,8,256]{2,1,0:T(8,128)} %bitcast.77, f32[128,8,256]{2,1,0:T(8,128)} %bitcast.78), kind=kLoop, calls=%fused_computation.44 | loop fusion | flops 524288 | bytes 4194304 | tf_op jit(solution)/shard_map/concatenate | solution.py:175
  3.7 10.8 %all-to-all-start = ((f32[128,16,256]{2,1,0:T(8,128)}), f32[128,16,256]{2,1,0:T(8,128)S(1)}, u32[]{:S(2)}, u32[]{:S(2)}) async-start(f32[128,16,256]{2,1,0:T(8,128)} %pad_maximum_fusion), calls=%async_computation | async-start | bytes 4194304 | tf_op jit(solution)/shard_map/all_to_all | solution.py:178
  14.5 1.0 constant_dynamic-slice_fusion
  15.5 1.4 collective-permute-start.5
  16.9 2.9 %collective-permute-start.6 = (f32[4,2,8,256]{3,2,1,0:T(8,128)S(1)}, f32[4,2,8,256]{3,2,1,0:T(8,128)S(1)}, u32[]{:S(2)}, u32[]{:S(2)}) collective-permute-start(f32[4,2,8,256]{3,2,1,0:T(8,128)S(1)} %get-tuple-element.22), channel_id=1, source_target_pairs={{0,2},{1,3},{2,0},{3,1},{4,6},{5,7},{6,4},{7,5},{8,10},{9,11},{10,... | collective-permute-start | bytes 196616 | tf_op jit(solution)/shard_map/ppermute | solution.py:20
  19.9 0.9 collective-permute-start.7
  21.5 1.3 collective-permute-start
  22.7 0.8 collective-permute-done
  23.6 1.2 collective-permute-start.1
  24.8 2.4 collective-permute-start.2
  27.2 14.0 %collective-permute-done.5 = f32[4,2,8,256]{3,2,1,0:T(8,128)S(1)} collective-permute-done((f32[4,2,8,256]{3,2,1,0:T(8,128)S(1)}, f32[4,2,8,256]{3,2,1,0:T(8,128)S(1)}, u32[]{:S(2)}, u32[]{:S(2)}) %collective-permute-start.5) | collective-permute-done | bytes 65568 | tf_op jit(solution)/shard_map/ppermute | solution.py:20
  41.2 3.6 %collective-permute-start.3 = (s32[16]{0:T(128)S(1)}, s32[16]{0:T(128)S(1)}, u32[]{:S(2)}, u32[]{:S(2)}) collective-permute-start(s32[16]{0:T(128)S(1)} %fusion.74), channel_id=1, source_target_pairs={{0,48},{16,0},{32,16},{48,32},{1,49},{17,1},{33,17},{49,33},{2,50}... | collective-permute-start | bytes 200 | tf_op jit(solution)/shard_map/ppermute | solution.py:20
  44.8 0.0 collective-permute-done.6
  44.8 0.7 dynamic-slice_bitcast_fusion.2
  45.5 0.4 collective-permute-start.8
  45.9 1.8 collective-permute-start.4
  47.7 0.6 pad_add_fusion.place
  48.3 1.6 collective-permute-done.4
  49.9 0.5 add.372.offs
  50.5 0.0 copy-start
  50.5 0.6 copy-done.13
  51.1 0.7 copy-done
  51.9 3.1 %shard_map.77 = (f32[128,8,256]{2,1,0:T(8,128)}, f32[4,2,8,256]{3,2,1,0:T(8,128)}, f32[4,2,8,256]{3,2,1,0:T(8,128)}, f32[4,2,8,256]{3,2,1,0:T(8,128)}, f32[4,2,8,256]{3,2,1,0:T(8,128)}) custom-call(s32[16]{0:T(128)} %add.372.offs, s32[2]{0:T(128)} %pad_add_fusion.place, f32[128,16,256]{2,1,0:T(8,128)} %copy-done, f32[4,4,8,256]{3,2,1,0:T(8,128)} %get-tuple-element.19.near, ...), custom_call_target="tpu_custom_call" | custom-call | flops 1048576 | bytes 4194304 | tf_op jit(solution)/shard_map/pallas_call | solution.py:85
  55.0 0.0 copy-start.1
  55.0 9.5 %all-to-all-start.1 = ((f32[128,8,256]{2,1,0:T(8,128)}), f32[128,8,256]{2,1,0:T(8,128)S(1)}, u32[]{:S(2)}, u32[]{:S(2)}) async-start(f32[128,8,256]{2,1,0:T(8,128)} %get-tuple-element.11), calls=%async_computation.1 | async-start | bytes 2097152 | tf_op jit(solution)/shard_map/all_to_all | solution.py:187
  64.5 1.4 collective-permute-start.9
  65.9 2.9 %collective-permute-start.10 = (f32[4,2,8,256]{3,2,1,0:T(8,128)S(1)}, f32[4,2,8,256]{3,2,1,0:T(8,128)S(1)}, u32[]{:S(2)}, u32[]{:S(2)}) collective-permute-start(f32[4,2,8,256]{3,2,1,0:T(8,128)S(1)} %copy-done.17), channel_id=1, source_target_pairs={{0,2},{1,3},{2,0},{3,1},{4,6},{5,7},{6,4},{7,5},{8,10},{9,11},{10,... | collective-permute-start | bytes 196616 | tf_op jit(solution)/shard_map/ppermute | solution.py:20
  68.9 0.9 collective-permute-start.11
  69.8 9.5 %collective-permute-done.9 = f32[4,2,8,256]{3,2,1,0:T(8,128)S(1)} collective-permute-done((f32[4,2,8,256]{3,2,1,0:T(8,128)S(1)}, f32[4,2,8,256]{3,2,1,0:T(8,128)S(1)}, u32[]{:S(2)}, u32[]{:S(2)}) %collective-permute-start.9) | collective-permute-done | bytes 65568 | tf_op jit(solution)/shard_map/ppermute | solution.py:20
  79.2 2.8 %collective-permute-done.10 = f32[4,2,8,256]{3,2,1,0:T(8,128)S(1)} collective-permute-done((f32[4,2,8,256]{3,2,1,0:T(8,128)S(1)}, f32[4,2,8,256]{3,2,1,0:T(8,128)S(1)}, u32[]{:S(2)}, u32[]{:S(2)}) %collective-permute-start.10) | collective-permute-done | bytes 65568 | tf_op jit(solution)/shard_map/ppermute | solution.py:20
  82.0 0.7 dynamic-slice_bitcast_fusion
  82.7 0.6 collective-permute-start.12
  83.4 3.3 %collective-permute-start.28 = (f32[4,64,256]{2,1,0:T(8,128)S(1)}, f32[4,64,256]{2,1,0:T(8,128)S(1)}, u32[]{:S(2)}, u32[]{:S(2)}) collective-permute-start(f32[4,64,256]{2,1,0:T(8,128)S(1)} %get-tuple-element.14), channel_id=1, source_target_pairs={{1,0},{2,1},{3,2},{4,3},{5,4},{6,5},{7,6},{9,8},{10,9},{11,10},{12... | collective-permute-start | bytes 786440 | tf_op jit(solution)/shard_map/ppermute | solution.py:28
  86.6 2.0 collective-permute-start.29
  88.7 0.6 copy-done.14
  89.3 1.7 shard_map.78
  91.0 2.1 collective-permute-start.20
  93.2 2.6 collective-permute-start.16
  95.8 0.4 collective-permute-start.14
  96.1 2.3 collective-permute-start.18
  98.4 2.5 collective-permute-start.13
  100.9 0.1 collective-permute-done.16.refs_4_
  101.1 0.7 copy-done.3
  101.8 2.5 collective-permute-start.24
  104.3 0.0 copy-start.12
  104.3 0.1 multiply_multiply_fusion
  104.4 3.9 %collective-permute-done.14.refs_2_ = f32[4,64,256]{2,1,0:T(8,128)} collective-permute-done((f32[4,64,256]{2,1,0:T(8,128)}, f32[4,64,256]{2,1,0:T(8,128)}, u32[]{:S(2)}, u32[]{:S(2)}) %collective-permute-start.14) | collective-permute-done | bytes 262176 | tf_op jit(solution)/shard_map/ppermute | solution.py:20
  108.3 0.4 collective-permute-start.26
  108.7 3.1 %collective-permute-start.17 = (f32[4,64,256]{2,1,0:T(8,128)S(1)}, f32[4,64,256]{2,1,0:T(8,128)S(1)}, u32[]{:S(2)}, u32[]{:S(2)}) collective-permute-start(f32[4,64,256]{2,1,0:T(8,128)S(1)} %copy-done.4), channel_id=1, source_target_pairs={{0,8},{8,0},{1,9},{9,1},{2,10},{10,2},{3,11},{11,3},{4,12},{12,4},... | collective-permute-start | bytes 786440 | tf_op jit(solution)/shard_map/ppermute | solution.py:20
  111.8 0.1 collective-permute-start.21
  111.9 2.0 collective-permute-done.22.refs_10_
  113.9 1.1 collective-permute-start.15
  115.0 0.0 collective-permute-start.19
  115.0 4.8 %fusion.33 = f32[16,64,256]{2,1,0:T(8,128)S(1)} fusion(f32[16,64,256]{2,1,0:T(8,128)S(1)} %bitcast.69, f32[4,64,256]{2,1,0:T(8,128)S(1)} %copy-done.12, f32[4,64,256]{2,1,0:T(8,128)S(1)} %copy-done.10, f32[1,16,64,256]{3,2,1,0:T(8,128)} %param.8, f32[16,64,256]{2,1,0:T(8,128)S(1)} %bitcast.67), kind=kLoop, calls=%fused_computation.90 | loop fusion | flops 10747904 | bytes 4718592 | tf_op jit(solution)/shard_map/add | solution.py:191
  119.9 0.9 fusion.73
  120.7 0.5 collective-permute-start.23
  121.2 0.1 collective-permute-start.25
  121.3 0.4 collective-permute-start.27
  121.7 5.2 %collective-permute-start.30 = (f32[4,64,256]{2,1,0:T(8,128)}, f32[4,64,256]{2,1,0:T(8,128)}, u32[]{:S(2)}, u32[]{:S(2)}) collective-permute-start(f32[4,64,256]{2,1,0:T(8,128)} %get-tuple-element.12), channel_id=1, source_target_pairs={{1,0},{2,1},{3,2},{4,3},{5,4},{6,5},{7,6},{9,8},{10,9},{11,10},{12... | collective-permute-start | bytes 786440 | tf_op jit(solution)/shard_map/ppermute | solution.py:28
  127.0 0.7 copy-done.6
  127.7 1.9 collective-permute-start.31
  129.7 0.7 stack.106.rows
  130.4 129.0 %shard_map.79 = f32[4,16,64,256]{3,2,1,0:T(8,128)} custom-call(s32[16]{0:T(128)} %stack.106.rows, f32[4,64,256]{2,1,0:T(8,128)} %bitcast.75, f32[4,64,256]{2,1,0:T(8,128)} %collective-permute-done.13.refs_1_, f32[4,64,256]{2,1,0:T(8,128)} %collective-permute-done.14.refs_2_, f32[4,64,256]{2,1,0:T(8,128)} %copy-done.7, f32[4,64,256]{2,1,0:T(8,128)} %copy-done.3, ...), custom_call_target="tpu_custom_call" | custom-call | bytes 8388608 | tf_op jit(solution)/shard_map/pallas_call | solution.py:130
  259.4 4.6 %fusion.9 = f32[1,16,64,256]{3,2,1,0:T(8,128)} fusion(f32[16,64,256]{2,1,0:T(8,128)S(1)} %fusion.33, f32[4,64,256]{2,1,0:T(8,128)S(1)} %collective-permute-done.31, f32[4,64,256]{2,1,0:T(8,128)} %collective-permute-done.30, f32[1,16,64,256]{3,2,1,0:T(8,128)S(1)} %copy-done.1, f32[16,64,256]{2,1,0:T(8,128)S(1)} %bitcast.68), kind=kLoop, calls=%fused_computation.66 | loop fusion | flops 10747904 | bytes 4718592 | tf_op jit(solution)/shard_map/broadcast_in_dim | solution.py:194
  (63 shorter events, 0.2 us)
Async XLA Ops:
  3.7 46.8 %all-to-all-start = ((f32[128,16,256]{2,1,0:T(8,128)}), f32[128,16,256]{2,1,0:T(8,128)S(1)}, u32[]{:S(2)}, u32[]{:S(2)}) async-start(f32[128,16,256]{2,1,0:T(8,128)} %pad_maximum_fusion), calls=%async_computation | async-start | bytes 4194304 | tf_op jit(solution)/shard_map/all_to_all | solution.py:178
  15.5 25.7 %collective-permute-start.5 = (f32[4,2,8,256]{3,2,1,0:T(8,128)S(1)}, f32[4,2,8,256]{3,2,1,0:T(8,128)S(1)}, u32[]{:S(2)}, u32[]{:S(2)}) collective-permute-start(f32[4,2,8,256]{3,2,1,0:T(8,128)S(1)} %get-tuple-element.23), channel_id=1, source_target_pairs={{0,1},{1,2},{2,3},{3,0},{4,5},{5,6},{6,7},{7,4},{8,9},{9,10},{10,1... | collective-permute-start | bytes 196616 | tf_op jit(solution)/shard_map/ppermute | solution.py:20
  16.9 27.9 %collective-permute-start.6 = (f32[4,2,8,256]{3,2,1,0:T(8,128)S(1)}, f32[4,2,8,256]{3,2,1,0:T(8,128)S(1)}, u32[]{:S(2)}, u32[]{:S(2)}) collective-permute-start(f32[4,2,8,256]{3,2,1,0:T(8,128)S(1)} %get-tuple-element.22), channel_id=1, source_target_pairs={{0,2},{1,3},{2,0},{3,1},{4,6},{5,7},{6,4},{7,5},{8,10},{9,11},{10,... | collective-permute-start | bytes 196616 | tf_op jit(solution)/shard_map/ppermute | solution.py:20
  19.9 24.9 %collective-permute-start.7 = (f32[4,2,8,256]{3,2,1,0:T(8,128)S(1)}, f32[4,2,8,256]{3,2,1,0:T(8,128)S(1)}, u32[]{:S(2)}, u32[]{:S(2)}) collective-permute-start(f32[4,2,8,256]{3,2,1,0:T(8,128)S(1)} %get-tuple-element.21), channel_id=1, source_target_pairs={{0,3},{1,0},{2,1},{3,2},{4,7},{5,4},{6,5},{7,6},{8,11},{9,8},{10,9... | collective-permute-start | bytes 196616 | tf_op jit(solution)/shard_map/ppermute | solution.py:20
  21.5 2.1 collective-permute-start
  23.6 22.3 %collective-permute-start.1 = (s32[16]{0:T(128)S(1)}, s32[16]{0:T(128)S(1)}, u32[]{:S(2)}, u32[]{:S(2)}) collective-permute-start(s32[16]{0:T(128)S(1)} %fusion.74), channel_id=1, source_target_pairs={{0,16},{16,32},{32,48},{48,0},{1,17},{17,33},{33,49},{49,1},{2,18}... | collective-permute-start | bytes 200 | tf_op jit(solution)/shard_map/ppermute | solution.py:20
  24.8 21.1 %collective-permute-start.2 = (s32[16]{0:T(128)S(1)}, s32[16]{0:T(128)S(1)}, u32[]{:S(2)}, u32[]{:S(2)}) collective-permute-start(s32[16]{0:T(128)S(1)} %fusion.74), channel_id=1, source_target_pairs={{0,32},{16,48},{32,0},{48,16},{1,33},{17,49},{33,1},{49,17},{2,34}... | collective-permute-start | bytes 200 | tf_op jit(solution)/shard_map/ppermute | solution.py:20
  41.2 4.7 %collective-permute-start.3 = (s32[16]{0:T(128)S(1)}, s32[16]{0:T(128)S(1)}, u32[]{:S(2)}, u32[]{:S(2)}) collective-permute-start(s32[16]{0:T(128)S(1)} %fusion.74), channel_id=1, source_target_pairs={{0,48},{16,0},{32,16},{48,32},{1,49},{17,1},{33,17},{49,33},{2,50}... | collective-permute-start | bytes 200 | tf_op jit(solution)/shard_map/ppermute | solution.py:20
  45.5 5.0 %collective-permute-start.8 = (f32[4,4,8,256]{3,2,1,0:T(8,128)S(1)}, f32[4,4,8,256]{3,2,1,0:T(8,128)S(1)}, u32[]{:S(2)}, u32[]{:S(2)}) collective-permute-start(f32[4,4,8,256]{3,2,1,0:T(8,128)S(1)} %get-tuple-element.18), channel_id=1, source_target_pairs={{0,4},{4,0},{1,5},{5,1},{2,6},{6,2},{3,7},{7,3},{8,12},{12,8},{9,1... | collective-permute-start | bytes 393224 | tf_op jit(solution)/shard_map/ppermute | solution.py:20
  45.9 4.0 %collective-permute-start.4 = (s32[16]{0:T(128)S(1)}, s32[16]{0:T(128)S(1)}, u32[]{:S(2)}, u32[]{:S(2)}) collective-permute-start(s32[16]{0:T(128)S(1)} %add_add_fusion), channel_id=1, source_target_pairs={{0,64},{64,0},{1,65},{65,1},{2,66},{66,2},{3,67},{67,3},{4,68},{68... | collective-permute-start | bytes 200 | tf_op jit(solution)/shard_map/ppermute | solution.py:20
  50.5 0.6 copy-start.13
  50.5 1.4 copy-start
  54.9 9.5 %copy-start.18 = (f32[4,2,8,256]{3,2,1,0:T(8,128)S(1)}, f32[4,2,8,256]{3,2,1,0:T(8,128)}, u32[]{:S(2)}) copy-start(f32[4,2,8,256]{3,2,1,0:T(8,128)} %get-tuple-element.8) | copy-start | bytes 196612
  54.9 11.0 %copy-start.17 = (f32[4,2,8,256]{3,2,1,0:T(8,128)S(1)}, f32[4,2,8,256]{3,2,1,0:T(8,128)}, u32[]{:S(2)}) copy-start(f32[4,2,8,256]{3,2,1,0:T(8,128)} %get-tuple-element.9) | copy-start | bytes 196612
  54.9 13.9 %copy-start.16 = (f32[4,2,8,256]{3,2,1,0:T(8,128)S(1)}, f32[4,2,8,256]{3,2,1,0:T(8,128)}, u32[]{:S(2)}) copy-start(f32[4,2,8,256]{3,2,1,0:T(8,128)} %get-tuple-element.10) | copy-start | bytes 196612
  55.0 27.1 %copy-start.15 = (f32[4,2,8,256]{3,2,1,0:T(8,128)S(1)}, f32[4,2,8,256]{3,2,1,0:T(8,128)}, u32[]{:S(2)}) copy-start(f32[4,2,8,256]{3,2,1,0:T(8,128)} %get-tuple-element.7) | copy-start | bytes 196612
  55.0 28.3 %copy-start.1 = (f32[1,16,64,256]{3,2,1,0:T(8,128)S(1)}, f32[1,16,64,256]{3,2,1,0:T(8,128)}, u32[]{:S(2)}) copy-start(f32[1,16,64,256]{3,2,1,0:T(8,128)} %param.9) | copy-start | bytes 3145732
  55.0 49.3 %all-to-all-start.1 = ((f32[128,8,256]{2,1,0:T(8,128)}), f32[128,8,256]{2,1,0:T(8,128)S(1)}, u32[]{:S(2)}, u32[]{:S(2)}) async-start(f32[128,8,256]{2,1,0:T(8,128)} %get-tuple-element.11), calls=%async_computation.1 | async-start | bytes 2097152 | tf_op jit(solution)/shard_map/all_to_all | solution.py:187
  64.5 14.8 %collective-permute-start.9 = (f32[4,2,8,256]{3,2,1,0:T(8,128)S(1)}, f32[4,2,8,256]{3,2,1,0:T(8,128)S(1)}, u32[]{:S(2)}, u32[]{:S(2)}) collective-permute-start(f32[4,2,8,256]{3,2,1,0:T(8,128)S(1)} %copy-done.18), channel_id=1, source_target_pairs={{0,1},{1,2},{2,3},{3,0},{4,5},{5,6},{6,7},{7,4},{8,9},{9,10},{10,1... | collective-permute-start | bytes 196616 | tf_op jit(solution)/shard_map/ppermute | solution.py:20
  65.9 16.1 %collective-permute-start.10 = (f32[4,2,8,256]{3,2,1,0:T(8,128)S(1)}, f32[4,2,8,256]{3,2,1,0:T(8,128)S(1)}, u32[]{:S(2)}, u32[]{:S(2)}) collective-permute-start(f32[4,2,8,256]{3,2,1,0:T(8,128)S(1)} %copy-done.17), channel_id=1, source_target_pairs={{0,2},{1,3},{2,0},{3,1},{4,6},{5,7},{6,4},{7,5},{8,10},{9,11},{10,... | collective-permute-start | bytes 196616 | tf_op jit(solution)/shard_map/ppermute | solution.py:20
  68.9 13.2 %collective-permute-start.11 = (f32[4,2,8,256]{3,2,1,0:T(8,128)S(1)}, f32[4,2,8,256]{3,2,1,0:T(8,128)S(1)}, u32[]{:S(2)}, u32[]{:S(2)}) collective-permute-start(f32[4,2,8,256]{3,2,1,0:T(8,128)S(1)} %copy-done.16), channel_id=1, source_target_pairs={{0,3},{1,0},{2,1},{3,2},{4,7},{5,4},{6,5},{7,6},{8,11},{9,8},{10,9... | collective-permute-start | bytes 196616 | tf_op jit(solution)/shard_map/ppermute | solution.py:20
  82.7 5.9 %collective-permute-start.12 = (f32[4,4,8,256]{3,2,1,0:T(8,128)S(1)}, f32[4,4,8,256]{3,2,1,0:T(8,128)S(1)}, u32[]{:S(2)}, u32[]{:S(2)}) collective-permute-start(f32[4,4,8,256]{3,2,1,0:T(8,128)S(1)} %get-tuple-element.16), channel_id=1, source_target_pairs={{0,4},{4,0},{1,5},{5,1},{2,6},{6,2},{3,7},{7,3},{8,12},{12,8},{9,1... | collective-permute-start | bytes 393224 | tf_op jit(solution)/shard_map/ppermute | solution.py:20
  83.4 12.8 %collective-permute-start.28 = (f32[4,64,256]{2,1,0:T(8,128)S(1)}, f32[4,64,256]{2,1,0:T(8,128)S(1)}, u32[]{:S(2)}, u32[]{:S(2)}) collective-permute-start(f32[4,64,256]{2,1,0:T(8,128)S(1)} %get-tuple-element.14), channel_id=1, source_target_pairs={{1,0},{2,1},{3,2},{4,3},{5,4},{6,5},{7,6},{9,8},{10,9},{11,10},{12... | collective-permute-start | bytes 786440 | tf_op jit(solution)/shard_map/ppermute | solution.py:28
  86.6 11.8 %collective-permute-start.29 = (f32[4,64,256]{2,1,0:T(8,128)S(1)}, f32[4,64,256]{2,1,0:T(8,128)S(1)}, u32[]{:S(2)}, u32[]{:S(2)}) collective-permute-start(f32[4,64,256]{2,1,0:T(8,128)S(1)} %get-tuple-element.15), channel_id=1, source_target_pairs={{0,1},{1,2},{2,3},{3,4},{4,5},{5,6},{6,7},{8,9},{9,10},{10,11},{11... | collective-permute-start | bytes 786440 | tf_op jit(solution)/shard_map/ppermute | solution.py:27
  88.7 0.7 copy-start.14
  91.0 9.9 %collective-permute-start.20 = (f32[4,64,256]{2,1,0:T(8,128)}, f32[4,64,256]{2,1,0:T(8,128)S(1)}, u32[]{:S(2)}, u32[]{:S(2)}) collective-permute-start(f32[4,64,256]{2,1,0:T(8,128)} %bitcast.70), channel_id=1, source_target_pairs={{0,64},{64,0},{1,65},{65,1},{2,66},{66,2},{3,67},{67,3},{4,68},{68... | collective-permute-start | bytes 786440 | tf_op jit(solution)/shard_map/ppermute | solution.py:20
  93.2 7.9 %collective-permute-start.16 = (f32[4,64,256]{2,1,0:T(8,128)}, f32[4,64,256]{2,1,0:T(8,128)S(1)}, u32[]{:S(2)}, u32[]{:S(2)}) collective-permute-start(f32[4,64,256]{2,1,0:T(8,128)} %bitcast.71), channel_id=1, source_target_pairs={{0,32},{16,48},{32,0},{48,16},{1,33},{17,49},{33,1},{49,17},{2,34}... | collective-permute-start | bytes 786440 | tf_op jit(solution)/shard_map/ppermute | solution.py:20
  95.8 12.5 %collective-permute-start.14 = (f32[4,64,256]{2,1,0:T(8,128)}, f32[4,64,256]{2,1,0:T(8,128)}, u32[]{:S(2)}, u32[]{:S(2)}) collective-permute-start(f32[4,64,256]{2,1,0:T(8,128)} %bitcast.72), channel_id=1, source_target_pairs={{0,16},{16,32},{32,48},{48,0},{1,17},{17,33},{33,49},{49,1},{2,18}... | collective-permute-start | bytes 786440 | tf_op jit(solution)/shard_map/ppermute | solution.py:20
  96.1 8.2 %copy-start.9 = (f32[4,64,256]{2,1,0:T(8,128)}, f32[4,64,256]{2,1,0:T(8,128)S(1)}, u32[]{:S(2)}) copy-start(f32[4,64,256]{2,1,0:T(8,128)S(1)} %collective-permute-done.28) | copy-start | bytes 786436
  96.1 12.6 %collective-permute-start.18 = (f32[4,64,256]{2,1,0:T(8,128)}, f32[4,64,256]{2,1,0:T(8,128)}, u32[]{:S(2)}, u32[]{:S(2)}) collective-permute-start(f32[4,64,256]{2,1,0:T(8,128)} %bitcast.73), channel_id=1, source_target_pairs={{0,48},{16,0},{32,16},{48,32},{1,49},{17,1},{33,17},{49,33},{2,50}... | collective-permute-start | bytes 786440 | tf_op jit(solution)/shard_map/ppermute | solution.py:20
  98.4 5.8 %copy-start.11 = (f32[4,64,256]{2,1,0:T(8,128)}, f32[4,64,256]{2,1,0:T(8,128)S(1)}, u32[]{:S(2)}) copy-start(f32[4,64,256]{2,1,0:T(8,128)S(1)} %collective-permute-done.29) | copy-start | bytes 786436
  98.4 13.3 %collective-permute-start.13 = (f32[4,64,256]{2,1,0:T(8,128)}, f32[4,64,256]{2,1,0:T(8,128)}, u32[]{:S(2)}, u32[]{:S(2)}) collective-permute-start(f32[4,64,256]{2,1,0:T(8,128)} %bitcast.74), channel_id=1, source_target_pairs={{0,8},{8,0},{1,9},{9,1},{2,10},{10,2},{3,11},{11,3},{4,12},{12,4},... | collective-permute-start | bytes 786440 | tf_op jit(solution)/shard_map/ppermute | solution.py:20
  100.9 18.9 %copy-start.2 = (f32[4,64,256]{2,1,0:T(8,128)}, f32[4,64,256]{2,1,0:T(8,128)S(1)}, u32[]{:S(2)}) copy-start(f32[4,64,256]{2,1,0:T(8,128)S(1)} %collective-permute-done.20.refs_8_) | copy-start | bytes 786436
  100.9 13.0 %collective-permute-start.22 = (f32[4,64,256]{2,1,0:T(8,128)S(1)}, f32[4,64,256]{2,1,0:T(8,128)}, u32[]{:S(2)}, u32[]{:S(2)}) collective-permute-start(f32[4,64,256]{2,1,0:T(8,128)S(1)} %collective-permute-done.20.refs_8_), channel_id=1, source_target_pairs={{0,16},{16,32},{32,48},{48,0},{1,17},{17,33},{33,49},{49,1},{2,18}... | collective-permute-start | bytes 786440 | tf_op jit(solution)/shard_map/ppermute | solution.py:20
  101.1 0.7 copy-start.3
  101.8 13.2 %collective-permute-start.24 = (f32[4,64,256]{2,1,0:T(8,128)S(1)}, f32[4,64,256]{2,1,0:T(8,128)}, u32[]{:S(2)}, u32[]{:S(2)}) collective-permute-start(f32[4,64,256]{2,1,0:T(8,128)S(1)} %collective-permute-done.20.refs_8_), channel_id=1, source_target_pairs={{0,48},{16,0},{32,16},{48,32},{1,49},{17,1},{33,17},{49,33},{2,50}... | collective-permute-start | bytes 786440 | tf_op jit(solution)/shard_map/ppermute | solution.py:20
  104.3 4.0 %copy-start.4 = (f32[4,64,256]{2,1,0:T(8,128)S(1)}, f32[4,64,256]{2,1,0:T(8,128)}, u32[]{:S(2)}) copy-start(f32[4,64,256]{2,1,0:T(8,128)} %copy-done.3) | copy-start | bytes 786436
  104.3 10.7 %copy-start.10 = (f32[4,64,256]{2,1,0:T(8,128)S(1)}, f32[4,64,256]{2,1,0:T(8,128)}, u32[]{:S(2)}) copy-start(f32[4,64,256]{2,1,0:T(8,128)} %copy-done.9) | copy-start | bytes 786436
  104.3 10.7 %copy-start.12 = (f32[4,64,256]{2,1,0:T(8,128)S(1)}, f32[4,64,256]{2,1,0:T(8,128)}, u32[]{:S(2)}) copy-start(f32[4,64,256]{2,1,0:T(8,128)} %copy-done.11) | copy-start | bytes 786436
  108.3 12.4 %collective-permute-start.26 = (f32[4,64,256]{2,1,0:T(8,128)S(1)}, f32[4,64,256]{2,1,0:T(8,128)}, u32[]{:S(2)}, u32[]{:S(2)}) collective-permute-start(f32[4,64,256]{2,1,0:T(8,128)S(1)} %copy-done.4), channel_id=1, source_target_pairs={{0,64},{64,0},{1,65},{65,1},{2,66},{66,2},{3,67},{67,3},{4,68},{68... | collective-permute-start | bytes 786440 | tf_op jit(solution)/shard_map/ppermute | solution.py:20
  108.7 12.6 %collective-permute-start.17 = (f32[4,64,256]{2,1,0:T(8,128)S(1)}, f32[4,64,256]{2,1,0:T(8,128)S(1)}, u32[]{:S(2)}, u32[]{:S(2)}) collective-permute-start(f32[4,64,256]{2,1,0:T(8,128)S(1)} %copy-done.4), channel_id=1, source_target_pairs={{0,8},{8,0},{1,9},{9,1},{2,10},{10,2},{3,11},{11,3},{4,12},{12,4},... | collective-permute-start | bytes 786440 | tf_op jit(solution)/shard_map/ppermute | solution.py:20
  111.8 15.2 %collective-permute-start.21 = (f32[4,64,256]{2,1,0:T(8,128)S(1)}, f32[4,64,256]{2,1,0:T(8,128)S(1)}, u32[]{:S(2)}, u32[]{:S(2)}) collective-permute-start(f32[4,64,256]{2,1,0:T(8,128)S(1)} %collective-permute-done.20.refs_8_), channel_id=1, source_target_pairs={{0,8},{8,0},{1,9},{9,1},{2,10},{10,2},{3,11},{11,3},{4,12},{12,4},... | collective-permute-start | bytes 786440 | tf_op jit(solution)/shard_map/ppermute | solution.py:20
  113.9 7.3 %collective-permute-start.15 = (f32[4,64,256]{2,1,0:T(8,128)}, f32[4,64,256]{2,1,0:T(8,128)S(1)}, u32[]{:S(2)}, u32[]{:S(2)}) collective-permute-start(f32[4,64,256]{2,1,0:T(8,128)} %collective-permute-done.14.refs_2_), channel_id=1, source_target_pairs={{0,8},{8,0},{1,9},{9,1},{2,10},{10,2},{3,11},{11,3},{4,12},{12,4},... | collective-permute-start | bytes 786440 | tf_op jit(solution)/shard_map/ppermute | solution.py:20
  115.0 6.8 %collective-permute-start.19 = (f32[4,64,256]{2,1,0:T(8,128)}, f32[4,64,256]{2,1,0:T(8,128)S(1)}, u32[]{:S(2)}, u32[]{:S(2)}) collective-permute-start(f32[4,64,256]{2,1,0:T(8,128)} %collective-permute-done.18.refs_6_), channel_id=1, source_target_pairs={{0,8},{8,0},{1,9},{9,1},{2,10},{10,2},{3,11},{11,3},{4,12},{12,4},... | collective-permute-start | bytes 786440 | tf_op jit(solution)/shard_map/ppermute | solution.py:20
  120.7 9.7 %collective-permute-start.23 = (f32[4,64,256]{2,1,0:T(8,128)}, f32[4,64,256]{2,1,0:T(8,128)}, u32[]{:S(2)}, u32[]{:S(2)}) collective-permute-start(f32[4,64,256]{2,1,0:T(8,128)} %collective-permute-done.22.refs_10_), channel_id=1, source_target_pairs={{0,8},{8,0},{1,9},{9,1},{2,10},{10,2},{3,11},{11,3},{4,12},{12,4},... | collective-permute-start | bytes 786440 | tf_op jit(solution)/shard_map/ppermute | solution.py:20
  121.2 5.8 %copy-start.7 = (f32[4,64,256]{2,1,0:T(8,128)}, f32[4,64,256]{2,1,0:T(8,128)S(1)}, u32[]{:S(2)}) copy-start(f32[4,64,256]{2,1,0:T(8,128)S(1)} %collective-permute-done.15.refs_3_) | copy-start | bytes 786436
  121.2 9.2 %collective-permute-start.25 = (f32[4,64,256]{2,1,0:T(8,128)}, f32[4,64,256]{2,1,0:T(8,128)}, u32[]{:S(2)}, u32[]{:S(2)}) collective-permute-start(f32[4,64,256]{2,1,0:T(8,128)} %collective-permute-done.24.refs_12_), channel_id=1, source_target_pairs={{0,8},{8,0},{1,9},{9,1},{2,10},{10,2},{3,11},{11,3},{4,12},{12,4},... | collective-permute-start | bytes 786440 | tf_op jit(solution)/shard_map/ppermute | solution.py:20
  121.3 5.7 %copy-start.5 = (f32[4,64,256]{2,1,0:T(8,128)}, f32[4,64,256]{2,1,0:T(8,128)S(1)}, u32[]{:S(2)}) copy-start(f32[4,64,256]{2,1,0:T(8,128)S(1)} %collective-permute-done.17.refs_5_) | copy-start | bytes 786436
  121.3 9.1 %collective-permute-start.27 = (f32[4,64,256]{2,1,0:T(8,128)}, f32[4,64,256]{2,1,0:T(8,128)}, u32[]{:S(2)}, u32[]{:S(2)}) collective-permute-start(f32[4,64,256]{2,1,0:T(8,128)} %collective-permute-done.26.refs_14_), channel_id=1, source_target_pairs={{0,8},{8,0},{1,9},{9,1},{2,10},{10,2},{3,11},{11,3},{4,12},{12,4},... | collective-permute-start | bytes 786440 | tf_op jit(solution)/shard_map/ppermute | solution.py:20
  121.7 5.3 %copy-start.8 = (f32[4,64,256]{2,1,0:T(8,128)}, f32[4,64,256]{2,1,0:T(8,128)S(1)}, u32[]{:S(2)}) copy-start(f32[4,64,256]{2,1,0:T(8,128)S(1)} %collective-permute-done.19.refs_7_) | copy-start | bytes 786436
  121.7 137.7 %collective-permute-start.30 = (f32[4,64,256]{2,1,0:T(8,128)}, f32[4,64,256]{2,1,0:T(8,128)}, u32[]{:S(2)}, u32[]{:S(2)}) collective-permute-start(f32[4,64,256]{2,1,0:T(8,128)} %get-tuple-element.12), channel_id=1, source_target_pairs={{1,0},{2,1},{3,2},{4,3},{5,4},{6,5},{7,6},{9,8},{10,9},{11,10},{12... | collective-permute-start | bytes 786440 | tf_op jit(solution)/shard_map/ppermute | solution.py:28
  127.0 0.7 copy-start.6
  127.7 131.7 %collective-permute-start.31 = (f32[4,64,256]{2,1,0:T(8,128)}, f32[4,64,256]{2,1,0:T(8,128)S(1)}, u32[]{:S(2)}, u32[]{:S(2)}) collective-permute-start(f32[4,64,256]{2,1,0:T(8,128)} %get-tuple-element.13), channel_id=1, source_target_pairs={{0,1},{1,2},{2,3},{3,4},{4,5},{5,6},{6,7},{8,9},{9,10},{10,11},{11... | collective-permute-start | bytes 786440 | tf_op jit(solution)/shard_map/ppermute | solution.py:27

commit v3 on v2

v3 whole, which is shorter than its diff:
```python
import jax
import jax.numpy as jnp
import numpy as np
from jax import lax
from jax.experimental import pallas as pl
from jax.experimental.pallas import tpu as pltpu
from jax.sharding import Mesh, PartitionSpec as P

STENCIL = (-205.0 / 72.0, 8.0 / 5.0, -1.0 / 5.0, 8.0 / 315.0, -1.0 / 560.0)
RATE = 0.2
COURANT = 0.11

AXES = ("yh", "x", "c", "yl", "z")
SIZES = {"yh": 2, "x": 4, "c": 2, "yl": 2, "z": 4}
SHOT = ("yh", "x", "c")
SLAB = ("yl", "z")


def rotate(value, axis, steps):
    count = SIZES[axis]
    return lax.ppermute(value, axis, [(i, (i + steps) % count) for i in range(count)])


def banded(length, centre):
    matrix = centre * np.eye(length)
    for reach in range(1, 5):
        matrix += STENCIL[reach] * (np.eye(length, k=reach) + np.eye(length, k=-reach))
    return jnp.asarray(matrix, jnp.float32)


def halo(last, first):
    before = lax.ppermute(last, SLAB, [(i, (i + 1) % 8) for i in range(8)])
    after = lax.ppermute(first, SLAB, [((i + 1) % 8, i) for i in range(8)])
    return before, after


def dot(a, b):
    return jnp.dot(a, b, precision=lax.Precision.HIGHEST, preferred_element_type=jnp.float32)


def inside(field, depth, width, out):
    planes = field.shape[0]
    out[...] = dot(field[...].reshape(planes * 64, 256), depth[...]).reshape(planes, 64, 256)
    for i in range(planes):
        total = dot(width[...], field[i])
        for reach in range(1, 5):
            near = [field[j] for j in (i - reach, i + reach) if 0 <= j < planes]
            total += STENCIL[reach] * sum(near[1:], near[0])
        out[i] += total


def beyond(before, after, i, planes):
    if i < 4:
        return sum(STENCIL[reach] * before[4 + i - reach] for reach in range(i + 1, 5))
    low = planes - i
    return sum(STENCIL[reach] * after[reach - low] for reach in range(low, 5))


def first_kernel(previous, current, depth, width, base, lap):
    base[...] = 2.0 * current[...] - previous[...]
    inside(current, depth, width, lap)


def second_kernel(ends, back, base, lap, current, before, after, depth, width, most, squared, first, last, one):
    for plane in range(16):
        for block in range(8):
            for half in range(2):
                value = back[8 * plane + block, 8 * half : 8 * half + 8]
                at = (plane, slice(8 * block, 8 * block + 8), slice(128 * half, 128 * half + 128))
                squared[at] = (value * COURANT) ** 2
    for i in range(16):
        total = lap[i]
        if i < 4:
            total += jnp.where(ends[0] == 0, 0.0, beyond(before, after, i, 16))
        if i >= 12:
            total += jnp.where(ends[0] == 7, 0.0, beyond(before, after, i, 16))
        one[i] = base[i] + squared[i] * total
    first[...] = one[:4]
    last[...] = one[12:]
    inside(one, depth, width, most)
    for i in range(16):
        most[i] = 2.0 * one[i] - current[i] + squared[i] * most[i]


def third_kernel(ends, most, squared, before, after, out):
    out[4:12] = most[4:12]
    for i in (0, 1, 2, 3):
        out[i] = most[i] + squared[i] * jnp.where(ends[0] == 0, 0.0, beyond(before, after, i, 16))
    for i in (12, 13, 14, 15):
        out[i] = most[i] + squared[i] * jnp.where(ends[0] == 7, 0.0, beyond(before, after, i, 16))


def on_slab(kernel, outs, *args, scalars=0, scratch=(), bytes_accessed=8 << 20):
    vmem = pl.BlockSpec(memory_space=pltpu.VMEM)
    smem = pl.BlockSpec(memory_space=pltpu.SMEM)
    return pl.pallas_call(
        kernel,
        out_shape=[jax.ShapeDtypeStruct((planes, 64, 256), jnp.float32) for planes in outs],
        in_specs=[smem] * scalars + [vmem] * (len(args) - scalars),
        out_specs=[vmem] * len(outs),
        scratch_shapes=list(scratch),
        cost_estimate=pl.CostEstimate(flops=1 << 27, bytes_accessed=bytes_accessed, transcendentals=0),
    )(*args)


def pack_kernel(place, offset, gradient, illumination, velocity, out):
    for half in range(2):
        lanes = slice(128 * half, 128 * half + 128)
        out[:, 8 * half : 8 * half + 8] = gradient[:, :, lanes]
        out[:, 16 + 8 * half : 24 + 8 * half] = illumination[:, :, lanes]
    tile = velocity[...]
    upper = lax.broadcasted_iota(jnp.int32, tile.shape, 1) // 4
    out[:, 32:] = jnp.where(upper == place[2], tile, offset[0].astype(jnp.float32))


def pack(place, offsets, gradient, illumination, velocity):
    return pl.pallas_call(
        pack_kernel,
        grid_spec=pltpu.PrefetchScalarGridSpec(
            num_scalar_prefetch=2,
            grid=(1,),
            in_specs=[pl.BlockSpec((128, 8, 256), lambda i, place, offset: (0, 0, 0))] * 2
            + [pl.BlockSpec((None, 128, 8, 128), lambda i, place, offset: (place[0], 0, 0, place[1]))],
            out_specs=pl.BlockSpec((128, 40, 128), lambda i, place, offset: (0, 0, 0)),
        ),
        out_shape=jax.ShapeDtypeStruct((128, 40, 128), gradient.dtype),
        cost_estimate=pl.CostEstimate(flops=0, bytes_accessed=5 << 20, transcendentals=0),
    )(
        place,
        offsets,
        gradient.reshape(128, 8, 256),
        illumination.reshape(128, 8, 256),
        velocity.reshape(4, 128, 8, 256),
    )


def model_kernel(offs, sent, early, out, grad, illum):
    grad[...] = jnp.zeros_like(grad)
    illum[...] = jnp.zeros_like(illum)
    for shot in range(16):
        first = offs[shot]
        grad[pl.ds(first, 8)] += sent[8 * shot : 8 * shot + 8, :16]
        illum[pl.ds(first, 8)] += sent[8 * shot : 8 * shot + 8, 16:32]
    for pair in range(8):
        slabs, rows = pl.ds(8 * (pair // 2), 8), pl.ds(8 * (pair % 2), 8)
        low = sent[16 * pair : 16 * pair + 8, 32:]
        high = sent[16 * pair + 8 : 16 * pair + 16, 32:]
        velocity = jnp.where(lax.broadcasted_iota(jnp.int32, low.shape, 1) < 4, low, high)
        new = velocity - RATE * grad[slabs, rows] / (illum[slabs, rows] + 1.0)
        grad[slabs, rows] = new
        out[16 * pair : 16 * pair + 8, 16:] = new
        out[16 * pair + 8 : 16 * pair + 16, 16:] = new
    for shot in range(16):
        out[8 * shot : 8 * shot + 8, :16] = grad[pl.ds(offs[shot], 8)]


def update_model(offs, sent, early):
    vmem = pl.BlockSpec(memory_space=pltpu.VMEM)
    return pl.pallas_call(
        model_kernel,
        out_shape=jax.ShapeDtypeStruct((128, 24, 128), sent.dtype),
        in_specs=[pl.BlockSpec(memory_space=pltpu.SMEM), vmem, pl.BlockSpec(memory_space=pl.ANY)],
        out_specs=vmem,
        scratch_shapes=[pltpu.VMEM((32, 16, 128), sent.dtype)] * 2,
        cost_estimate=pl.CostEstimate(flops=1 << 20, bytes_accessed=4 << 20, transcendentals=0),
    )(offs, sent, early)


def place_kernel(spots, *refs):
    pieces, out, sems = refs[:16], refs[16], refs[17]
    copies = []
    for i, piece in enumerate(pieces):
        chip, core = spots[2 * i], spots[2 * i + 1]
        planes = pl.ds(pl.multiple_of(8 * core, 8), 8)
        lanes = pl.ds(pl.multiple_of(128 * lax.rem(chip, 2), 128), 128)
        target = out.at[lax.div(chip, 2), planes, :, lanes]
        copies.append(pltpu.make_async_copy(piece, target, sems.at[i]))
    for copy in copies:
        copy.start()
    for copy in copies:
        copy.wait()


def place_pieces(spots, pieces):
    vmem = pl.BlockSpec(memory_space=pltpu.VMEM)
    return pl.pallas_call(
        place_kernel,
        out_shape=jax.ShapeDtypeStruct((4, 16, 64, 256), pieces[0].dtype),
        in_specs=[pl.BlockSpec(memory_space=pltpu.SMEM)] + [vmem] * 16,
        out_specs=pl.BlockSpec(memory_space=pltpu.HBM),
        scratch_shapes=[pltpu.SemaphoreType.DMA((16,))],
        cost_estimate=pl.CostEstimate(flops=0, bytes_accessed=1 << 27, transcendentals=0),
    )(spots, *pieces)


def gather_model(own, between):
    yh, x, c = (lax.axis_index(a) for a in SHOT)
    first = [rotate(own, "x", k) for k in (1, 2, 3)] + [rotate(own, "yh", 1)]
    first, between = lax.optimization_barrier((first, between))
    found = [(own, 0, 0)] + [(first[k - 1], 0, k) for k in (1, 2, 3)]
    found.append((first[3], 1, 0))
    found += [(rotate(first[3], "x", k), 1, k) for k in (1, 3)]
    found.append((rotate(first[1], "yh", 1), 1, 2))
    pieces, spots = [], []
    for value, dy, dx in found:
        chip = ((yh + dy) % 2) * 4 + (x - dx) % 4
        pieces += [value, rotate(value, "c", 1)]
        spots += [chip, c, chip, 1 - c]
    return place_pieces(jnp.stack(spots).astype(jnp.int32), pieces), between


def on_device(gradient, illumination, u_prev, u_cur, velocity, offsets):
    u_prev, u_cur = u_prev[0], u_cur[0]
    yh, x, c = (lax.axis_index(a) for a in SHOT)
    place = jnp.stack([2 * yh + x // 2, x % 2, c, lax.axis_index(SLAB)]).astype(jnp.int32)

    sent = pack(place, offsets, gradient, illumination, velocity)
    sent = lax.all_to_all(sent, AXES, 0, 0)
    low, high = sent[0::16, 36, 0], sent[8::16, 32, 0]
    offs = jnp.stack([low, high], axis=1).reshape(16).astype(jnp.int32)

    back = lax.all_to_all(update_model(offs, sent, u_cur), AXES, 0, 0)

    depth, width = banded(256, 3.0 * STENCIL[0]), banded(64, 0.0)
    base, lap = on_slab(first_kernel, (16, 16), u_prev, u_cur, depth, width)
    around = halo(u_cur[12:], u_cur[:4])
    back, base, lap = lax.optimization_barrier((back, base, lap))

    own = lax.dynamic_slice(back, (64 * c, 16, 0), (64, 8, 128)).reshape(8, 64, 128)
    field = pltpu.VMEM((16, 64, 256), jnp.float32)
    step = on_slab(
        second_kernel, (16, 16, 4, 4), place[3:], back, base, lap, u_cur, *around, depth, width,
        scalars=1, scratch=[field],
    )
    new_model, (most, squared, first, last) = gather_model(own, tuple(step))
    around = halo(last, first)
    (final,) = on_slab(third_kernel, (16,), place[3:], most, squared, *around, scalars=1)
    return new_model, final[None]


def solution(mesh):
    fine = Mesh(mesh.devices.reshape(tuple(SIZES[a] for a in AXES)), AXES)
    field = P(SHOT, SLAB, None, None)
    model = P(None, SLAB, None, None)
    return jax.shard_map(
        on_device,
        mesh=fine,
        in_specs=(field, field, field, field, model, P(SHOT)),
        out_specs=(model, field),
        check_vma=False,
    )
```

time: 265 us -> 134 us (0.51)
  Pallas kernels: 134 us -> 25.2 us
  blocking collectives: 0 us -> 45.7 us
  starting transfers between devices: 72.4 us -> 33.8 us
  waiting for transfers between devices: 34.9 us -> 21.5 us
  other arithmetic: 13.8 us -> 0.67 us
  local copies, waits for them, and re-layouts: 7.42 us -> 3.03 us
    pallas_call x3 -> x6, Pallas kernels: 134 us -> 25.2 us  [the longest x3 13.6 us: on_slab(): pl.pallas_call(kernel, out_shape=[jax.ShapeDtypeStruct((planes, 64, 256),...]
    all_to_all x0 -> x1, blocking collectives: none -> 45.7 us  [on_device(): sent = lax.all_to_all(sent, AXES, 0, 0)]
    ppermute x28 -> x15, waiting for transfers between devices: 34.8 us -> 4.43 us  [rotate(): lax.ppermute(value, axis, [(i, (i + steps) % count) for i in range(count)])]
    ppermute x28 -> x15, starting transfers between devices: 39.8 us -> 21.5 us  [rotate(): lax.ppermute(value, axis, [(i, (i + steps) % count) for i in range(count)])]
    all_to_all x2 -> x1, waiting for transfers between devices: 0.01 us -> 15.9 us  [on_device(): back = lax.all_to_all(update_model(offs, sent, u_cur), AXES, 0, 0)]
    all_to_all x2 -> x1, starting transfers between devices: 20.2 us -> 5.56 us  [on_device(): back = lax.all_to_all(update_model(offs, sent, u_cur), AXES, 0, 0)]
    ppermute x4, starting transfers between devices: 12.4 us -> 6.78 us  [the longest x2 5.29 us: halo(): after = lax.ppermute(first, SLAB, [((i + 1) % 8, i) for i in range(8)])]
    add x4 -> x0, other arithmetic: 5.4 us -> none  [the longest x1 4.85 us: on_device(): one = base + squared * first_lap]
  transfers between devices with their start and end apart: 34 -> 20, of which waited for: 8 -> 4; matrix products, arithmetic and copies ran while one was open for 4% -> 1% of each run, Pallas kernels for 49% -> 10%
where the time goes in v3:
time: 134 us; the launch traced here: 131 us
  blocking collectives  45.7 us (34%)
  starting transfers between devices  33.8 us (25%)
  Pallas kernels  25.2 us (19%)
  waiting for transfers between devices  21.5 us (16%)
  local copies, waits for them, and re-layouts  3.03 us (2%)
  between operations  1.55 us (1%)
    all_to_all x1, blocking collectives, on_device(): sent = lax.all_to_all(sent, AXES, 0, 0)  45.7 us
    ppermute x15, starting transfers between devices, rotate(): lax.ppermute(value, axis, [(i, (i + steps) % count) for i in range(count)])  21.5 us
    all_to_all x1, waiting for transfers between devices, on_device(): back = lax.all_to_all(update_model(offs, sent, u_cur), AXES, 0, 0)  15.9 us
    pallas_call x3, Pallas kernels, on_slab(): pl.pallas_call(kernel, out_shape=[jax.ShapeDtypeStruct((planes, 64, 256),...  13.6 us
    all_to_all x1, starting transfers between devices, on_device(): back = lax.all_to_all(update_model(offs, sent, u_cur), AXES, 0, 0)  5.56 us
    ppermute x2, starting transfers between devices, halo(): after = lax.ppermute(first, SLAB, [((i + 1) % 8, i) for i in range(8)])  5.29 us
    ppermute x15, waiting for transfers between devices, rotate(): lax.ppermute(value, axis, [(i, (i + steps) % count) for i in range(count)])  4.43 us
    pallas_call x1, Pallas kernels, place_pieces(): pl.pallas_call(place_kernel, out_shape=jax.ShapeDtypeStruct((4, 16, 64, 2...  4.29 us
  transfers between devices with their start and end apart: 20, of which 4 were waited for; matrix products, arithmetic and copies ran while one was open for 1% of the time, Pallas kernels for 10%

profile of v3, /device:TPU:9, one launch (start us, length us, event | category | flops | bytes accessed | tf_op | source)
XLA Modules:
  0.0 131.5 jit_solution(15100170346382141358)
XLA Ops:
  1.3 0.7 pad_add_fusion.place
  2.0 4.0 %shard_map.95 = f32[128,40,128]{2,1,0:T(8,128)} custom-call(s32[4]{0:T(128)} %pad_add_fusion.place, s32[1]{0:T(128)S(6)} %copy.12.offset, f32[128,8,256]{2,1,0:T(8,128)} %bitcast.30, f32[128,8,256]{2,1,0:T(8,128)} %bitcast.31, f32[4,128,8,256]{3,2,1,0:T(8,128)} %bitcast.29), custom_call_target="tpu_custom_call" | custom-call | bytes 5242880 | tf_op jit(solution)/shard_map/pallas_call | solution.py:117
  6.0 45.7 %all_to_all.10.sent = f32[128,40,128]{2,1,0:T(8,128)S(1)} all-to-all(f32[128,40,128]{2,1,0:T(8,128)} %shard_map.95), channel_id=1, replica_groups=mesh['yh'=2,'x'=4,'c'=2,'yl'=2,'z'=4] {'yh','x','c','yl','z'}, dimensions={0} | all-to-all | bytes 5242880 | tf_op jit(solution)/shard_map/all_to_all | solution.py:218
  51.6 0.1 slice_reduce_fusion.1
  51.8 0.1 copy.11
  51.9 0.8 convert_element_type.6.offs
  52.7 0.4 copy-done.1
  53.1 3.3 %shard_map.96 = f32[128,24,128]{2,1,0:T(8,128)} custom-call(s32[16]{0:T(128)} %convert_element_type.6.offs, f32[128,40,128]{2,1,0:T(8,128)} %copy-done.1, f32[16,64,256]{2,1,0:T(8,128)} %bitcast.26), custom_call_target="tpu_custom_call" | custom-call | flops 1048576 | bytes 4194304 | tf_op jit(solution)/shard_map/pallas_call | solution.py:159
  56.5 5.6 %all-to-all-start.1 = ((f32[128,24,128]{2,1,0:T(8,128)}), f32[128,24,128]{2,1,0:T(8,128)S(1)}, u32[]{:S(2)}, u32[]{:S(2)}) async-start(f32[128,24,128]{2,1,0:T(8,128)} %shard_map.96), calls=%async_computation.1 | async-start | bytes 3145728 | tf_op jit(solution)/shard_map/all_to_all | solution.py:222
  62.0 0.0 copy-done
  62.1 3.2 %collective-permute-start.6 = (f32[4,64,256]{2,1,0:T(8,128)S(1)}, f32[4,64,256]{2,1,0:T(8,128)S(1)}, u32[]{:S(2)}, u32[]{:S(2)}) collective-permute-start(f32[4,64,256]{2,1,0:T(8,128)S(1)} %get-tuple-element.38), channel_id=1, source_target_pairs={{1,0},{2,1},{3,2},{4,3},{5,4},{6,5},{7,6},{0,7},{9,8},{10,9},{11,1... | collective-permute-start | bytes 786440 | tf_op jit(solution)/shard_map/ppermute | solution.py:33
  65.3 0.0 collective-permute-start.5
  65.3 4.9 %shard_map.97 = (f32[16,64,256]{2,1,0:T(8,128)}, f32[16,64,256]{2,1,0:T(8,128)}) custom-call(f32[16,64,256]{2,1,0:T(8,128)} %bitcast.38, f32[16,64,256]{2,1,0:T(8,128)} %bitcast.27, f32[256,256]{1,0:T(8,128)} %constant.112.clone.depth, f32[64,64]{1,0:T(8,128)} %constant.113.clone.width), custom_call_target="tpu_custom_call" | custom-call | flops 134217728 | bytes 8388608 | tf_op jit(solution)/shard_map/pallas_call | solution.py:96
  70.2 15.9 %all-to-all-done.1.back = f32[128,24,128]{2,1,0:T(8,128)S(1)} async-done(((f32[128,24,128]{2,1,0:T(8,128)}), f32[128,24,128]{2,1,0:T(8,128)S(1)}, u32[]{:S(2)}, u32[]{:S(2)}) %all-to-all-start.1) | async-done | bytes 1572896 | tf_op jit(solution)/shard_map/all_to_all | solution.py:222
  86.2 0.0 copy-start.3
  86.2 0.8 collective-permute-start.4
  87.0 1.3 collective-permute-start.3
  88.2 0.9 collective-permute-start.2
  89.1 0.0 collective-permute-done.6.after
  89.1 0.0 collective-permute-start.1
  89.1 0.0 collective-permute-done.5.before
  89.1 3.8 %collective-permute-start = (f32[8,64,128]{2,1,0:T(8,128)S(1)}, f32[8,64,128]{2,1,0:T(8,128)S(1)}, u32[]{:S(2)}, u32[]{:S(2)}) collective-permute-start(f32[8,64,128]{2,1,0:T(8,128)S(1)} %bitcast.36), channel_id=1, source_target_pairs={{0,8},{8,0},{1,9},{9,1},{2,10},{10,2},{3,11},{11,3},{4,12},{12,4},... | collective-permute-start | bytes 786440 | tf_op jit(solution)/shard_map/ppermute | solution.py:21
  92.9 0.0 copy-done.2
  92.9 0.0 copy-done.17
  92.9 5.9 %shard_map.98 = (f32[16,64,256]{2,1,0:T(8,128)}, f32[16,64,256]{2,1,0:T(8,128)}, f32[4,64,256]{2,1,0:T(8,128)}, f32[4,64,256]{2,1,0:T(8,128)}) custom-call(s32[1]{0:T(128)} %bitcast.12.ends, f32[128,24,128]{2,1,0:T(8,128)} %copy-done.2, f32[16,64,256]{2,1,0:T(8,128)} %get-tuple-element.22.base, f32[16,64,256]{2,1,0:T(8,128)} %get-tuple-element.23.lap, ...), custom_call_target="tpu_custom_call" | custom-call | flops 134217728 | bytes 8388608 | tf_op jit(solution)/shard_map/pallas_call | solution.py:96
  98.8 0.0 copy-done.3
  98.8 0.0 collective-permute-done.4.refs_8_
  98.8 0.0 copy-start.4
  98.8 0.0 collective-permute-done.3.refs_6_
  98.8 0.0 copy-start.5
  98.8 0.0 collective-permute-done.2.refs_4_
  98.8 0.0 copy-start.6
  98.9 3.6 %collective-permute-done.1.refs_2_ = f32[8,64,128]{2,1,0:T(8,128)S(1)} collective-permute-done((f32[8,64,128]{2,1,0:T(8,128)S(1)}, f32[8,64,128]{2,1,0:T(8,128)S(1)}, u32[]{:S(2)}, u32[]{:S(2)}) %collective-permute-start.1) | collective-permute-done | bytes 262176 | tf_op jit(solution)/shard_map/ppermute | solution.py:21
  102.5 1.5 %collective-permute-start.17 = (f32[4,64,256]{2,1,0:T(8,128)}, f32[4,64,256]{2,1,0:T(8,128)}, u32[]{:S(2)}, u32[]{:S(2)}) collective-permute-start(f32[4,64,256]{2,1,0:T(8,128)} %get-tuple-element.34), channel_id=1, source_target_pairs={{0,1},{1,2},{2,3},{3,4},{4,5},{5,6},{6,7},{7,0},{8,9},{9,10},{10,1... | collective-permute-start | bytes 786440 | tf_op jit(solution)/shard_map/ppermute | solution.py:32
  103.9 2.1 %collective-permute-start.18 = (f32[4,64,256]{2,1,0:T(8,128)}, f32[4,64,256]{2,1,0:T(8,128)}, u32[]{:S(2)}, u32[]{:S(2)}) collective-permute-start(f32[4,64,256]{2,1,0:T(8,128)} %get-tuple-element.35), channel_id=1, source_target_pairs={{1,0},{2,1},{3,2},{4,3},{5,4},{6,5},{7,6},{0,7},{9,8},{10,9},{11,1... | collective-permute-start | bytes 786440 | tf_op jit(solution)/shard_map/ppermute | solution.py:33
  106.0 2.2 %collective-permute-start.7 = (f32[8,64,128]{2,1,0:T(8,128)S(1)}, f32[8,64,128]{2,1,0:T(8,128)S(1)}, u32[]{:S(2)}, u32[]{:S(2)}) collective-permute-start(f32[8,64,128]{2,1,0:T(8,128)S(1)} %collective-permute-done.1.refs_2_), channel_id=1, source_target_pairs={{0,8},{8,0},{1,9},{9,1},{2,10},{10,2},{3,11},{11,3},{4,12},{12,4},... | collective-permute-start | bytes 786440 | tf_op jit(solution)/shard_map/ppermute | solution.py:21
  108.2 0.0 collective-permute-start.9
  108.2 0.0 collective-permute-done.refs_1_
  108.2 1.6 %collective-permute-start.15 = (f32[8,64,128]{2,1,0:T(8,128)S(1)}, f32[8,64,128]{2,1,0:T(8,128)S(1)}, u32[]{:S(2)}, u32[]{:S(2)}) collective-permute-start(f32[8,64,128]{2,1,0:T(8,128)S(1)} %collective-permute-done.2.refs_4_), channel_id=1, source_target_pairs={{0,64},{64,0},{1,65},{65,1},{2,66},{66,2},{3,67},{67,3},{4,68},{68... | collective-permute-start | bytes 786440 | tf_op jit(solution)/shard_map/ppermute | solution.py:21
  109.9 1.2 collective-permute-done.17.before
  111.0 0.6 collective-permute-start.13
  111.7 0.0 collective-permute-done.18.after
  111.7 0.9 collective-permute-start.11
  112.5 0.0 collective-permute-done.7.refs_3_
  112.5 4.7 %collective-permute-start.8 = (f32[8,64,128]{2,1,0:T(8,128)S(1)}, f32[8,64,128]{2,1,0:T(8,128)S(1)}, u32[]{:S(2)}, u32[]{:S(2)}) collective-permute-start(f32[8,64,128]{2,1,0:T(8,128)S(1)} %collective-permute-done.2.refs_4_), channel_id=1, source_target_pairs={{0,8},{8,0},{1,9},{9,1},{2,10},{10,2},{3,11},{11,3},{4,12},{12,4},... | collective-permute-start | bytes 786440 | tf_op jit(solution)/shard_map/ppermute | solution.py:21
  117.2 0.0 collective-permute-done.9.refs_7_
  117.2 0.1 collective-permute-start.10
  117.3 0.8 collective-permute-done.15.refs_14_
  118.2 2.1 %collective-permute-start.16 = (f32[8,64,128]{2,1,0:T(8,128)S(1)}, f32[8,64,128]{2,1,0:T(8,128)S(1)}, u32[]{:S(2)}, u32[]{:S(2)}) collective-permute-start(f32[8,64,128]{2,1,0:T(8,128)S(1)} %collective-permute-done.15.refs_14_), channel_id=1, source_target_pairs={{0,8},{8,0},{1,9},{9,1},{2,10},{10,2},{3,11},{11,3},{4,12},{12,4},... | collective-permute-start | bytes 786440 | tf_op jit(solution)/shard_map/ppermute | solution.py:21
  120.2 0.0 collective-permute-done.13.refs_12_
  120.2 1.4 %collective-permute-start.14 = (f32[8,64,128]{2,1,0:T(8,128)S(1)}, f32[8,64,128]{2,1,0:T(8,128)}, u32[]{:S(2)}, u32[]{:S(2)}) collective-permute-start(f32[8,64,128]{2,1,0:T(8,128)S(1)} %collective-permute-done.13.refs_12_), channel_id=1, source_target_pairs={{0,8},{8,0},{1,9},{9,1},{2,10},{10,2},{3,11},{11,3},{4,12},{12,4},... | collective-permute-start | bytes 786440 | tf_op jit(solution)/shard_map/ppermute | solution.py:21
  121.6 0.0 collective-permute-done.11.refs_10_
  121.6 1.2 collective-permute-start.12
  122.8 0.7 stack.81.spots
  123.5 2.8 %shard_map.100 = f32[16,64,256]{2,1,0:T(8,128)} custom-call(s32[1]{0:T(128)} %bitcast.12.ends, f32[16,64,256]{2,1,0:T(8,128)} %get-tuple-element.32.most, f32[16,64,256]{2,1,0:T(8,128)} %get-tuple-element.33.squared, f32[4,64,256]{2,1,0:T(8,128)} %collective-permute-done.17.before, f32[4,64,256]{2,1,0:T(8,128)} %collective-permute-done.18.after), custom_call_target="tpu_custom_call" | custom-call | flops 134217728 | bytes 8388608 | tf_op jit(solution)/shard_map/pallas_call | solution.py:96
  126.3 0.0 collective-permute-done.8.refs_5_
  126.3 0.0 collective-permute-done.10.refs_9_
  126.3 0.0 collective-permute-done.16.refs_15_
  126.3 0.0 collective-permute-done.14.refs_13_
  126.4 0.0 collective-permute-done.12.refs_11_
  126.5 0.5 copy-done.14
  127.0 0.1 copy-done.15
  127.1 0.1 copy-done.16
  127.2 4.3 %shard_map.99 = f32[4,16,64,256]{3,2,1,0:T(8,128)} custom-call(s32[32]{0:T(128)} %stack.81.spots, f32[8,64,128]{2,1,0:T(8,128)} %bitcast.37, f32[8,64,128]{2,1,0:T(8,128)} %copy-done.8, f32[8,64,128]{2,1,0:T(8,128)} %copy-done.7, f32[8,64,128]{2,1,0:T(8,128)} %copy-done.9, f32[8,64,128]{2,1,0:T(8,128)} %copy-done.6, f32[8,64,128]{2,1,0:T(8,128)} %copy-done.14, ...), custom_call_target="tpu_custom_call" | custom-call | bytes 134217728 | tf_op jit(solution)/shard_map/pallas_call | solution.py:186
  (27 shorter events, 0.1 us)
Async XLA Ops:
  51.6 1.5 %copy-start.1 = (f32[128,40,128]{2,1,0:T(8,128)}, f32[128,40,128]{2,1,0:T(8,128)S(1)}, u32[]{:S(2)}) copy-start(f32[128,40,128]{2,1,0:T(8,128)S(1)} %all_to_all.10.sent) | copy-start | bytes 7864324
  56.5 5.6 %copy-start = (f32[1,16,64,256]{3,2,1,0:T(8,128)S(1)}, f32[1,16,64,256]{3,2,1,0:T(8,128)}, u32[]{:S(2)}) copy-start(f32[1,16,64,256]{3,2,1,0:T(8,128)} %param.11) | copy-start | bytes 3145732
  56.5 29.7 %all-to-all-start.1 = ((f32[128,24,128]{2,1,0:T(8,128)}), f32[128,24,128]{2,1,0:T(8,128)S(1)}, u32[]{:S(2)}, u32[]{:S(2)}) async-start(f32[128,24,128]{2,1,0:T(8,128)} %shard_map.96), calls=%async_computation.1 | async-start | bytes 3145728 | tf_op jit(solution)/shard_map/all_to_all | solution.py:222
  62.1 27.0 %collective-permute-start.6 = (f32[4,64,256]{2,1,0:T(8,128)S(1)}, f32[4,64,256]{2,1,0:T(8,128)S(1)}, u32[]{:S(2)}, u32[]{:S(2)}) collective-permute-start(f32[4,64,256]{2,1,0:T(8,128)S(1)} %get-tuple-element.38), channel_id=1, source_target_pairs={{1,0},{2,1},{3,2},{4,3},{5,4},{6,5},{7,6},{0,7},{9,8},{10,9},{11,1... | collective-permute-start | bytes 786440 | tf_op jit(solution)/shard_map/ppermute | solution.py:33
  65.3 23.8 %collective-permute-start.5 = (f32[4,64,256]{2,1,0:T(8,128)S(1)}, f32[4,64,256]{2,1,0:T(8,128)}, u32[]{:S(2)}, u32[]{:S(2)}) collective-permute-start(f32[4,64,256]{2,1,0:T(8,128)S(1)} %get-tuple-element.39), channel_id=1, source_target_pairs={{0,1},{1,2},{2,3},{3,4},{4,5},{5,6},{6,7},{7,0},{8,9},{9,10},{10,1... | collective-permute-start | bytes 786440 | tf_op jit(solution)/shard_map/ppermute | solution.py:32
  86.1 6.8 %copy-start.2 = (f32[128,24,128]{2,1,0:T(8,128)}, f32[128,24,128]{2,1,0:T(8,128)S(1)}, u32[]{:S(2)}) copy-start(f32[128,24,128]{2,1,0:T(8,128)S(1)} %all-to-all-done.1.back) | copy-start | bytes 4718596
  86.2 12.6 %copy-start.3 = (f32[64,8,128]{2,1,0:T(8,128)}, f32[64,8,128]{2,1,0:T(8,128)S(1)}, u32[]{:S(2)}) copy-start(f32[64,8,128]{2,1,0:T(8,128)S(1)} %constant_dynamic-slice_fusion) | copy-start | bytes 786436
  86.2 12.6 %collective-permute-start.4 = (f32[8,64,128]{2,1,0:T(8,128)S(1)}, f32[8,64,128]{2,1,0:T(8,128)S(1)}, u32[]{:S(2)}, u32[]{:S(2)}) collective-permute-start(f32[8,64,128]{2,1,0:T(8,128)S(1)} %bitcast.32), channel_id=1, source_target_pairs={{0,64},{64,0},{1,65},{65,1},{2,66},{66,2},{3,67},{67,3},{4,68},{68... | collective-permute-start | bytes 786440 | tf_op jit(solution)/shard_map/ppermute | solution.py:21
  87.0 11.8 %collective-permute-start.3 = (f32[8,64,128]{2,1,0:T(8,128)S(1)}, f32[8,64,128]{2,1,0:T(8,128)S(1)}, u32[]{:S(2)}, u32[]{:S(2)}) collective-permute-start(f32[8,64,128]{2,1,0:T(8,128)S(1)} %bitcast.33), channel_id=1, source_target_pairs={{0,48},{16,0},{32,16},{48,32},{1,49},{17,1},{33,17},{49,33},{2,50}... | collective-permute-start | bytes 786440 | tf_op jit(solution)/shard_map/ppermute | solution.py:21
  88.2 10.6 %collective-permute-start.2 = (f32[8,64,128]{2,1,0:T(8,128)S(1)}, f32[8,64,128]{2,1,0:T(8,128)S(1)}, u32[]{:S(2)}, u32[]{:S(2)}) collective-permute-start(f32[8,64,128]{2,1,0:T(8,128)S(1)} %bitcast.34), channel_id=1, source_target_pairs={{0,32},{16,48},{32,0},{48,16},{1,33},{17,49},{33,1},{49,17},{2,34}... | collective-permute-start | bytes 786440 | tf_op jit(solution)/shard_map/ppermute | solution.py:21
  89.1 3.8 %copy-start.17 = (f32[4,64,256]{2,1,0:T(8,128)}, f32[4,64,256]{2,1,0:T(8,128)S(1)}, u32[]{:S(2)}) copy-start(f32[4,64,256]{2,1,0:T(8,128)S(1)} %collective-permute-done.6.after) | copy-start | bytes 786436
  89.1 13.3 %collective-permute-start.1 = (f32[8,64,128]{2,1,0:T(8,128)S(1)}, f32[8,64,128]{2,1,0:T(8,128)S(1)}, u32[]{:S(2)}, u32[]{:S(2)}) collective-permute-start(f32[8,64,128]{2,1,0:T(8,128)S(1)} %bitcast.35), channel_id=1, source_target_pairs={{0,16},{16,32},{32,48},{48,0},{1,17},{17,33},{33,49},{49,1},{2,18}... | collective-permute-start | bytes 786440 | tf_op jit(solution)/shard_map/ppermute | solution.py:21
  89.1 19.1 %collective-permute-start = (f32[8,64,128]{2,1,0:T(8,128)S(1)}, f32[8,64,128]{2,1,0:T(8,128)S(1)}, u32[]{:S(2)}, u32[]{:S(2)}) collective-permute-start(f32[8,64,128]{2,1,0:T(8,128)S(1)} %bitcast.36), channel_id=1, source_target_pairs={{0,8},{8,0},{1,9},{9,1},{2,10},{10,2},{3,11},{11,3},{4,12},{12,4},... | collective-permute-start | bytes 786440 | tf_op jit(solution)/shard_map/ppermute | solution.py:21
  98.8 27.6 %copy-start.4 = (f32[8,64,128]{2,1,0:T(8,128)}, f32[8,64,128]{2,1,0:T(8,128)S(1)}, u32[]{:S(2)}) copy-start(f32[8,64,128]{2,1,0:T(8,128)S(1)} %collective-permute-done.4.refs_8_) | copy-start | bytes 786436
  98.8 27.6 %copy-start.5 = (f32[8,64,128]{2,1,0:T(8,128)}, f32[8,64,128]{2,1,0:T(8,128)S(1)}, u32[]{:S(2)}) copy-start(f32[8,64,128]{2,1,0:T(8,128)S(1)} %collective-permute-done.3.refs_6_) | copy-start | bytes 786436
  98.8 27.5 %copy-start.6 = (f32[8,64,128]{2,1,0:T(8,128)}, f32[8,64,128]{2,1,0:T(8,128)S(1)}, u32[]{:S(2)}) copy-start(f32[8,64,128]{2,1,0:T(8,128)S(1)} %collective-permute-done.2.refs_4_) | copy-start | bytes 786436
  102.4 24.0 %copy-start.7 = (f32[8,64,128]{2,1,0:T(8,128)}, f32[8,64,128]{2,1,0:T(8,128)S(1)}, u32[]{:S(2)}) copy-start(f32[8,64,128]{2,1,0:T(8,128)S(1)} %collective-permute-done.1.refs_2_) | copy-start | bytes 786436
  102.5 8.6 %collective-permute-start.17 = (f32[4,64,256]{2,1,0:T(8,128)}, f32[4,64,256]{2,1,0:T(8,128)}, u32[]{:S(2)}, u32[]{:S(2)}) collective-permute-start(f32[4,64,256]{2,1,0:T(8,128)} %get-tuple-element.34), channel_id=1, source_target_pairs={{0,1},{1,2},{2,3},{3,4},{4,5},{5,6},{6,7},{7,0},{8,9},{9,10},{10,1... | collective-permute-start | bytes 786440 | tf_op jit(solution)/shard_map/ppermute | solution.py:32
  103.9 7.7 %collective-permute-start.18 = (f32[4,64,256]{2,1,0:T(8,128)}, f32[4,64,256]{2,1,0:T(8,128)}, u32[]{:S(2)}, u32[]{:S(2)}) collective-permute-start(f32[4,64,256]{2,1,0:T(8,128)} %get-tuple-element.35), channel_id=1, source_target_pairs={{1,0},{2,1},{3,2},{4,3},{5,4},{6,5},{7,6},{0,7},{9,8},{10,9},{11,1... | collective-permute-start | bytes 786440 | tf_op jit(solution)/shard_map/ppermute | solution.py:33
  106.0 6.5 %collective-permute-start.7 = (f32[8,64,128]{2,1,0:T(8,128)S(1)}, f32[8,64,128]{2,1,0:T(8,128)S(1)}, u32[]{:S(2)}, u32[]{:S(2)}) collective-permute-start(f32[8,64,128]{2,1,0:T(8,128)S(1)} %collective-permute-done.1.refs_2_), channel_id=1, source_target_pairs={{0,8},{8,0},{1,9},{9,1},{2,10},{10,2},{3,11},{11,3},{4,12},{12,4},... | collective-permute-start | bytes 786440 | tf_op jit(solution)/shard_map/ppermute | solution.py:21
  108.2 9.0 %collective-permute-start.9 = (f32[8,64,128]{2,1,0:T(8,128)S(1)}, f32[8,64,128]{2,1,0:T(8,128)S(1)}, u32[]{:S(2)}, u32[]{:S(2)}) collective-permute-start(f32[8,64,128]{2,1,0:T(8,128)S(1)} %collective-permute-done.3.refs_6_), channel_id=1, source_target_pairs={{0,8},{8,0},{1,9},{9,1},{2,10},{10,2},{3,11},{11,3},{4,12},{12,4},... | collective-permute-start | bytes 786440 | tf_op jit(solution)/shard_map/ppermute | solution.py:21
  108.2 18.2 %copy-start.8 = (f32[8,64,128]{2,1,0:T(8,128)}, f32[8,64,128]{2,1,0:T(8,128)S(1)}, u32[]{:S(2)}) copy-start(f32[8,64,128]{2,1,0:T(8,128)S(1)} %collective-permute-done.refs_1_) | copy-start | bytes 786436
  108.2 9.9 %collective-permute-start.15 = (f32[8,64,128]{2,1,0:T(8,128)S(1)}, f32[8,64,128]{2,1,0:T(8,128)S(1)}, u32[]{:S(2)}, u32[]{:S(2)}) collective-permute-start(f32[8,64,128]{2,1,0:T(8,128)S(1)} %collective-permute-done.2.refs_4_), channel_id=1, source_target_pairs={{0,64},{64,0},{1,65},{65,1},{2,66},{66,2},{3,67},{67,3},{4,68},{68... | collective-permute-start | bytes 786440 | tf_op jit(solution)/shard_map/ppermute | solution.py:21
  111.0 9.2 %collective-permute-start.13 = (f32[8,64,128]{2,1,0:T(8,128)S(1)}, f32[8,64,128]{2,1,0:T(8,128)S(1)}, u32[]{:S(2)}, u32[]{:S(2)}) collective-permute-start(f32[8,64,128]{2,1,0:T(8,128)S(1)} %collective-permute-done.4.refs_8_), channel_id=1, source_target_pairs={{0,48},{16,0},{32,16},{48,32},{1,49},{17,1},{33,17},{49,33},{2,50}... | collective-permute-start | bytes 786440 | tf_op jit(solution)/shard_map/ppermute | solution.py:21
  111.7 9.9 %collective-permute-start.11 = (f32[8,64,128]{2,1,0:T(8,128)S(1)}, f32[8,64,128]{2,1,0:T(8,128)S(1)}, u32[]{:S(2)}, u32[]{:S(2)}) collective-permute-start(f32[8,64,128]{2,1,0:T(8,128)S(1)} %collective-permute-done.4.refs_8_), channel_id=1, source_target_pairs={{0,16},{16,32},{32,48},{48,0},{1,17},{17,33},{33,49},{49,1},{2,18}... | collective-permute-start | bytes 786440 | tf_op jit(solution)/shard_map/ppermute | solution.py:21
  112.5 13.9 %copy-start.9 = (f32[8,64,128]{2,1,0:T(8,128)}, f32[8,64,128]{2,1,0:T(8,128)S(1)}, u32[]{:S(2)}) copy-start(f32[8,64,128]{2,1,0:T(8,128)S(1)} %collective-permute-done.7.refs_3_) | copy-start | bytes 786436
  112.5 13.8 %collective-permute-start.8 = (f32[8,64,128]{2,1,0:T(8,128)S(1)}, f32[8,64,128]{2,1,0:T(8,128)S(1)}, u32[]{:S(2)}, u32[]{:S(2)}) collective-permute-start(f32[8,64,128]{2,1,0:T(8,128)S(1)} %collective-permute-done.2.refs_4_), channel_id=1, source_target_pairs={{0,8},{8,0},{1,9},{9,1},{2,10},{10,2},{3,11},{11,3},{4,12},{12,4},... | collective-permute-start | bytes 786440 | tf_op jit(solution)/shard_map/ppermute | solution.py:21
  117.2 9.2 %copy-start.10 = (f32[8,64,128]{2,1,0:T(8,128)}, f32[8,64,128]{2,1,0:T(8,128)S(1)}, u32[]{:S(2)}) copy-start(f32[8,64,128]{2,1,0:T(8,128)S(1)} %collective-permute-done.9.refs_7_) | copy-start | bytes 786436
  117.2 9.1 %collective-permute-start.10 = (f32[8,64,128]{2,1,0:T(8,128)S(1)}, f32[8,64,128]{2,1,0:T(8,128)S(1)}, u32[]{:S(2)}, u32[]{:S(2)}) collective-permute-start(f32[8,64,128]{2,1,0:T(8,128)S(1)} %collective-permute-done.4.refs_8_), channel_id=1, source_target_pairs={{0,8},{8,0},{1,9},{9,1},{2,10},{10,2},{3,11},{11,3},{4,12},{12,4},... | collective-permute-start | bytes 786440 | tf_op jit(solution)/shard_map/ppermute | solution.py:21
  118.2 8.3 %copy-start.11 = (f32[8,64,128]{2,1,0:T(8,128)}, f32[8,64,128]{2,1,0:T(8,128)S(1)}, u32[]{:S(2)}) copy-start(f32[8,64,128]{2,1,0:T(8,128)S(1)} %collective-permute-done.15.refs_14_) | copy-start | bytes 786436
  118.2 8.2 %collective-permute-start.16 = (f32[8,64,128]{2,1,0:T(8,128)S(1)}, f32[8,64,128]{2,1,0:T(8,128)S(1)}, u32[]{:S(2)}, u32[]{:S(2)}) collective-permute-start(f32[8,64,128]{2,1,0:T(8,128)S(1)} %collective-permute-done.15.refs_14_), channel_id=1, source_target_pairs={{0,8},{8,0},{1,9},{9,1},{2,10},{10,2},{3,11},{11,3},{4,12},{12,4},... | collective-permute-start | bytes 786440 | tf_op jit(solution)/shard_map/ppermute | solution.py:21
  120.2 6.2 %copy-start.12 = (f32[8,64,128]{2,1,0:T(8,128)}, f32[8,64,128]{2,1,0:T(8,128)S(1)}, u32[]{:S(2)}) copy-start(f32[8,64,128]{2,1,0:T(8,128)S(1)} %collective-permute-done.13.refs_12_) | copy-start | bytes 786436
  120.2 6.1 %collective-permute-start.14 = (f32[8,64,128]{2,1,0:T(8,128)S(1)}, f32[8,64,128]{2,1,0:T(8,128)}, u32[]{:S(2)}, u32[]{:S(2)}) collective-permute-start(f32[8,64,128]{2,1,0:T(8,128)S(1)} %collective-permute-done.13.refs_12_), channel_id=1, source_target_pairs={{0,8},{8,0},{1,9},{9,1},{2,10},{10,2},{3,11},{11,3},{4,12},{12,4},... | collective-permute-start | bytes 786440 | tf_op jit(solution)/shard_map/ppermute | solution.py:21
  121.6 4.9 %copy-start.13 = (f32[8,64,128]{2,1,0:T(8,128)}, f32[8,64,128]{2,1,0:T(8,128)S(1)}, u32[]{:S(2)}) copy-start(f32[8,64,128]{2,1,0:T(8,128)S(1)} %collective-permute-done.11.refs_10_) | copy-start | bytes 786436
  121.6 4.8 %collective-permute-start.12 = (f32[8,64,128]{2,1,0:T(8,128)S(1)}, f32[8,64,128]{2,1,0:T(8,128)}, u32[]{:S(2)}, u32[]{:S(2)}) collective-permute-start(f32[8,64,128]{2,1,0:T(8,128)S(1)} %collective-permute-done.11.refs_10_), channel_id=1, source_target_pairs={{0,8},{8,0},{1,9},{9,1},{2,10},{10,2},{3,11},{11,3},{4,12},{12,4},... | collective-permute-start | bytes 786440 | tf_op jit(solution)/shard_map/ppermute | solution.py:21
  126.3 0.7 copy-start.14
  126.3 0.8 copy-start.15
  126.3 0.9 copy-start.16

commit v4 on v3

v4 whole, which is shorter than its diff:
```python
import functools

import jax
import jax.numpy as jnp
import numpy as np
from jax import lax
from jax.experimental import pallas as pl
from jax.experimental.pallas import tpu as pltpu
from jax.sharding import Mesh, PartitionSpec as P

STENCIL = (-205.0 / 72.0, 8.0 / 5.0, -1.0 / 5.0, 8.0 / 315.0, -1.0 / 560.0)
RATE = 0.2
COURANT = 0.11

AXES = ("yh", "x", "c", "yl", "z")
SIZES = {"yh": 2, "x": 4, "c": 2, "yl": 2, "z": 4}
SHOT = ("yh", "x", "c")
SLAB = ("yl", "z")


def rotate(value, axis, steps):
    count = SIZES[axis]
    return lax.ppermute(value, axis, [(i, (i + steps) % count) for i in range(count)])


def banded(length, centre):
    matrix = centre * np.eye(length)
    for reach in range(1, 5):
        matrix += STENCIL[reach] * (np.eye(length, k=reach) + np.eye(length, k=-reach))
    return jnp.asarray(matrix, jnp.float32)


def halo(last, first):
    before = lax.ppermute(last, SLAB, [(i, (i + 1) % 8) for i in range(8)])
    after = lax.ppermute(first, SLAB, [((i + 1) % 8, i) for i in range(8)])
    return before, after


def dot(a, b):
    return jnp.dot(a, b, precision=lax.Precision.HIGHEST, preferred_element_type=jnp.float32)


def inside(field, depth, width, out):
    planes = field.shape[0]
    out[...] = dot(field[...].reshape(planes * 64, 256), depth[...]).reshape(planes, 64, 256)
    for i in range(planes):
        total = dot(width[...], field[i])
        for reach in range(1, 5):
            near = [field[j] for j in (i - reach, i + reach) if 0 <= j < planes]
            total += STENCIL[reach] * sum(near[1:], near[0])
        out[i] += total


def beyond(before, after, i, planes):
    if i < 4:
        return sum(STENCIL[reach] * before[4 + i - reach] for reach in range(i + 1, 5))
    low = planes - i
    return sum(STENCIL[reach] * after[reach - low] for reach in range(low, 5))


def first_kernel(previous, current, depth, width, base, lap):
    inside(current, depth, width, lap)
    base[...] = 2.0 * current[...] - previous[...]


def second_kernel(back, base, lap, current, before, after, depth, width, most, squared, first, last, one):
    for plane in range(16):
        for block in range(8):
            for half in range(2):
                value = back[8 * plane + block, 8 * half : 8 * half + 8]
                at = (plane, slice(8 * block, 8 * block + 8), slice(128 * half, 128 * half + 128))
                squared[at] = (value * COURANT) ** 2
    for i in range(16):
        total = lap[i]
        if i < 4:
            total += jnp.where(lax.axis_index(SLAB) == 0, 0.0, beyond(before, after, i, 16))
        if i >= 12:
            total += jnp.where(lax.axis_index(SLAB) == 7, 0.0, beyond(before, after, i, 16))
        one[i] = base[i] + squared[i] * total
    first[...] = one[:4]
    last[...] = one[12:]
    inside(one, depth, width, most)
    for i in range(16):
        most[i] = 2.0 * one[i] - current[i] + squared[i] * most[i]


def last_kernel(most, squared, before, after, out):
    out[4:12] = most[4:12]
    for i in (0, 1, 2, 3):
        out[i] = most[i] + squared[i] * jnp.where(lax.axis_index(SLAB) == 0, 0.0, beyond(before, after, i, 16))
    for i in (12, 13, 14, 15):
        out[i] = most[i] + squared[i] * jnp.where(lax.axis_index(SLAB) == 7, 0.0, beyond(before, after, i, 16))


def on_slab(kernel, outs, *args, scratch=(), bytes_accessed=8 << 20):
    vmem = pl.BlockSpec(memory_space=pltpu.VMEM)
    return pl.pallas_call(
        kernel,
        out_shape=[jax.ShapeDtypeStruct((planes, 64, 256), jnp.float32) for planes in outs],
        in_specs=[vmem] * len(args),
        out_specs=[vmem] * len(outs),
        scratch_shapes=list(scratch),
        cost_estimate=pl.CostEstimate(flops=1 << 27, bytes_accessed=bytes_accessed, transcendentals=0),
        compiler_params=pltpu.CompilerParams(vmem_limit_bytes=20 << 20),
    )(*args)


def chip_index():
    return 4 * lax.axis_index("yh") + lax.axis_index("x")


def pack_kernel(offset, gradient, illumination, velocity, out, packed, tile, arrived, left):
    chip, c = chip_index(), lax.axis_index("c")
    half = pl.ds(pl.multiple_of(128 * lax.rem(chip, 2), 128), 128)
    parts = [pl.ds(32 * i, 32) for i in range(4)]
    reads = []
    for i, part in enumerate(parts):
        pairs = [(velocity.at[lax.div(chip, 2), part, :, half], tile.at[part])]
        for k, source in enumerate((gradient, illumination)):
            for h in range(2):
                to = packed.at[part, pl.ds(16 * k + 8 * h, 8)]
                pairs.append((source.at[part, :, pl.ds(128 * h, 128)], to))
        reads.append([pltpu.make_async_copy(a, b, arrived.at[5 * i + j]) for j, (a, b) in enumerate(pairs)])
        for copy in reads[-1]:
            copy.start()
    writes = []
    for i, part in enumerate(parts):
        for copy in reads[i]:
            copy.wait()
        upper = lax.broadcasted_iota(jnp.int32, (32, 8, 128), 1) // 4
        packed[part, 32:] = jnp.where(upper == c, tile[part], offset[0].astype(jnp.float32))
        writes.append(pltpu.make_async_copy(packed.at[part], out.at[part], left.at[i]))
        writes[-1].start()
    for copy in writes:
        copy.wait()


def pack(offsets, gradient, illumination, velocity):
    anywhere = pl.BlockSpec(memory_space=pl.ANY)
    return pl.pallas_call(
        pack_kernel,
        out_shape=jax.ShapeDtypeStruct((128, 40, 128), gradient.dtype),
        in_specs=[pl.BlockSpec(memory_space=pltpu.SMEM)] + [anywhere] * 3,
        out_specs=anywhere,
        scratch_shapes=[
            pltpu.VMEM((128, 40, 128), gradient.dtype),
            pltpu.VMEM((128, 8, 128), gradient.dtype),
            pltpu.SemaphoreType.DMA((20,)),
            pltpu.SemaphoreType.DMA((4,)),
        ],
        cost_estimate=pl.CostEstimate(flops=0, bytes_accessed=5 << 20, transcendentals=0),
        compiler_params=pltpu.CompilerParams(vmem_limit_bytes=60 << 20),
    )(
        offsets,
        gradient.reshape(128, 8, 256),
        illumination.reshape(128, 8, 256),
        velocity.reshape(4, 128, 8, 256),
    )


def model_kernel(sent, out, grad, illum, marks, arrived):
    copy = pltpu.make_async_copy(sent.at[:, 0, pl.ds(32, 8)], marks, arrived)
    copy.start()
    grad[...] = jnp.zeros_like(grad)
    illum[...] = jnp.zeros_like(illum)
    copy.wait()
    offs = [marks[shot, 4 - 4 * (shot % 2), 0].astype(jnp.int32) for shot in range(16)]
    for shot in range(16):
        grad[pl.ds(offs[shot], 8)] += sent[shot, :, :16]
        illum[pl.ds(offs[shot], 8)] += sent[shot, :, 16:32]
    for pair in range(8):
        slabs, rows = pl.ds(8 * (pair // 2), 8), pl.ds(8 * (pair % 2), 8)
        low = sent[2 * pair, :, 32:]
        high = sent[2 * pair + 1, :, 32:]
        velocity = jnp.where(lax.broadcasted_iota(jnp.int32, low.shape, 1) < 4, low, high)
        new = velocity - RATE * grad[slabs, rows] / (illum[slabs, rows] + 1.0)
        grad[slabs, rows] = new
        out[16 * pair : 16 * pair + 8, 16:] = new
        out[16 * pair + 8 : 16 * pair + 16, 16:] = new
    for shot in range(16):
        out[8 * shot : 8 * shot + 8, :16] = grad[pl.ds(offs[shot], 8)]


def update_model(sent):
    vmem = pl.BlockSpec(memory_space=pltpu.VMEM)
    return pl.pallas_call(
        model_kernel,
        out_shape=jax.ShapeDtypeStruct((128, 24, 128), sent.dtype),
        in_specs=[vmem],
        out_specs=vmem,
        scratch_shapes=[pltpu.VMEM((32, 16, 128), sent.dtype)] * 2
        + [pltpu.SMEM((16, 8, 128), sent.dtype), pltpu.SemaphoreType.DMA],
        cost_estimate=pl.CostEstimate(flops=1 << 20, bytes_accessed=4 << 20, transcendentals=0),
        compiler_params=pltpu.CompilerParams(vmem_limit_bytes=10 << 20),
    )(sent.reshape(16, 8, 40, 128))


def place_kernel(spots, *refs):
    pieces, out, sems = refs[: len(spots)], refs[-2], refs[-1]
    yh, x, c = (lax.axis_index(a) for a in SHOT)
    copies = []
    for i, (piece, (dy, dx, dc)) in enumerate(zip(pieces, spots)):
        chip = lax.rem(yh + dy, 2) * 4 + lax.rem(x + 4 - dx, 4)
        core = 0 if dc is None else lax.rem(c + dc, 2)
        planes = pl.ds(pl.multiple_of(8 * core, 8), piece.shape[0])
        lanes = pl.ds(pl.multiple_of(128 * lax.rem(chip, 2), 128), 128)
        target = out.at[lax.div(chip, 2), planes, :, lanes]
        copies.append(pltpu.make_async_copy(piece, target, sems.at[i]))
    for copy in copies:
        copy.start()
    for copy in copies:
        copy.wait()


def place_pieces(pieces, model=None):
    count = len(pieces)
    anywhere = pl.BlockSpec(memory_space=pl.ANY)
    hbm = pl.BlockSpec(memory_space=pltpu.HBM)
    rest = [] if model is None else [model]
    values = [piece[0] for piece in pieces]
    return pl.pallas_call(
        functools.partial(place_kernel, [piece[1:] for piece in pieces]),
        out_shape=jax.ShapeDtypeStruct((4, 16, 64, 256), values[0].dtype),
        in_specs=[anywhere] * count + [hbm] * len(rest),
        out_specs=hbm,
        input_output_aliases={count: 0} if rest else {},
        scratch_shapes=[pltpu.SemaphoreType.DMA((count,))],
        cost_estimate=pl.CostEstimate(flops=0, bytes_accessed=count << 19, transcendentals=0),
        compiler_params=pltpu.CompilerParams(vmem_limit_bytes=4 << 20),
    )(*values, *rest)


def gather_and_step(block, own, step, advance):
    def with_other_core(values):
        return [
            piece
            for value, dy, dx in values
            for piece in ((value, dy, dx, 0), (rotate(value, "c", 1), dy, dx, 1))
        ]

    one, two, three = (rotate(own, "x", k) for k in (1, 2, 3))
    flip = rotate(own, "yh", 1)
    most, squared, first, last = step
    around = halo(last, first)
    (one, two, three, flip), most = lax.optimization_barrier(((one, two, three, flip), most))
    second = [rotate(flip, "x", 1), rotate(flip, "x", 3), rotate(two, "yh", 1)]
    final = advance(most, squared, around)
    pieces = with_other_core([(one, 0, 1), (two, 0, 2), (three, 0, 3), (flip, 1, 0)])
    model = place_pieces([(block, 0, 0, None)] + pieces)
    second, model, final = lax.optimization_barrier((second, model, final))
    return place_pieces(with_other_core([(second[0], 1, 1), (second[1], 1, 3), (second[2], 1, 2)]), model), final


def on_device(gradient, illumination, u_prev, u_cur, velocity, offsets):
    u_prev, u_cur = u_prev[0], u_cur[0]
    c = lax.axis_index("c")

    sent = lax.all_to_all(pack(offsets, gradient, illumination, velocity), AXES, 0, 0)
    back = lax.all_to_all(update_model(sent), AXES, 0, 0)

    around = halo(u_cur[12:], u_cur[:4])
    depth, width = banded(256, 3.0 * STENCIL[0]), banded(64, 0.0)

    block = back[:, 16:]
    own = lax.dynamic_slice(block, (64 * c, 0, 0), (64, 8, 128)).reshape(8, 64, 128)
    field = pltpu.VMEM((16, 64, 256), jnp.float32)
    current, previous = u_cur, u_prev
    base, lap = on_slab(first_kernel, (16, 16), previous, current, depth, width)
    step = on_slab(
        second_kernel, (16, 16, 4, 4), back, base, lap, current, *around, depth, width, scratch=[field]
    )

    def advance(most, squared, around):
        return on_slab(last_kernel, (16,), most, squared, *around)[0]

    new_model, final = gather_and_step(block.reshape(16, 64, 128), own, tuple(step), advance)
    return new_model, final[None]


def solution(mesh):
    fine = Mesh(mesh.devices.reshape(tuple(SIZES[a] for a in AXES)), AXES)
    field = P(SHOT, SLAB, None, None)
    model = P(None, SLAB, None, None)
    return jax.shard_map(
        on_device,
        mesh=fine,
        in_specs=(field, field, field, field, model, P(SHOT)),
        out_specs=(model, field),
        check_vma=False,
    )
```

time: 134 us -> 122 us (0.910); the launches traced: 131 us -> 122 us
  Pallas kernels: 25.2 us -> 13.4 us
  waiting for transfers between devices: 21.5 us -> 30.9 us
  starting transfers between devices: 33.8 us -> 27.5 us
    pallas_call x3, Pallas kernels: 13.6 us -> 5.72 us  [on_slab(): pl.pallas_call(kernel, out_shape=[jax.ShapeDtypeStruct((planes, 64, 256),...]
    ppermute x15 -> x14, waiting for transfers between devices: 4.43 us -> 10.8 us  [rotate(): lax.ppermute(value, axis, [(i, (i + steps) % count) for i in range(count)])]
    ppermute x15 -> x14, starting transfers between devices: 21.5 us -> 15.2 us  [rotate(): lax.ppermute(value, axis, [(i, (i + steps) % count) for i in range(count)])]
    all_to_all x1, waiting for transfers between devices: 15.9 us -> 20.1 us  [on_device(): back = lax.all_to_all(update_model(sent), AXES, 0, 0)]
    pallas_call x2 -> x3, Pallas kernels: 8.28 us -> 5.63 us  [the longest x1 2.89 us: pack(): pl.pallas_call(pack_kernel, out_shape=jax.ShapeDtypeStruct((128, 40, 128)...]
  transfers between devices with their start and end apart: 20 -> 19, of which waited for: 4 -> 8; matrix products, arithmetic and copies ran while one was open for 1% -> 1% of each run, Pallas kernels for 10% -> 6%
where the time goes in v4:
time: 122 us
  blocking collectives  45.7 us (37%)
  waiting for transfers between devices  30.9 us (25%)
  starting transfers between devices  27.5 us (23%)
  Pallas kernels  13.4 us (11%)
  local copies, waits for them, and re-layouts  3.27 us (3%)
  between operations  1.4 us (1%)
    all_to_all x1, blocking collectives, on_device(): lax.all_to_all(pack(offsets, gradient, illumination, velocity), AXES, 0, 0)  45.7 us
    all_to_all x1, waiting for transfers between devices, on_device(): back = lax.all_to_all(update_model(sent), AXES, 0, 0)  20.1 us
    ppermute x14, starting transfers between devices, rotate(): lax.ppermute(value, axis, [(i, (i + steps) % count) for i in range(count)])  15.2 us
    ppermute x14, waiting for transfers between devices, rotate(): lax.ppermute(value, axis, [(i, (i + steps) % count) for i in range(count)])  10.8 us
    ppermute x2, starting transfers between devices, halo(): after = lax.ppermute(first, SLAB, [((i + 1) % 8, i) for i in range(8)])  5.98 us
    pallas_call x3, Pallas kernels, on_slab(): pl.pallas_call(kernel, out_shape=[jax.ShapeDtypeStruct((planes, 64, 256),...  5.72 us
    all_to_all x1, starting transfers between devices, on_device(): back = lax.all_to_all(update_model(sent), AXES, 0, 0)  5.56 us
    pallas_call x1, Pallas kernels, pack(): pl.pallas_call(pack_kernel, out_shape=jax.ShapeDtypeStruct((128, 40, 128)...  2.89 us
  transfers between devices with their start and end apart: 19, of which 8 were waited for; matrix products, arithmetic and copies ran while one was open for 1% of the time, Pallas kernels for 6%

profile of v4, /device:TPU:9, one launch (start us, length us, event | category | flops | bytes accessed | tf_op | source)
XLA Modules:
  0.0 122.1 jit_solution(7156925643033309206)
XLA Ops:
  1.3 2.9 %shard_map.95 = f32[128,40,128]{2,1,0:T(8,128)} custom-call(s32[1]{0:T(128)S(6)} %copy.12.offset, f32[128,8,256]{2,1,0:T(8,128)} %bitcast.19, f32[128,8,256]{2,1,0:T(8,128)} %bitcast.20, f32[4,128,8,256]{3,2,1,0:T(8,128)} %bitcast.18), custom_call_target="tpu_custom_call" | custom-call | bytes 5242880 | tf_op jit(solution)/shard_map/pallas_call | solution.py:140
  4.2 45.7 %all_to_all.10 = f32[128,40,128]{2,1,0:T(8,128)S(1)} all-to-all(f32[128,40,128]{2,1,0:T(8,128)} %shard_map.95), channel_id=1, replica_groups=mesh['yh'=2,'x'=4,'c'=2,'yl'=2,'z'=4] {'yh','x','c','yl','z'}, dimensions={0} | all-to-all | bytes 5242880 | tf_op jit(solution)/shard_map/all_to_all | solution.py:258
  49.9 2.0 %shard_map.96 = f32[128,24,128]{2,1,0:T(8,128)S(1)} custom-call(f32[16,8,40,128]{3,2,1,0:T(8,128)S(1)} %bitcast.13), custom_call_target="tpu_custom_call" | custom-call | flops 1048576 | bytes 4194304 | tf_op jit(solution)/shard_map/pallas_call | solution.py:186
  51.9 0.0 copy-start.1
  51.9 1.1 copy-done.1
  53.0 0.0 copy-start
  53.0 0.0 copy-start.3
  53.0 0.0 copy-start.4
  53.0 5.6 %all-to-all-start.1 = ((f32[128,24,128]{2,1,0:T(8,128)}), f32[128,24,128]{2,1,0:T(8,128)S(1)}, u32[]{:S(2)}, u32[]{:S(2)}) async-start(f32[128,24,128]{2,1,0:T(8,128)} %copy-done.1), calls=%async_computation.1 | async-start | bytes 3145728 | tf_op jit(solution)/shard_map/all_to_all | solution.py:259
  58.6 0.0 copy-done
  58.6 0.8 slice_bitcast_fusion
  59.4 3.1 %collective-permute-start.5 = (f32[4,64,256]{2,1,0:T(8,128)}, f32[4,64,256]{2,1,0:T(8,128)S(1)}, u32[]{:S(2)}, u32[]{:S(2)}) collective-permute-start(f32[4,64,256]{2,1,0:T(8,128)} %get-tuple-element.34), channel_id=1, source_target_pairs={{1,0},{2,1},{3,2},{4,3},{5,4},{6,5},{7,6},{0,7},{9,8},{10,9},{11,1... | collective-permute-start | bytes 786440 | tf_op jit(solution)/shard_map/ppermute | solution.py:35
  62.6 0.0 collective-permute-start.4
  62.6 20.1 %all-to-all-done.1.back = f32[128,24,128]{2,1,0:T(8,128)S(1)} async-done(((f32[128,24,128]{2,1,0:T(8,128)}), f32[128,24,128]{2,1,0:T(8,128)S(1)}, u32[]{:S(2)}, u32[]{:S(2)}) %all-to-all-start.1) | async-done | bytes 1572896 | tf_op jit(solution)/shard_map/all_to_all | solution.py:259
  82.8 0.8 collective-permute-start.3
  83.6 1.3 %collective-permute-start.2 = (f32[8,64,128]{2,1,0:T(8,128)S(1)}, f32[8,64,128]{2,1,0:T(8,128)S(1)}, u32[]{:S(2)}, u32[]{:S(2)}) collective-permute-start(f32[8,64,128]{2,1,0:T(8,128)S(1)} %bitcast.23), channel_id=1, source_target_pairs={{0,48},{16,0},{32,16},{48,32},{1,49},{17,1},{33,17},{49,33},{2,50}... | collective-permute-start | bytes 786440 | tf_op jit(solution)/shard_map/ppermute | solution.py:23
  84.8 0.9 collective-permute-start.1
  85.7 0.0 collective-permute-done.5.after
  85.7 0.0 collective-permute-start
  85.7 0.0 copy-done.3
  85.7 0.0 copy-done.4
  85.7 0.0 copy-start.2
  85.7 1.2 copy-done.2
  86.9 2.2 %shard_map.97 = (f32[16,64,256]{2,1,0:T(8,128)S(1)}, f32[16,64,256]{2,1,0:T(8,128)S(1)}) custom-call(f32[16,64,256]{2,1,0:T(8,128)S(1)} %bitcast.17, f32[16,64,256]{2,1,0:T(8,128)S(1)} %bitcast.14, f32[256,256]{1,0:T(8,128)S(1)} %copy-done.3, f32[64,64]{1,0:T(8,128)S(1)} %copy-done.4), custom_call_target="tpu_custom_call" | custom-call | flops 134217728 | bytes 8388608 | tf_op jit(solution)/shard_map/pallas_call | solution.py:97
  89.2 0.0 collective-permute-done.4.before
  89.2 2.4 %shard_map.98 = (f32[16,64,256]{2,1,0:T(8,128)S(1)}, f32[16,64,256]{2,1,0:T(8,128)S(1)}, f32[4,64,256]{2,1,0:T(8,128)S(1)}, f32[4,64,256]{2,1,0:T(8,128)S(1)}) custom-call(f32[128,24,128]{2,1,0:T(8,128)S(1)} %all-to-all-done.1.back, f32[16,64,256]{2,1,0:T(8,128)S(1)} %get-tuple-element.18.base, f32[16,64,256]{2,1,0:T(8,128)S(1)} %get-tuple-element.19.lap, ...), custom_call_target="tpu_custom_call" | custom-call | flops 134217728 | bytes 8388608 | tf_op jit(solution)/shard_map/pallas_call | solution.py:97
  91.6 0.8 collective-permute-start.13
  92.4 0.0 collective-permute-done.3.refs_7_
  92.4 2.8 %collective-permute-start.14 = (f32[4,64,256]{2,1,0:T(8,128)S(1)}, f32[4,64,256]{2,1,0:T(8,128)S(1)}, u32[]{:S(2)}, u32[]{:S(2)}) collective-permute-start(f32[4,64,256]{2,1,0:T(8,128)S(1)} %get-tuple-element.28), channel_id=1, source_target_pairs={{1,0},{2,1},{3,2},{4,3},{5,4},{6,5},{7,6},{0,7},{9,8},{10,9},{11,1... | collective-permute-start | bytes 786440 | tf_op jit(solution)/shard_map/ppermute | solution.py:35
  95.2 0.0 collective-permute-done.2.refs_5_
  95.2 0.0 collective-permute-done.1.refs_3_
  95.2 3.9 %collective-permute-done.refs_1_ = f32[8,64,128]{2,1,0:T(8,128)S(1)} collective-permute-done((f32[8,64,128]{2,1,0:T(8,128)S(1)}, f32[8,64,128]{2,1,0:T(8,128)S(1)}, u32[]{:S(2)}, u32[]{:S(2)}) %collective-permute-start) | collective-permute-done | bytes 262176 | tf_op jit(solution)/shard_map/ppermute | solution.py:23
  99.1 1.6 %collective-permute-start.9 = (f32[8,64,128]{2,1,0:T(8,128)S(1)}, f32[8,64,128]{2,1,0:T(8,128)S(1)}, u32[]{:S(2)}, u32[]{:S(2)}) collective-permute-start(f32[8,64,128]{2,1,0:T(8,128)S(1)} %collective-permute-done.refs_1_), channel_id=1, source_target_pairs={{0,8},{8,0},{1,9},{9,1},{2,10},{10,2},{3,11},{11,3},{4,12},{12,4},... | collective-permute-start | bytes 786440 | tf_op jit(solution)/shard_map/ppermute | solution.py:23
  100.7 0.0 collective-permute-start.11
  100.7 0.5 collective-permute-start.10
  101.2 0.0 collective-permute-done.13.before
  101.2 2.7 %collective-permute-start.12 = (f32[8,64,128]{2,1,0:T(8,128)S(1)}, f32[8,64,128]{2,1,0:T(8,128)S(1)}, u32[]{:S(2)}, u32[]{:S(2)}) collective-permute-start(f32[8,64,128]{2,1,0:T(8,128)S(1)} %collective-permute-done.3.refs_7_), channel_id=1, source_target_pairs={{0,8},{8,0},{1,9},{9,1},{2,10},{10,2},{3,11},{11,3},{4,12},{12,4},... | collective-permute-start | bytes 786440 | tf_op jit(solution)/shard_map/ppermute | solution.py:23
  103.9 0.0 collective-permute-done.14.after
  103.9 3.1 %collective-permute-start.8 = (f32[8,64,128]{2,1,0:T(8,128)S(1)}, f32[8,64,128]{2,1,0:T(8,128)S(1)}, u32[]{:S(2)}, u32[]{:S(2)}) collective-permute-start(f32[8,64,128]{2,1,0:T(8,128)S(1)} %collective-permute-done.1.refs_3_), channel_id=1, source_target_pairs={{0,64},{64,0},{1,65},{65,1},{2,66},{66,2},{3,67},{67,3},{4,68},{68... | collective-permute-start | bytes 786440 | tf_op jit(solution)/shard_map/ppermute | solution.py:23
  107.0 0.0 collective-permute-done.9.refs_2_
  107.0 2.1 %collective-permute-start.7 = (f32[8,64,128]{2,1,0:T(8,128)S(1)}, f32[8,64,128]{2,1,0:T(8,128)S(1)}, u32[]{:S(2)}, u32[]{:S(2)}) collective-permute-start(f32[8,64,128]{2,1,0:T(8,128)S(1)} %collective-permute-done.3.refs_7_), channel_id=1, source_target_pairs={{0,48},{16,0},{32,16},{48,32},{1,49},{17,1},{33,17},{49,33},{2,50}... | collective-permute-start | bytes 786440 | tf_op jit(solution)/shard_map/ppermute | solution.py:23
  109.1 0.0 collective-permute-done.11.refs_6_
  109.1 0.3 collective-permute-start.6
  109.4 1.1 shard_map.100
  110.6 0.0 collective-permute-done.10.refs_4_
  110.6 0.0 collective-permute-done.12.refs_8_
  110.6 1.6 %shard_map.99.refs_6_ = f32[4,16,64,256]{3,2,1,0:T(8,128)} custom-call(f32[16,64,128]{2,1,0:T(8,128)S(1)} %bitcast.16, f32[8,64,128]{2,1,0:T(8,128)S(1)} %collective-permute-done.refs_1_, f32[8,64,128]{2,1,0:T(8,128)S(1)} %collective-permute-done.9.refs_2_, f32[8,64,128]{2,1,0:T(8,128)S(1)} %collective-permute-done.1.refs_3_, ...), custom_call_target="tpu_custom_call" | custom-call | bytes 4718592 | tf_op jit(solution)/shard_map/pallas_call | solution.py:221
  112.1 1.5 %collective-permute-done.8.refs_4_ = f32[8,64,128]{2,1,0:T(8,128)S(1)} collective-permute-done((f32[8,64,128]{2,1,0:T(8,128)S(1)}, f32[8,64,128]{2,1,0:T(8,128)S(1)}, u32[]{:S(2)}, u32[]{:S(2)}) %collective-permute-start.8) | collective-permute-done | bytes 262176 | tf_op jit(solution)/shard_map/ppermute | solution.py:23
  113.6 2.2 %collective-permute-done.7.refs_2_ = f32[8,64,128]{2,1,0:T(8,128)S(1)} collective-permute-done((f32[8,64,128]{2,1,0:T(8,128)S(1)}, f32[8,64,128]{2,1,0:T(8,128)S(1)}, u32[]{:S(2)}, u32[]{:S(2)}) %collective-permute-start.7) | collective-permute-done | bytes 262176 | tf_op jit(solution)/shard_map/ppermute | solution.py:23
  115.8 1.8 %collective-permute-done.6.refs_0_ = f32[8,64,128]{2,1,0:T(8,128)S(1)} collective-permute-done((f32[8,64,128]{2,1,0:T(8,128)S(1)}, f32[8,64,128]{2,1,0:T(8,128)S(1)}, u32[]{:S(2)}, u32[]{:S(2)}) %collective-permute-start.6) | collective-permute-done | bytes 262176 | tf_op jit(solution)/shard_map/ppermute | solution.py:23
  117.6 1.4 %collective-permute-start.15 = (f32[8,64,128]{2,1,0:T(8,128)S(1)}, f32[8,64,128]{2,1,0:T(8,128)S(1)}, u32[]{:S(2)}, u32[]{:S(2)}) collective-permute-start(f32[8,64,128]{2,1,0:T(8,128)S(1)} %collective-permute-done.6.refs_0_), channel_id=1, source_target_pairs={{0,8},{8,0},{1,9},{9,1},{2,10},{10,2},{3,11},{11,3},{4,12},{12,4},... | collective-permute-start | bytes 786440 | tf_op jit(solution)/shard_map/ppermute | solution.py:23
  119.0 0.0 collective-permute-start.16
  119.0 0.5 collective-permute-start.17
  119.6 0.7 collective-permute-done.15.refs_1_
  120.2 0.4 collective-permute-done.16.refs_3_
  120.6 0.4 collective-permute-done.17.refs_5_
  121.0 1.2 shard_map.101
  (2 shorter events, 0.1 us)
Async XLA Ops:
  51.9 1.1 copy-start.1
  53.0 5.6 %copy-start = (f32[1,16,64,256]{3,2,1,0:T(8,128)S(1)}, f32[1,16,64,256]{3,2,1,0:T(8,128)}, u32[]{:S(2)}) copy-start(f32[1,16,64,256]{3,2,1,0:T(8,128)} %param.11) | copy-start | bytes 3145732
  53.0 32.7 %copy-start.3 = (f32[256,256]{1,0:T(8,128)S(1)}, f32[256,256]{1,0:T(8,128)}, u32[]{:S(2)}) copy-start(f32[256,256]{1,0:T(8,128)} %constant.16.clone.depth) | copy-start | bytes 786436
  53.0 32.7 %copy-start.4 = (f32[64,64]{1,0:T(8,128)S(1)}, f32[64,64]{1,0:T(8,128)}, u32[]{:S(2)}) copy-start(f32[64,64]{1,0:T(8,128)} %constant.17.clone.width) | copy-start | bytes 49156
  53.0 29.7 %all-to-all-start.1 = ((f32[128,24,128]{2,1,0:T(8,128)}), f32[128,24,128]{2,1,0:T(8,128)S(1)}, u32[]{:S(2)}, u32[]{:S(2)}) async-start(f32[128,24,128]{2,1,0:T(8,128)} %copy-done.1), calls=%async_computation.1 | async-start | bytes 3145728 | tf_op jit(solution)/shard_map/all_to_all | solution.py:259
  59.4 26.3 %collective-permute-start.5 = (f32[4,64,256]{2,1,0:T(8,128)}, f32[4,64,256]{2,1,0:T(8,128)S(1)}, u32[]{:S(2)}, u32[]{:S(2)}) collective-permute-start(f32[4,64,256]{2,1,0:T(8,128)} %get-tuple-element.34), channel_id=1, source_target_pairs={{1,0},{2,1},{3,2},{4,3},{5,4},{6,5},{7,6},{0,7},{9,8},{10,9},{11,1... | collective-permute-start | bytes 786440 | tf_op jit(solution)/shard_map/ppermute | solution.py:35
  62.6 26.6 %collective-permute-start.4 = (f32[4,64,256]{2,1,0:T(8,128)}, f32[4,64,256]{2,1,0:T(8,128)S(1)}, u32[]{:S(2)}, u32[]{:S(2)}) collective-permute-start(f32[4,64,256]{2,1,0:T(8,128)} %get-tuple-element.35), channel_id=1, source_target_pairs={{0,1},{1,2},{2,3},{3,4},{4,5},{5,6},{6,7},{7,0},{8,9},{9,10},{10,1... | collective-permute-start | bytes 786440 | tf_op jit(solution)/shard_map/ppermute | solution.py:34
  82.8 9.6 %collective-permute-start.3 = (f32[8,64,128]{2,1,0:T(8,128)S(1)}, f32[8,64,128]{2,1,0:T(8,128)S(1)}, u32[]{:S(2)}, u32[]{:S(2)}) collective-permute-start(f32[8,64,128]{2,1,0:T(8,128)S(1)} %bitcast.22), channel_id=1, source_target_pairs={{0,64},{64,0},{1,65},{65,1},{2,66},{66,2},{3,67},{67,3},{4,68},{68... | collective-permute-start | bytes 786440 | tf_op jit(solution)/shard_map/ppermute | solution.py:23
  83.6 11.6 %collective-permute-start.2 = (f32[8,64,128]{2,1,0:T(8,128)S(1)}, f32[8,64,128]{2,1,0:T(8,128)S(1)}, u32[]{:S(2)}, u32[]{:S(2)}) collective-permute-start(f32[8,64,128]{2,1,0:T(8,128)S(1)} %bitcast.23), channel_id=1, source_target_pairs={{0,48},{16,0},{32,16},{48,32},{1,49},{17,1},{33,17},{49,33},{2,50}... | collective-permute-start | bytes 786440 | tf_op jit(solution)/shard_map/ppermute | solution.py:23
  84.8 10.4 %collective-permute-start.1 = (f32[8,64,128]{2,1,0:T(8,128)S(1)}, f32[8,64,128]{2,1,0:T(8,128)S(1)}, u32[]{:S(2)}, u32[]{:S(2)}) collective-permute-start(f32[8,64,128]{2,1,0:T(8,128)S(1)} %bitcast.24), channel_id=1, source_target_pairs={{0,32},{16,48},{32,0},{48,16},{1,33},{17,49},{33,1},{49,17},{2,34}... | collective-permute-start | bytes 786440 | tf_op jit(solution)/shard_map/ppermute | solution.py:23
  85.7 13.4 %collective-permute-start = (f32[8,64,128]{2,1,0:T(8,128)S(1)}, f32[8,64,128]{2,1,0:T(8,128)S(1)}, u32[]{:S(2)}, u32[]{:S(2)}) collective-permute-start(f32[8,64,128]{2,1,0:T(8,128)S(1)} %bitcast.25), channel_id=1, source_target_pairs={{0,16},{16,32},{32,48},{48,0},{1,17},{17,33},{33,49},{49,1},{2,18}... | collective-permute-start | bytes 786440 | tf_op jit(solution)/shard_map/ppermute | solution.py:23
  85.7 1.2 %copy-start.2 = (f32[1,16,64,256]{3,2,1,0:T(8,128)S(1)}, f32[1,16,64,256]{3,2,1,0:T(8,128)}, u32[]{:S(2)}) copy-start(f32[1,16,64,256]{3,2,1,0:T(8,128)} %param.10) | copy-start | bytes 3145732
  91.6 9.6 %collective-permute-start.13 = (f32[4,64,256]{2,1,0:T(8,128)S(1)}, f32[4,64,256]{2,1,0:T(8,128)S(1)}, u32[]{:S(2)}, u32[]{:S(2)}) collective-permute-start(f32[4,64,256]{2,1,0:T(8,128)S(1)} %get-tuple-element.27), channel_id=1, source_target_pairs={{0,1},{1,2},{2,3},{3,4},{4,5},{5,6},{6,7},{7,0},{8,9},{9,10},{10,1... | collective-permute-start | bytes 786440 | tf_op jit(solution)/shard_map/ppermute | solution.py:34
  92.4 11.6 %collective-permute-start.14 = (f32[4,64,256]{2,1,0:T(8,128)S(1)}, f32[4,64,256]{2,1,0:T(8,128)S(1)}, u32[]{:S(2)}, u32[]{:S(2)}) collective-permute-start(f32[4,64,256]{2,1,0:T(8,128)S(1)} %get-tuple-element.28), channel_id=1, source_target_pairs={{1,0},{2,1},{3,2},{4,3},{5,4},{6,5},{7,6},{0,7},{9,8},{10,9},{11,1... | collective-permute-start | bytes 786440 | tf_op jit(solution)/shard_map/ppermute | solution.py:35
  99.1 7.9 %collective-permute-start.9 = (f32[8,64,128]{2,1,0:T(8,128)S(1)}, f32[8,64,128]{2,1,0:T(8,128)S(1)}, u32[]{:S(2)}, u32[]{:S(2)}) collective-permute-start(f32[8,64,128]{2,1,0:T(8,128)S(1)} %collective-permute-done.refs_1_), channel_id=1, source_target_pairs={{0,8},{8,0},{1,9},{9,1},{2,10},{10,2},{3,11},{11,3},{4,12},{12,4},... | collective-permute-start | bytes 786440 | tf_op jit(solution)/shard_map/ppermute | solution.py:23
  100.7 8.4 %collective-permute-start.11 = (f32[8,64,128]{2,1,0:T(8,128)S(1)}, f32[8,64,128]{2,1,0:T(8,128)S(1)}, u32[]{:S(2)}, u32[]{:S(2)}) collective-permute-start(f32[8,64,128]{2,1,0:T(8,128)S(1)} %collective-permute-done.2.refs_5_), channel_id=1, source_target_pairs={{0,8},{8,0},{1,9},{9,1},{2,10},{10,2},{3,11},{11,3},{4,12},{12,4},... | collective-permute-start | bytes 786440 | tf_op jit(solution)/shard_map/ppermute | solution.py:23
  100.7 9.9 %collective-permute-start.10 = (f32[8,64,128]{2,1,0:T(8,128)S(1)}, f32[8,64,128]{2,1,0:T(8,128)S(1)}, u32[]{:S(2)}, u32[]{:S(2)}) collective-permute-start(f32[8,64,128]{2,1,0:T(8,128)S(1)} %collective-permute-done.1.refs_3_), channel_id=1, source_target_pairs={{0,8},{8,0},{1,9},{9,1},{2,10},{10,2},{3,11},{11,3},{4,12},{12,4},... | collective-permute-start | bytes 786440 | tf_op jit(solution)/shard_map/ppermute | solution.py:23
  101.2 9.4 %collective-permute-start.12 = (f32[8,64,128]{2,1,0:T(8,128)S(1)}, f32[8,64,128]{2,1,0:T(8,128)S(1)}, u32[]{:S(2)}, u32[]{:S(2)}) collective-permute-start(f32[8,64,128]{2,1,0:T(8,128)S(1)} %collective-permute-done.3.refs_7_), channel_id=1, source_target_pairs={{0,8},{8,0},{1,9},{9,1},{2,10},{10,2},{3,11},{11,3},{4,12},{12,4},... | collective-permute-start | bytes 786440 | tf_op jit(solution)/shard_map/ppermute | solution.py:23
  103.9 9.7 %collective-permute-start.8 = (f32[8,64,128]{2,1,0:T(8,128)S(1)}, f32[8,64,128]{2,1,0:T(8,128)S(1)}, u32[]{:S(2)}, u32[]{:S(2)}) collective-permute-start(f32[8,64,128]{2,1,0:T(8,128)S(1)} %collective-permute-done.1.refs_3_), channel_id=1, source_target_pairs={{0,64},{64,0},{1,65},{65,1},{2,66},{66,2},{3,67},{67,3},{4,68},{68... | collective-permute-start | bytes 786440 | tf_op jit(solution)/shard_map/ppermute | solution.py:23
  107.0 8.8 %collective-permute-start.7 = (f32[8,64,128]{2,1,0:T(8,128)S(1)}, f32[8,64,128]{2,1,0:T(8,128)S(1)}, u32[]{:S(2)}, u32[]{:S(2)}) collective-permute-start(f32[8,64,128]{2,1,0:T(8,128)S(1)} %collective-permute-done.3.refs_7_), channel_id=1, source_target_pairs={{0,48},{16,0},{32,16},{48,32},{1,49},{17,1},{33,17},{49,33},{2,50}... | collective-permute-start | bytes 786440 | tf_op jit(solution)/shard_map/ppermute | solution.py:23
  109.1 8.5 %collective-permute-start.6 = (f32[8,64,128]{2,1,0:T(8,128)S(1)}, f32[8,64,128]{2,1,0:T(8,128)S(1)}, u32[]{:S(2)}, u32[]{:S(2)}) collective-permute-start(f32[8,64,128]{2,1,0:T(8,128)S(1)} %collective-permute-done.3.refs_7_), channel_id=1, source_target_pairs={{0,16},{16,32},{32,48},{48,0},{1,17},{17,33},{33,49},{49,1},{2,18}... | collective-permute-start | bytes 786440 | tf_op jit(solution)/shard_map/ppermute | solution.py:23
  117.6 2.6 %collective-permute-start.15 = (f32[8,64,128]{2,1,0:T(8,128)S(1)}, f32[8,64,128]{2,1,0:T(8,128)S(1)}, u32[]{:S(2)}, u32[]{:S(2)}) collective-permute-start(f32[8,64,128]{2,1,0:T(8,128)S(1)} %collective-permute-done.6.refs_0_), channel_id=1, source_target_pairs={{0,8},{8,0},{1,9},{9,1},{2,10},{10,2},{3,11},{11,3},{4,12},{12,4},... | collective-permute-start | bytes 786440 | tf_op jit(solution)/shard_map/ppermute | solution.py:23
  119.0 1.5 %collective-permute-start.16 = (f32[8,64,128]{2,1,0:T(8,128)S(1)}, f32[8,64,128]{2,1,0:T(8,128)S(1)}, u32[]{:S(2)}, u32[]{:S(2)}) collective-permute-start(f32[8,64,128]{2,1,0:T(8,128)S(1)} %collective-permute-done.7.refs_2_), channel_id=1, source_target_pairs={{0,8},{8,0},{1,9},{9,1},{2,10},{10,2},{3,11},{11,3},{4,12},{12,4},... | collective-permute-start | bytes 786440 | tf_op jit(solution)/shard_map/ppermute | solution.py:23
  119.0 1.9 %collective-permute-start.17 = (f32[8,64,128]{2,1,0:T(8,128)S(1)}, f32[8,64,128]{2,1,0:T(8,128)S(1)}, u32[]{:S(2)}, u32[]{:S(2)}) collective-permute-start(f32[8,64,128]{2,1,0:T(8,128)S(1)} %collective-permute-done.8.refs_4_), channel_id=1, source_target_pairs={{0,8},{8,0},{1,9},{9,1},{2,10},{10,2},{3,11},{11,3},{4,12},{12,4},... | collective-permute-start | bytes 786440 | tf_op jit(solution)/shard_map/ppermute | solution.py:23

commit v5 on v4

--- a/solution.py
+++ b/solution.py
@@ -84,15 +84,7 @@
         most[i] = 2.0 * one[i] - current[i] + squared[i] * most[i]
 
 
-def last_kernel(most, squared, before, after, out):
-    out[4:12] = most[4:12]
-    for i in (0, 1, 2, 3):
-        out[i] = most[i] + squared[i] * jnp.where(lax.axis_index(SLAB) == 0, 0.0, beyond(before, after, i, 16))
-    for i in (12, 13, 14, 15):
-        out[i] = most[i] + squared[i] * jnp.where(lax.axis_index(SLAB) == 7, 0.0, beyond(before, after, i, 16))
-
-
-def on_slab(kernel, outs, *args, scratch=(), bytes_accessed=8 << 20):
+def on_slab(kernel, outs, *args, scratch=()):
     vmem = pl.BlockSpec(memory_space=pltpu.VMEM)
     return pl.pallas_call(
         kernel,
@@ -100,7 +92,7 @@
         in_specs=[vmem] * len(args),
         out_specs=[vmem] * len(outs),
         scratch_shapes=list(scratch),
-        cost_estimate=pl.CostEstimate(flops=1 << 27, bytes_accessed=bytes_accessed, transcendentals=0),
+        cost_estimate=pl.CostEstimate(flops=0, bytes_accessed=1 << 10, transcendentals=0),
         compiler_params=pltpu.CompilerParams(vmem_limit_bytes=20 << 20),
     )(*args)
 
@@ -195,42 +187,54 @@
     )(sent.reshape(16, 8, 40, 128))
 
 
-def place_kernel(spots, *refs):
-    pieces, out, sems = refs[: len(spots)], refs[-2], refs[-1]
+def last_kernel(spots, *refs):
+    count = len(spots)
+    pieces, (most, squared, before, after, model, out, ends, sems) = refs[:count], refs[count:]
     yh, x, c = (lax.axis_index(a) for a in SHOT)
-    copies = []
+    middle = pl.ds(4, 8)
+    copies = [pltpu.make_async_copy(most.at[middle], out.at[middle], sems.at[count])]
     for i, (piece, (dy, dx, dc)) in enumerate(zip(pieces, spots)):
         chip = lax.rem(yh + dy, 2) * 4 + lax.rem(x + 4 - dx, 4)
         core = 0 if dc is None else lax.rem(c + dc, 2)
         planes = pl.ds(pl.multiple_of(8 * core, 8), piece.shape[0])
         lanes = pl.ds(pl.multiple_of(128 * lax.rem(chip, 2), 128), 128)
-        target = out.at[lax.div(chip, 2), planes, :, lanes]
+        target = model.at[lax.div(chip, 2), planes, :, lanes]
         copies.append(pltpu.make_async_copy(piece, target, sems.at[i]))
     for copy in copies:
         copy.start()
+    slab = lax.axis_index(SLAB)
+    for i in range(4):
+        ends[i] = most[i] + squared[i] * jnp.where(slab == 0, 0.0, beyond(before, after, i, 16))
+        j = 12 + i
+        ends[4 + i] = most[j] + squared[j] * jnp.where(slab == 7, 0.0, beyond(before, after, j, 16))
+    for i in range(2):
+        edge = pltpu.make_async_copy(ends.at[pl.ds(4 * i, 4)], out.at[pl.ds(12 * i, 4)], sems.at[count + 1 + i])
+        edge.start()
+        copies.append(edge)
     for copy in copies:
         copy.wait()
 
 
-def place_pieces(pieces, model=None):
+def finish(pieces, most, squared, before, after):
     count = len(pieces)
     anywhere = pl.BlockSpec(memory_space=pl.ANY)
+    vmem = pl.BlockSpec(memory_space=pltpu.VMEM)
     hbm = pl.BlockSpec(memory_space=pltpu.HBM)
-    rest = [] if model is None else [model]
-    values = [piece[0] for piece in pieces]
-    return pl.pallas_call(
-        functools.partial(place_kernel, [piece[1:] for piece in pieces]),
-        out_shape=jax.ShapeDtypeStruct((4, 16, 64, 256), values[0].dtype),
-        in_specs=[anywhere] * count + [hbm] * len(rest),
-        out_specs=hbm,
-        input_output_aliases={count: 0} if rest else {},
-        scratch_shapes=[pltpu.SemaphoreType.DMA((count,))],
-        cost_estimate=pl.CostEstimate(flops=0, bytes_accessed=count << 19, transcendentals=0),
-        compiler_params=pltpu.CompilerParams(vmem_limit_bytes=4 << 20),
-    )(*values, *rest)
-
-
-def gather_and_step(block, own, step, advance):
+    return pl.pallas_call(
+        functools.partial(last_kernel, [piece[1:] for piece in pieces]),
+        out_shape=[
+            jax.ShapeDtypeStruct((4, 16, 64, 256), most.dtype),
+            jax.ShapeDtypeStruct((16, 64, 256), most.dtype),
+        ],
+        in_specs=[anywhere] * count + [vmem] * 4,
+        out_specs=[hbm] * 2,
+        scratch_shapes=[pltpu.VMEM((8, 64, 256), most.dtype), pltpu.SemaphoreType.DMA((count + 3,))],
+        cost_estimate=pl.CostEstimate(flops=0, bytes_accessed=10 << 20, transcendentals=0),
+        compiler_params=pltpu.CompilerParams(vmem_limit_bytes=8 << 20),
+    )(*[piece[0] for piece in pieces], most, squared, before, after)
+
+
+def gather_and_step(block, own, step):
     def with_other_core(values):
         return [
             piece
@@ -244,11 +248,11 @@
     around = halo(last, first)
     (one, two, three, flip), most = lax.optimization_barrier(((one, two, three, flip), most))
     second = [rotate(flip, "x", 1), rotate(flip, "x", 3), rotate(two, "yh", 1)]
-    final = advance(most, squared, around)
-    pieces = with_other_core([(one, 0, 1), (two, 0, 2), (three, 0, 3), (flip, 1, 0)])
-    model = place_pieces([(block, 0, 0, None)] + pieces)
-    second, model, final = lax.optimization_barrier((second, model, final))
-    return place_pieces(with_other_core([(second[0], 1, 1), (second[1], 1, 3), (second[2], 1, 2)]), model), final
+    (one, two, three, flip), around = lax.optimization_barrier(((one, two, three, flip), around))
+    pieces = [(block, 0, 0, None)]
+    pieces += with_other_core([(one, 0, 1), (two, 0, 2), (three, 0, 3), (flip, 1, 0)])
+    pieces += with_other_core([(second[0], 1, 1), (second[1], 1, 3), (second[2], 1, 2)])
+    return finish(pieces, most, squared, *around)
 
 
 def on_device(gradient, illumination, u_prev, u_cur, velocity, offsets):
@@ -270,10 +274,7 @@
         second_kernel, (16, 16, 4, 4), back, base, lap, current, *around, depth, width, scratch=[field]
     )
 
-    def advance(most, squared, around):
-        return on_slab(last_kernel, (16,), most, squared, *around)[0]
-
-    new_model, final = gather_and_step(block.reshape(16, 64, 128), own, tuple(step), advance)
+    new_model, final = gather_and_step(block.reshape(16, 64, 128), own, tuple(step))
     return new_model, final[None]
 
 

time: 122 us -> 118 us (0.967)
  starting transfers between devices: 27.5 us -> 25.5 us
  Pallas kernels: 13.4 us -> 11.9 us
    ppermute x14, starting transfers between devices: 15.2 us -> 13.2 us  [rotate(): lax.ppermute(value, axis, [(i, (i + steps) % count) for i in range(count)])]
    pallas_call x3 -> x2, Pallas kernels: 5.72 us -> 4.59 us  [on_slab(): pl.pallas_call(kernel, out_shape=[jax.ShapeDtypeStruct((planes, 64, 256),...]
    pallas_call x2 -> x1, Pallas kernels: 2.74 us -> 2.48 us  [finish(): pl.pallas_call(functools.partial(last_kernel, [piece[1:] for piece in pie...]
  transfers between devices with their start and end apart: 19 -> 19, of which waited for: 8 -> 8; matrix products, arithmetic and copies ran while one was open for 1% -> 1% of each run, Pallas kernels for 6% -> 4%
where the time goes in v5:
time: 118 us
  blocking collectives  45.7 us (39%)
  waiting for transfers between devices  30.2 us (26%)
  starting transfers between devices  25.5 us (22%)
  Pallas kernels  11.9 us (10%)
  local copies, waits for them, and re-layouts  3.28 us (3%)
  between operations  1.4 us (1%)
    all_to_all x1, blocking collectives, on_device(): lax.all_to_all(pack(offsets, gradient, illumination, velocity), AXES, 0, 0)  45.7 us
    all_to_all x1, waiting for transfers between devices, on_device(): back = lax.all_to_all(update_model(sent), AXES, 0, 0)  20.1 us
    ppermute x14, starting transfers between devices, rotate(): lax.ppermute(value, axis, [(i, (i + steps) % count) for i in range(count)])  13.2 us
    ppermute x14, waiting for transfers between devices, rotate(): lax.ppermute(value, axis, [(i, (i + steps) % count) for i in range(count)])  10.1 us
    ppermute x2, starting transfers between devices, halo(): after = lax.ppermute(first, SLAB, [((i + 1) % 8, i) for i in range(8)])  5.98 us
    all_to_all x1, starting transfers between devices, on_device(): back = lax.all_to_all(update_model(sent), AXES, 0, 0)  5.56 us
    pallas_call x2, Pallas kernels, on_slab(): pl.pallas_call(kernel, out_shape=[jax.ShapeDtypeStruct((planes, 64, 256),...  4.59 us
    pallas_call x1, Pallas kernels, pack(): pl.pallas_call(pack_kernel, out_shape=jax.ShapeDtypeStruct((128, 40, 128)...  2.89 us
  transfers between devices with their start and end apart: 19, of which 8 were waited for; matrix products, arithmetic and copies ran while one was open for 1% of the time, Pallas kernels for 4%

profile of v5, /device:TPU:9, one launch (start us, length us, event | category | flops | bytes accessed | tf_op | source)
XLA Modules:
  0.0 118.0 jit_solution(10898328009575510381)
XLA Ops:
  1.3 2.9 %shard_map.95 = f32[128,40,128]{2,1,0:T(8,128)} custom-call(s32[1]{0:T(128)S(6)} %copy.10.offset, f32[128,8,256]{2,1,0:T(8,128)} %bitcast.19, f32[128,8,256]{2,1,0:T(8,128)} %bitcast.20, f32[4,128,8,256]{3,2,1,0:T(8,128)} %bitcast.18), custom_call_target="tpu_custom_call" | custom-call | bytes 5242880 | tf_op jit(solution)/shard_map/pallas_call | solution.py:132
  4.2 45.7 %all_to_all.10 = f32[128,40,128]{2,1,0:T(8,128)S(1)} all-to-all(f32[128,40,128]{2,1,0:T(8,128)} %shard_map.95), channel_id=1, replica_groups=mesh['yh'=2,'x'=4,'c'=2,'yl'=2,'z'=4] {'yh','x','c','yl','z'}, dimensions={0} | all-to-all | bytes 5242880 | tf_op jit(solution)/shard_map/all_to_all | solution.py:262
  49.9 2.0 %shard_map.96 = f32[128,24,128]{2,1,0:T(8,128)S(1)} custom-call(f32[16,8,40,128]{3,2,1,0:T(8,128)S(1)} %bitcast.13), custom_call_target="tpu_custom_call" | custom-call | flops 1048576 | bytes 4194304 | tf_op jit(solution)/shard_map/pallas_call | solution.py:178
  51.9 0.0 copy-start.1
  51.9 1.1 copy-done.1
  53.0 0.0 copy-start
  53.0 0.0 copy-start.3
  53.0 0.0 copy-start.4
  53.0 5.6 %all-to-all-start.1 = ((f32[128,24,128]{2,1,0:T(8,128)}), f32[128,24,128]{2,1,0:T(8,128)S(1)}, u32[]{:S(2)}, u32[]{:S(2)}) async-start(f32[128,24,128]{2,1,0:T(8,128)} %copy-done.1), calls=%async_computation.1 | async-start | bytes 3145728 | tf_op jit(solution)/shard_map/all_to_all | solution.py:263
  58.6 0.0 copy-done
  58.6 0.9 slice_bitcast_fusion
  59.5 3.1 %collective-permute-start.5 = (f32[4,64,256]{2,1,0:T(8,128)}, f32[4,64,256]{2,1,0:T(8,128)S(1)}, u32[]{:S(2)}, u32[]{:S(2)}) collective-permute-start(f32[4,64,256]{2,1,0:T(8,128)} %get-tuple-element.40), channel_id=1, source_target_pairs={{1,0},{2,1},{3,2},{4,3},{5,4},{6,5},{7,6},{0,7},{9,8},{10,9},{11,1... | collective-permute-start | bytes 786440 | tf_op jit(solution)/shard_map/ppermute | solution.py:35
  62.6 0.0 collective-permute-start.4
  62.6 20.1 %all-to-all-done.1.back = f32[128,24,128]{2,1,0:T(8,128)S(1)} async-done(((f32[128,24,128]{2,1,0:T(8,128)}), f32[128,24,128]{2,1,0:T(8,128)S(1)}, u32[]{:S(2)}, u32[]{:S(2)}) %all-to-all-start.1) | async-done | bytes 1572896 | tf_op jit(solution)/shard_map/all_to_all | solution.py:263
  82.8 0.8 collective-permute-start.3
  83.6 1.3 %collective-permute-start.2 = (f32[8,64,128]{2,1,0:T(8,128)S(1)}, f32[8,64,128]{2,1,0:T(8,128)S(1)}, u32[]{:S(2)}, u32[]{:S(2)}) collective-permute-start(f32[8,64,128]{2,1,0:T(8,128)S(1)} %bitcast.22), channel_id=1, source_target_pairs={{0,48},{16,0},{32,16},{48,32},{1,49},{17,1},{33,17},{49,33},{2,50}... | collective-permute-start | bytes 786440 | tf_op jit(solution)/shard_map/ppermute | solution.py:23
  84.8 0.9 collective-permute-start.1
  85.7 0.0 collective-permute-done.5.after
  85.7 0.0 collective-permute-start
  85.7 0.0 copy-done.3
  85.7 0.0 copy-done.4
  85.7 0.0 copy-start.2
  85.7 1.2 %copy-done.2 = f32[1,16,64,256]{3,2,1,0:T(8,128)S(1)} copy-done((f32[1,16,64,256]{3,2,1,0:T(8,128)S(1)}, f32[1,16,64,256]{3,2,1,0:T(8,128)}, u32[]{:S(2)}) %copy-start.2) | copy-done | bytes 1048600
  86.9 2.2 %shard_map.97 = (f32[16,64,256]{2,1,0:T(8,128)S(1)}, f32[16,64,256]{2,1,0:T(8,128)S(1)}) custom-call(f32[16,64,256]{2,1,0:T(8,128)S(1)} %bitcast.17, f32[16,64,256]{2,1,0:T(8,128)S(1)} %bitcast.14, f32[256,256]{1,0:T(8,128)S(1)} %copy-done.3, f32[64,64]{1,0:T(8,128)S(1)} %copy-done.4), custom_call_target="tpu_custom_call" | custom-call | bytes 1024 | tf_op jit(solution)/shard_map/pallas_call | solution.py:89
  89.1 0.0 collective-permute-done.4.before
  89.2 2.4 %shard_map.98 = (f32[16,64,256]{2,1,0:T(8,128)S(1)}, f32[16,64,256]{2,1,0:T(8,128)S(1)}, f32[4,64,256]{2,1,0:T(8,128)S(1)}, f32[4,64,256]{2,1,0:T(8,128)S(1)}) custom-call(f32[128,24,128]{2,1,0:T(8,128)S(1)} %all-to-all-done.1.back, f32[16,64,256]{2,1,0:T(8,128)S(1)} %get-tuple-element.21.base, f32[16,64,256]{2,1,0:T(8,128)S(1)} %get-tuple-element.22.lap, ...), custom_call_target="tpu_custom_call" | custom-call | bytes 1024 | tf_op jit(solution)/shard_map/pallas_call | solution.py:89
  91.5 0.8 collective-permute-start.6
  92.3 0.0 collective-permute-done.3.refs_7_
  92.3 2.8 %collective-permute-start.7 = (f32[4,64,256]{2,1,0:T(8,128)S(1)}, f32[4,64,256]{2,1,0:T(8,128)S(1)}, u32[]{:S(2)}, u32[]{:S(2)}) collective-permute-start(f32[4,64,256]{2,1,0:T(8,128)S(1)} %get-tuple-element.29), channel_id=1, source_target_pairs={{1,0},{2,1},{3,2},{4,3},{5,4},{6,5},{7,6},{0,7},{9,8},{10,9},{11,1... | collective-permute-start | bytes 786440 | tf_op jit(solution)/shard_map/ppermute | solution.py:35
  95.2 0.0 collective-permute-done.2.refs_5_
  95.2 0.0 collective-permute-done.1.refs_3_
  95.2 3.9 %collective-permute-done.refs_1_ = f32[8,64,128]{2,1,0:T(8,128)S(1)} collective-permute-done((f32[8,64,128]{2,1,0:T(8,128)S(1)}, f32[8,64,128]{2,1,0:T(8,128)S(1)}, u32[]{:S(2)}, u32[]{:S(2)}) %collective-permute-start) | collective-permute-done | bytes 262176 | tf_op jit(solution)/shard_map/ppermute | solution.py:23
  99.1 0.0 collective-permute-start.14
  99.1 1.5 %collective-permute-start.12 = (f32[8,64,128]{2,1,0:T(8,128)S(1)}, f32[8,64,128]{2,1,0:T(8,128)S(1)}, u32[]{:S(2)}, u32[]{:S(2)}) collective-permute-start(f32[8,64,128]{2,1,0:T(8,128)S(1)} %collective-permute-done.3.refs_7_), channel_id=1, source_target_pairs={{0,16},{16,32},{32,48},{48,0},{1,17},{17,33},{33,49},{49,1},{2,18}... | collective-permute-start | bytes 786440 | tf_op jit(solution)/shard_map/ppermute | solution.py:23
  100.6 0.0 collective-permute-start.16
  100.6 0.0 collective-permute-done.6.refs_17_
  100.6 0.0 collective-permute-done.7.refs_18_
  100.6 5.2 %collective-permute-start.8 = (f32[8,64,128]{2,1,0:T(8,128)S(1)}, f32[8,64,128]{2,1,0:T(8,128)S(1)}, u32[]{:S(2)}, u32[]{:S(2)}) collective-permute-start(f32[8,64,128]{2,1,0:T(8,128)S(1)} %collective-permute-done.refs_1_), channel_id=1, source_target_pairs={{0,8},{8,0},{1,9},{9,1},{2,10},{10,2},{3,11},{11,3},{4,12},{12,4},... | collective-permute-start | bytes 786440 | tf_op jit(solution)/shard_map/ppermute | solution.py:23
  105.7 0.1 collective-permute-start.9
  105.8 4.5 %collective-permute-done.16.refs_13_ = f32[8,64,128]{2,1,0:T(8,128)S(1)} collective-permute-done((f32[8,64,128]{2,1,0:T(8,128)S(1)}, f32[8,64,128]{2,1,0:T(8,128)S(1)}, u32[]{:S(2)}, u32[]{:S(2)}) %collective-permute-start.16) | collective-permute-done | bytes 262176 | tf_op jit(solution)/shard_map/ppermute | solution.py:23
  110.3 2.5 %collective-permute-start.10 = (f32[8,64,128]{2,1,0:T(8,128)S(1)}, f32[8,64,128]{2,1,0:T(8,128)S(1)}, u32[]{:S(2)}, u32[]{:S(2)}) collective-permute-start(f32[8,64,128]{2,1,0:T(8,128)S(1)} %collective-permute-done.2.refs_5_), channel_id=1, source_target_pairs={{0,8},{8,0},{1,9},{9,1},{2,10},{10,2},{3,11},{11,3},{4,12},{12,4},... | collective-permute-start | bytes 786440 | tf_op jit(solution)/shard_map/ppermute | solution.py:23
  112.9 0.0 collective-permute-done.14.refs_11_
  112.9 0.0 collective-permute-start.11
  112.9 0.0 collective-permute-done.12.refs_9_
  112.9 0.5 collective-permute-start.17
  113.4 0.0 collective-permute-done.8.refs_2_
  113.4 0.1 collective-permute-start.15
  113.5 0.0 collective-permute-done.9.refs_4_
  113.5 0.4 collective-permute-start.13
  113.9 0.1 collective-permute-done.10.refs_6_
  114.1 0.4 collective-permute-done.11.refs_8_
  114.4 0.4 collective-permute-done.17.refs_14_
  114.8 0.4 collective-permute-done.15.refs_12_
  115.2 0.4 collective-permute-done.13.refs_10_
  115.6 2.5 %shard_map.99 = (f32[4,16,64,256]{3,2,1,0:T(8,128)}, f32[16,64,256]{2,1,0:T(8,128)}) custom-call(f32[16,64,128]{2,1,0:T(8,128)S(1)} %bitcast.16, f32[8,64,128]{2,1,0:T(8,128)S(1)} %collective-permute-done.refs_1_, f32[8,64,128]{2,1,0:T(8,128)S(1)} %collective-permute-done.8.refs_2_, f32[8,64,128]{2,1,0:T(8,128)S(1)} %collective-permute-done.1.refs_3_, ...), custom_call_target="tpu_custom_call" | custom-call | bytes 10485760 | tf_op jit(solution)/shard_map/pallas_call | solution.py:223
  (2 shorter events, 0.1 us)
Async XLA Ops:
  51.9 1.1 copy-start.1
  53.0 5.6 %copy-start = (f32[1,16,64,256]{3,2,1,0:T(8,128)S(1)}, f32[1,16,64,256]{3,2,1,0:T(8,128)}, u32[]{:S(2)}) copy-start(f32[1,16,64,256]{3,2,1,0:T(8,128)} %param.11) | copy-start | bytes 3145732
  53.0 32.7 %copy-start.3 = (f32[256,256]{1,0:T(8,128)S(1)}, f32[256,256]{1,0:T(8,128)}, u32[]{:S(2)}) copy-start(f32[256,256]{1,0:T(8,128)} %constant.16.clone.depth) | copy-start | bytes 786436
  53.0 32.7 %copy-start.4 = (f32[64,64]{1,0:T(8,128)S(1)}, f32[64,64]{1,0:T(8,128)}, u32[]{:S(2)}) copy-start(f32[64,64]{1,0:T(8,128)} %constant.17.clone.width) | copy-start | bytes 49156
  53.0 29.7 %all-to-all-start.1 = ((f32[128,24,128]{2,1,0:T(8,128)}), f32[128,24,128]{2,1,0:T(8,128)S(1)}, u32[]{:S(2)}, u32[]{:S(2)}) async-start(f32[128,24,128]{2,1,0:T(8,128)} %copy-done.1), calls=%async_computation.1 | async-start | bytes 3145728 | tf_op jit(solution)/shard_map/all_to_all | solution.py:263
  59.5 26.2 %collective-permute-start.5 = (f32[4,64,256]{2,1,0:T(8,128)}, f32[4,64,256]{2,1,0:T(8,128)S(1)}, u32[]{:S(2)}, u32[]{:S(2)}) collective-permute-start(f32[4,64,256]{2,1,0:T(8,128)} %get-tuple-element.40), channel_id=1, source_target_pairs={{1,0},{2,1},{3,2},{4,3},{5,4},{6,5},{7,6},{0,7},{9,8},{10,9},{11,1... | collective-permute-start | bytes 786440 | tf_op jit(solution)/shard_map/ppermute | solution.py:35
  62.6 26.6 %collective-permute-start.4 = (f32[4,64,256]{2,1,0:T(8,128)}, f32[4,64,256]{2,1,0:T(8,128)S(1)}, u32[]{:S(2)}, u32[]{:S(2)}) collective-permute-start(f32[4,64,256]{2,1,0:T(8,128)} %get-tuple-element.41), channel_id=1, source_target_pairs={{0,1},{1,2},{2,3},{3,4},{4,5},{5,6},{6,7},{7,0},{8,9},{9,10},{10,1... | collective-permute-start | bytes 786440 | tf_op jit(solution)/shard_map/ppermute | solution.py:34
  82.8 9.6 %collective-permute-start.3 = (f32[8,64,128]{2,1,0:T(8,128)S(1)}, f32[8,64,128]{2,1,0:T(8,128)S(1)}, u32[]{:S(2)}, u32[]{:S(2)}) collective-permute-start(f32[8,64,128]{2,1,0:T(8,128)S(1)} %bitcast.21), channel_id=1, source_target_pairs={{0,64},{64,0},{1,65},{65,1},{2,66},{66,2},{3,67},{67,3},{4,68},{68... | collective-permute-start | bytes 786440 | tf_op jit(solution)/shard_map/ppermute | solution.py:23
  83.6 11.6 %collective-permute-start.2 = (f32[8,64,128]{2,1,0:T(8,128)S(1)}, f32[8,64,128]{2,1,0:T(8,128)S(1)}, u32[]{:S(2)}, u32[]{:S(2)}) collective-permute-start(f32[8,64,128]{2,1,0:T(8,128)S(1)} %bitcast.22), channel_id=1, source_target_pairs={{0,48},{16,0},{32,16},{48,32},{1,49},{17,1},{33,17},{49,33},{2,50}... | collective-permute-start | bytes 786440 | tf_op jit(solution)/shard_map/ppermute | solution.py:23
  84.8 10.4 %collective-permute-start.1 = (f32[8,64,128]{2,1,0:T(8,128)S(1)}, f32[8,64,128]{2,1,0:T(8,128)S(1)}, u32[]{:S(2)}, u32[]{:S(2)}) collective-permute-start(f32[8,64,128]{2,1,0:T(8,128)S(1)} %bitcast.23), channel_id=1, source_target_pairs={{0,32},{16,48},{32,0},{48,16},{1,33},{17,49},{33,1},{49,17},{2,34}... | collective-permute-start | bytes 786440 | tf_op jit(solution)/shard_map/ppermute | solution.py:23
  85.7 13.4 %collective-permute-start = (f32[8,64,128]{2,1,0:T(8,128)S(1)}, f32[8,64,128]{2,1,0:T(8,128)S(1)}, u32[]{:S(2)}, u32[]{:S(2)}) collective-permute-start(f32[8,64,128]{2,1,0:T(8,128)S(1)} %bitcast.24), channel_id=1, source_target_pairs={{0,16},{16,32},{32,48},{48,0},{1,17},{17,33},{33,49},{49,1},{2,18}... | collective-permute-start | bytes 786440 | tf_op jit(solution)/shard_map/ppermute | solution.py:23
  85.7 1.2 %copy-start.2 = (f32[1,16,64,256]{3,2,1,0:T(8,128)S(1)}, f32[1,16,64,256]{3,2,1,0:T(8,128)}, u32[]{:S(2)}) copy-start(f32[1,16,64,256]{3,2,1,0:T(8,128)} %param.10) | copy-start | bytes 3145732
  91.5 9.0 %collective-permute-start.6 = (f32[4,64,256]{2,1,0:T(8,128)S(1)}, f32[4,64,256]{2,1,0:T(8,128)S(1)}, u32[]{:S(2)}, u32[]{:S(2)}) collective-permute-start(f32[4,64,256]{2,1,0:T(8,128)S(1)} %get-tuple-element.28), channel_id=1, source_target_pairs={{0,1},{1,2},{2,3},{3,4},{4,5},{5,6},{6,7},{7,0},{8,9},{9,10},{10,1... | collective-permute-start | bytes 786440 | tf_op jit(solution)/shard_map/ppermute | solution.py:34
  92.3 8.2 %collective-permute-start.7 = (f32[4,64,256]{2,1,0:T(8,128)S(1)}, f32[4,64,256]{2,1,0:T(8,128)S(1)}, u32[]{:S(2)}, u32[]{:S(2)}) collective-permute-start(f32[4,64,256]{2,1,0:T(8,128)S(1)} %get-tuple-element.29), channel_id=1, source_target_pairs={{1,0},{2,1},{3,2},{4,3},{5,4},{6,5},{7,6},{0,7},{9,8},{10,9},{11,1... | collective-permute-start | bytes 786440 | tf_op jit(solution)/shard_map/ppermute | solution.py:35
  99.1 13.8 %collective-permute-start.14 = (f32[8,64,128]{2,1,0:T(8,128)S(1)}, f32[8,64,128]{2,1,0:T(8,128)S(1)}, u32[]{:S(2)}, u32[]{:S(2)}) collective-permute-start(f32[8,64,128]{2,1,0:T(8,128)S(1)} %collective-permute-done.3.refs_7_), channel_id=1, source_target_pairs={{0,48},{16,0},{32,16},{48,32},{1,49},{17,1},{33,17},{49,33},{2,50}... | collective-permute-start | bytes 786440 | tf_op jit(solution)/shard_map/ppermute | solution.py:23
  99.1 13.8 %collective-permute-start.12 = (f32[8,64,128]{2,1,0:T(8,128)S(1)}, f32[8,64,128]{2,1,0:T(8,128)S(1)}, u32[]{:S(2)}, u32[]{:S(2)}) collective-permute-start(f32[8,64,128]{2,1,0:T(8,128)S(1)} %collective-permute-done.3.refs_7_), channel_id=1, source_target_pairs={{0,16},{16,32},{32,48},{48,0},{1,17},{17,33},{33,49},{49,1},{2,18}... | collective-permute-start | bytes 786440 | tf_op jit(solution)/shard_map/ppermute | solution.py:23
  100.6 9.8 %collective-permute-start.16 = (f32[8,64,128]{2,1,0:T(8,128)S(1)}, f32[8,64,128]{2,1,0:T(8,128)S(1)}, u32[]{:S(2)}, u32[]{:S(2)}) collective-permute-start(f32[8,64,128]{2,1,0:T(8,128)S(1)} %collective-permute-done.1.refs_3_), channel_id=1, source_target_pairs={{0,64},{64,0},{1,65},{65,1},{2,66},{66,2},{3,67},{67,3},{4,68},{68... | collective-permute-start | bytes 786440 | tf_op jit(solution)/shard_map/ppermute | solution.py:23
  100.6 12.8 %collective-permute-start.8 = (f32[8,64,128]{2,1,0:T(8,128)S(1)}, f32[8,64,128]{2,1,0:T(8,128)S(1)}, u32[]{:S(2)}, u32[]{:S(2)}) collective-permute-start(f32[8,64,128]{2,1,0:T(8,128)S(1)} %collective-permute-done.refs_1_), channel_id=1, source_target_pairs={{0,8},{8,0},{1,9},{9,1},{2,10},{10,2},{3,11},{11,3},{4,12},{12,4},... | collective-permute-start | bytes 786440 | tf_op jit(solution)/shard_map/ppermute | solution.py:23
  105.7 7.8 %collective-permute-start.9 = (f32[8,64,128]{2,1,0:T(8,128)S(1)}, f32[8,64,128]{2,1,0:T(8,128)S(1)}, u32[]{:S(2)}, u32[]{:S(2)}) collective-permute-start(f32[8,64,128]{2,1,0:T(8,128)S(1)} %collective-permute-done.1.refs_3_), channel_id=1, source_target_pairs={{0,8},{8,0},{1,9},{9,1},{2,10},{10,2},{3,11},{11,3},{4,12},{12,4},... | collective-permute-start | bytes 786440 | tf_op jit(solution)/shard_map/ppermute | solution.py:23
  110.3 3.7 %collective-permute-start.10 = (f32[8,64,128]{2,1,0:T(8,128)S(1)}, f32[8,64,128]{2,1,0:T(8,128)S(1)}, u32[]{:S(2)}, u32[]{:S(2)}) collective-permute-start(f32[8,64,128]{2,1,0:T(8,128)S(1)} %collective-permute-done.2.refs_5_), channel_id=1, source_target_pairs={{0,8},{8,0},{1,9},{9,1},{2,10},{10,2},{3,11},{11,3},{4,12},{12,4},... | collective-permute-start | bytes 786440 | tf_op jit(solution)/shard_map/ppermute | solution.py:23
  112.9 1.5 %collective-permute-start.11 = (f32[8,64,128]{2,1,0:T(8,128)S(1)}, f32[8,64,128]{2,1,0:T(8,128)S(1)}, u32[]{:S(2)}, u32[]{:S(2)}) collective-permute-start(f32[8,64,128]{2,1,0:T(8,128)S(1)} %collective-permute-done.3.refs_7_), channel_id=1, source_target_pairs={{0,8},{8,0},{1,9},{9,1},{2,10},{10,2},{3,11},{11,3},{4,12},{12,4},... | collective-permute-start | bytes 786440 | tf_op jit(solution)/shard_map/ppermute | solution.py:23
  112.9 1.9 %collective-permute-start.17 = (f32[8,64,128]{2,1,0:T(8,128)S(1)}, f32[8,64,128]{2,1,0:T(8,128)S(1)}, u32[]{:S(2)}, u32[]{:S(2)}) collective-permute-start(f32[8,64,128]{2,1,0:T(8,128)S(1)} %collective-permute-done.16.refs_13_), channel_id=1, source_target_pairs={{0,8},{8,0},{1,9},{9,1},{2,10},{10,2},{3,11},{11,3},{4,12},{12,4},... | collective-permute-start | bytes 786440 | tf_op jit(solution)/shard_map/ppermute | solution.py:23
  113.4 1.8 %collective-permute-start.15 = (f32[8,64,128]{2,1,0:T(8,128)S(1)}, f32[8,64,128]{2,1,0:T(8,128)S(1)}, u32[]{:S(2)}, u32[]{:S(2)}) collective-permute-start(f32[8,64,128]{2,1,0:T(8,128)S(1)} %collective-permute-done.14.refs_11_), channel_id=1, source_target_pairs={{0,8},{8,0},{1,9},{9,1},{2,10},{10,2},{3,11},{11,3},{4,12},{12,4},... | collective-permute-start | bytes 786440 | tf_op jit(solution)/shard_map/ppermute | solution.py:23
  113.5 2.1 %collective-permute-start.13 = (f32[8,64,128]{2,1,0:T(8,128)S(1)}, f32[8,64,128]{2,1,0:T(8,128)S(1)}, u32[]{:S(2)}, u32[]{:S(2)}) collective-permute-start(f32[8,64,128]{2,1,0:T(8,128)S(1)} %collective-permute-done.12.refs_9_), channel_id=1, source_target_pairs={{0,8},{8,0},{1,9},{9,1},{2,10},{10,2},{3,11},{11,3},{4,12},{12,4},... | collective-permute-start | bytes 786440 | tf_op jit(solution)/shard_map/ppermute | solution.py:23

commit v6 on v5

--- a/solution.py
+++ b/solution.py
@@ -104,7 +104,7 @@
 def pack_kernel(offset, gradient, illumination, velocity, out, packed, tile, arrived, left):
     chip, c = chip_index(), lax.axis_index("c")
     half = pl.ds(pl.multiple_of(128 * lax.rem(chip, 2), 128), 128)
-    parts = [pl.ds(32 * i, 32) for i in range(4)]
+    parts = [pl.ds(16 * i, 16) for i in range(8)]
     reads = []
     for i, part in enumerate(parts):
         pairs = [(velocity.at[lax.div(chip, 2), part, :, half], tile.at[part])]
@@ -119,7 +119,7 @@
     for i, part in enumerate(parts):
         for copy in reads[i]:
             copy.wait()
-        upper = lax.broadcasted_iota(jnp.int32, (32, 8, 128), 1) // 4
+        upper = lax.broadcasted_iota(jnp.int32, (16, 8, 128), 1) // 4
         packed[part, 32:] = jnp.where(upper == c, tile[part], offset[0].astype(jnp.float32))
         writes.append(pltpu.make_async_copy(packed.at[part], out.at[part], left.at[i]))
         writes[-1].start()
@@ -137,8 +137,8 @@
         scratch_shapes=[
             pltpu.VMEM((128, 40, 128), gradient.dtype),
             pltpu.VMEM((128, 8, 128), gradient.dtype),
-            pltpu.SemaphoreType.DMA((20,)),
-            pltpu.SemaphoreType.DMA((4,)),
+            pltpu.SemaphoreType.DMA((40,)),
+            pltpu.SemaphoreType.DMA((8,)),
         ],
         cost_estimate=pl.CostEstimate(flops=0, bytes_accessed=5 << 20, transcendentals=0),
         compiler_params=pltpu.CompilerParams(vmem_limit_bytes=60 << 20),
@@ -150,13 +150,13 @@
     )
 
 
-def model_kernel(sent, out, grad, illum, marks, arrived):
-    copy = pltpu.make_async_copy(sent.at[:, 0, pl.ds(32, 8)], marks, arrived)
-    copy.start()
+def model_kernel(sent, out, grad, illum):
     grad[...] = jnp.zeros_like(grad)
     illum[...] = jnp.zeros_like(illum)
-    copy.wait()
-    offs = [marks[shot, 4 - 4 * (shot % 2), 0].astype(jnp.int32) for shot in range(16)]
+    offs = []
+    for shot in range(16):
+        row = 36 - 4 * (shot % 2)
+        offs.append(jnp.max(sent[shot, 0, row : row + 1]).astype(jnp.int32))
     for shot in range(16):
         grad[pl.ds(offs[shot], 8)] += sent[shot, :, :16]
         illum[pl.ds(offs[shot], 8)] += sent[shot, :, 16:32]
@@ -180,8 +180,7 @@
         out_shape=jax.ShapeDtypeStruct((128, 24, 128), sent.dtype),
         in_specs=[vmem],
         out_specs=vmem,
-        scratch_shapes=[pltpu.VMEM((32, 16, 128), sent.dtype)] * 2
-        + [pltpu.SMEM((16, 8, 128), sent.dtype), pltpu.SemaphoreType.DMA],
+        scratch_shapes=[pltpu.VMEM((32, 16, 128), sent.dtype)] * 2,
         cost_estimate=pl.CostEstimate(flops=1 << 20, bytes_accessed=4 << 20, transcendentals=0),
         compiler_params=pltpu.CompilerParams(vmem_limit_bytes=10 << 20),
     )(sent.reshape(16, 8, 40, 128))

time: 118 us -> 117 us (level)
  Pallas kernels: 11.9 us -> 10.5 us
    pallas_call x1, Pallas kernels: 1.99 us -> 0.49 us  [update_model(): pl.pallas_call(model_kernel, out_shape=jax.ShapeDtypeStruct((128, 24, 128...]
where the time goes in v6:
time: 117 us
  blocking collectives  45.7 us (39%)
  waiting for transfers between devices  30.2 us (26%)
  starting transfers between devices  25.5 us (22%)
  Pallas kernels  10.5 us (9%)
  local copies, waits for them, and re-layouts  3.28 us (3%)
  between operations  1.39 us (1%)
    all_to_all x1, blocking collectives, on_device(): lax.all_to_all(pack(offsets, gradient, illumination, velocity), AXES, 0, 0)  45.7 us
    all_to_all x1, waiting for transfers between devices, on_device(): back = lax.all_to_all(update_model(sent), AXES, 0, 0)  20.1 us
    ppermute x14, starting transfers between devices, rotate(): lax.ppermute(value, axis, [(i, (i + steps) % count) for i in range(count)])  13.2 us
    ppermute x14, waiting for transfers between devices, rotate(): lax.ppermute(value, axis, [(i, (i + steps) % count) for i in range(count)])  10.1 us
    ppermute x2, starting transfers between devices, halo(): after = lax.ppermute(first, SLAB, [((i + 1) % 8, i) for i in range(8)])  5.98 us
    all_to_all x1, starting transfers between devices, on_device(): back = lax.all_to_all(update_model(sent), AXES, 0, 0)  5.56 us
    pallas_call x2, Pallas kernels, on_slab(): pl.pallas_call(kernel, out_shape=[jax.ShapeDtypeStruct((planes, 64, 256),...  4.59 us
    pallas_call x1, Pallas kernels, pack(): pl.pallas_call(pack_kernel, out_shape=jax.ShapeDtypeStruct((128, 40, 128)...  2.93 us
  transfers between devices with their start and end apart: 19, of which 8 were waited for; matrix products, arithmetic and copies ran while one was open for 1% of the time, Pallas kernels for 4%

profile of v6, /device:TPU:9, one launch (start us, length us, event | category | flops | bytes accessed | tf_op | source)
XLA Modules:
  0.0 116.6 jit_solution(7038774990324021484)
XLA Ops:
  1.3 2.9 %shard_map.95 = f32[128,40,128]{2,1,0:T(8,128)} custom-call(s32[1]{0:T(128)S(6)} %copy.10.offset, f32[128,8,256]{2,1,0:T(8,128)} %bitcast.19, f32[128,8,256]{2,1,0:T(8,128)} %bitcast.20, f32[4,128,8,256]{3,2,1,0:T(8,128)} %bitcast.18), custom_call_target="tpu_custom_call" | custom-call | bytes 5242880 | tf_op jit(solution)/shard_map/pallas_call | solution.py:132
  4.2 45.7 %all_to_all.10 = f32[128,40,128]{2,1,0:T(8,128)S(1)} all-to-all(f32[128,40,128]{2,1,0:T(8,128)} %shard_map.95), channel_id=1, replica_groups=mesh['yh'=2,'x'=4,'c'=2,'yl'=2,'z'=4] {'yh','x','c','yl','z'}, dimensions={0} | all-to-all | bytes 5242880 | tf_op jit(solution)/shard_map/all_to_all | solution.py:261
  49.9 0.5 shard_map.96
  50.4 0.0 copy-start.1
  50.4 1.1 copy-done.1
  51.6 0.0 copy-start
  51.6 0.0 copy-start.3
  51.6 0.0 copy-start.4
  51.6 5.6 %all-to-all-start.1 = ((f32[128,24,128]{2,1,0:T(8,128)}), f32[128,24,128]{2,1,0:T(8,128)S(1)}, u32[]{:S(2)}, u32[]{:S(2)}) async-start(f32[128,24,128]{2,1,0:T(8,128)} %copy-done.1), calls=%async_computation.1 | async-start | bytes 3145728 | tf_op jit(solution)/shard_map/all_to_all | solution.py:262
  57.1 0.0 copy-done
  57.1 0.9 slice_bitcast_fusion
  58.0 3.1 %collective-permute-start.5 = (f32[4,64,256]{2,1,0:T(8,128)}, f32[4,64,256]{2,1,0:T(8,128)S(1)}, u32[]{:S(2)}, u32[]{:S(2)}) collective-permute-start(f32[4,64,256]{2,1,0:T(8,128)} %get-tuple-element.40), channel_id=1, source_target_pairs={{1,0},{2,1},{3,2},{4,3},{5,4},{6,5},{7,6},{0,7},{9,8},{10,9},{11,1... | collective-permute-start | bytes 786440 | tf_op jit(solution)/shard_map/ppermute | solution.py:35
  61.1 0.0 collective-permute-start.4
  61.1 20.1 %all-to-all-done.1.back = f32[128,24,128]{2,1,0:T(8,128)S(1)} async-done(((f32[128,24,128]{2,1,0:T(8,128)}), f32[128,24,128]{2,1,0:T(8,128)S(1)}, u32[]{:S(2)}, u32[]{:S(2)}) %all-to-all-start.1) | async-done | bytes 1572896 | tf_op jit(solution)/shard_map/all_to_all | solution.py:262
  81.3 0.8 collective-permute-start.3
  82.1 1.3 %collective-permute-start.2 = (f32[8,64,128]{2,1,0:T(8,128)S(1)}, f32[8,64,128]{2,1,0:T(8,128)S(1)}, u32[]{:S(2)}, u32[]{:S(2)}) collective-permute-start(f32[8,64,128]{2,1,0:T(8,128)S(1)} %bitcast.22), channel_id=1, source_target_pairs={{0,48},{16,0},{32,16},{48,32},{1,49},{17,1},{33,17},{49,33},{2,50}... | collective-permute-start | bytes 786440 | tf_op jit(solution)/shard_map/ppermute | solution.py:23
  83.4 0.9 collective-permute-start.1
  84.2 0.0 collective-permute-done.5.after
  84.2 0.0 collective-permute-start
  84.2 0.0 copy-done.3
  84.2 0.0 copy-done.4
  84.2 0.0 copy-start.2
  84.3 1.2 %copy-done.2 = f32[1,16,64,256]{3,2,1,0:T(8,128)S(1)} copy-done((f32[1,16,64,256]{3,2,1,0:T(8,128)S(1)}, f32[1,16,64,256]{3,2,1,0:T(8,128)}, u32[]{:S(2)}) %copy-start.2) | copy-done | bytes 1048600
  85.5 2.2 %shard_map.97 = (f32[16,64,256]{2,1,0:T(8,128)S(1)}, f32[16,64,256]{2,1,0:T(8,128)S(1)}) custom-call(f32[16,64,256]{2,1,0:T(8,128)S(1)} %bitcast.17, f32[16,64,256]{2,1,0:T(8,128)S(1)} %bitcast.14, f32[256,256]{1,0:T(8,128)S(1)} %copy-done.3, f32[64,64]{1,0:T(8,128)S(1)} %copy-done.4), custom_call_target="tpu_custom_call" | custom-call | bytes 1024 | tf_op jit(solution)/shard_map/pallas_call | solution.py:89
  87.7 0.0 collective-permute-done.4.before
  87.7 2.4 %shard_map.98 = (f32[16,64,256]{2,1,0:T(8,128)S(1)}, f32[16,64,256]{2,1,0:T(8,128)S(1)}, f32[4,64,256]{2,1,0:T(8,128)S(1)}, f32[4,64,256]{2,1,0:T(8,128)S(1)}) custom-call(f32[128,24,128]{2,1,0:T(8,128)S(1)} %all-to-all-done.1.back, f32[16,64,256]{2,1,0:T(8,128)S(1)} %get-tuple-element.21.base, f32[16,64,256]{2,1,0:T(8,128)S(1)} %get-tuple-element.22.lap, ...), custom_call_target="tpu_custom_call" | custom-call | bytes 1024 | tf_op jit(solution)/shard_map/pallas_call | solution.py:89
  90.1 0.8 collective-permute-start.6
  90.9 0.0 collective-permute-done.3.refs_7_
  90.9 2.8 %collective-permute-start.7 = (f32[4,64,256]{2,1,0:T(8,128)S(1)}, f32[4,64,256]{2,1,0:T(8,128)S(1)}, u32[]{:S(2)}, u32[]{:S(2)}) collective-permute-start(f32[4,64,256]{2,1,0:T(8,128)S(1)} %get-tuple-element.29), channel_id=1, source_target_pairs={{1,0},{2,1},{3,2},{4,3},{5,4},{6,5},{7,6},{0,7},{9,8},{10,9},{11,1... | collective-permute-start | bytes 786440 | tf_op jit(solution)/shard_map/ppermute | solution.py:35
  93.7 0.0 collective-permute-done.2.refs_5_
  93.7 0.0 collective-permute-done.1.refs_3_
  93.7 3.9 %collective-permute-done.refs_1_ = f32[8,64,128]{2,1,0:T(8,128)S(1)} collective-permute-done((f32[8,64,128]{2,1,0:T(8,128)S(1)}, f32[8,64,128]{2,1,0:T(8,128)S(1)}, u32[]{:S(2)}, u32[]{:S(2)}) %collective-permute-start) | collective-permute-done | bytes 262176 | tf_op jit(solution)/shard_map/ppermute | solution.py:23
  97.6 0.0 collective-permute-start.14
  97.6 1.5 %collective-permute-start.12 = (f32[8,64,128]{2,1,0:T(8,128)S(1)}, f32[8,64,128]{2,1,0:T(8,128)S(1)}, u32[]{:S(2)}, u32[]{:S(2)}) collective-permute-start(f32[8,64,128]{2,1,0:T(8,128)S(1)} %collective-permute-done.3.refs_7_), channel_id=1, source_target_pairs={{0,16},{16,32},{32,48},{48,0},{1,17},{17,33},{33,49},{49,1},{2,18}... | collective-permute-start | bytes 786440 | tf_op jit(solution)/shard_map/ppermute | solution.py:23
  99.1 0.0 collective-permute-start.16
  99.1 0.0 collective-permute-done.6.refs_17_
  99.1 0.0 collective-permute-done.7.refs_18_
  99.1 5.2 %collective-permute-start.8 = (f32[8,64,128]{2,1,0:T(8,128)S(1)}, f32[8,64,128]{2,1,0:T(8,128)S(1)}, u32[]{:S(2)}, u32[]{:S(2)}) collective-permute-start(f32[8,64,128]{2,1,0:T(8,128)S(1)} %collective-permute-done.refs_1_), channel_id=1, source_target_pairs={{0,8},{8,0},{1,9},{9,1},{2,10},{10,2},{3,11},{11,3},{4,12},{12,4},... | collective-permute-start | bytes 786440 | tf_op jit(solution)/shard_map/ppermute | solution.py:23
  104.3 0.1 collective-permute-start.9
  104.4 4.5 %collective-permute-done.16.refs_13_ = f32[8,64,128]{2,1,0:T(8,128)S(1)} collective-permute-done((f32[8,64,128]{2,1,0:T(8,128)S(1)}, f32[8,64,128]{2,1,0:T(8,128)S(1)}, u32[]{:S(2)}, u32[]{:S(2)}) %collective-permute-start.16) | collective-permute-done | bytes 262176 | tf_op jit(solution)/shard_map/ppermute | solution.py:23
  108.9 2.5 %collective-permute-start.10 = (f32[8,64,128]{2,1,0:T(8,128)S(1)}, f32[8,64,128]{2,1,0:T(8,128)S(1)}, u32[]{:S(2)}, u32[]{:S(2)}) collective-permute-start(f32[8,64,128]{2,1,0:T(8,128)S(1)} %collective-permute-done.2.refs_5_), channel_id=1, source_target_pairs={{0,8},{8,0},{1,9},{9,1},{2,10},{10,2},{3,11},{11,3},{4,12},{12,4},... | collective-permute-start | bytes 786440 | tf_op jit(solution)/shard_map/ppermute | solution.py:23
  111.4 0.0 collective-permute-done.14.refs_11_
  111.4 0.0 collective-permute-start.11
  111.4 0.0 collective-permute-done.12.refs_9_
  111.4 0.5 collective-permute-start.17
  112.0 0.0 collective-permute-done.8.refs_2_
  112.0 0.1 collective-permute-start.15
  112.0 0.0 collective-permute-done.9.refs_4_
  112.0 0.4 collective-permute-start.13
  112.5 0.1 collective-permute-done.10.refs_6_
  112.6 0.4 collective-permute-done.11.refs_8_
  113.0 0.4 collective-permute-done.17.refs_14_
  113.3 0.4 collective-permute-done.15.refs_12_
  113.7 0.4 collective-permute-done.13.refs_10_
  114.1 2.5 %shard_map.99 = (f32[4,16,64,256]{3,2,1,0:T(8,128)}, f32[16,64,256]{2,1,0:T(8,128)}) custom-call(f32[16,64,128]{2,1,0:T(8,128)S(1)} %bitcast.16, f32[8,64,128]{2,1,0:T(8,128)S(1)} %collective-permute-done.refs_1_, f32[8,64,128]{2,1,0:T(8,128)S(1)} %collective-permute-done.8.refs_2_, f32[8,64,128]{2,1,0:T(8,128)S(1)} %collective-permute-done.1.refs_3_, ...), custom_call_target="tpu_custom_call" | custom-call | bytes 10485760 | tf_op jit(solution)/shard_map/pallas_call | solution.py:222
  (2 shorter events, 0.1 us)
Async XLA Ops:
  50.4 1.1 copy-start.1
  51.6 5.6 %copy-start = (f32[1,16,64,256]{3,2,1,0:T(8,128)S(1)}, f32[1,16,64,256]{3,2,1,0:T(8,128)}, u32[]{:S(2)}) copy-start(f32[1,16,64,256]{3,2,1,0:T(8,128)} %param.11) | copy-start | bytes 3145732
  51.6 32.7 %copy-start.3 = (f32[256,256]{1,0:T(8,128)S(1)}, f32[256,256]{1,0:T(8,128)}, u32[]{:S(2)}) copy-start(f32[256,256]{1,0:T(8,128)} %constant.16.clone.depth) | copy-start | bytes 786436
  51.6 32.7 %copy-start.4 = (f32[64,64]{1,0:T(8,128)S(1)}, f32[64,64]{1,0:T(8,128)}, u32[]{:S(2)}) copy-start(f32[64,64]{1,0:T(8,128)} %constant.17.clone.width) | copy-start | bytes 49156
  51.6 29.7 %all-to-all-start.1 = ((f32[128,24,128]{2,1,0:T(8,128)}), f32[128,24,128]{2,1,0:T(8,128)S(1)}, u32[]{:S(2)}, u32[]{:S(2)}) async-start(f32[128,24,128]{2,1,0:T(8,128)} %copy-done.1), calls=%async_computation.1 | async-start | bytes 3145728 | tf_op jit(solution)/shard_map/all_to_all | solution.py:262
  58.0 26.2 %collective-permute-start.5 = (f32[4,64,256]{2,1,0:T(8,128)}, f32[4,64,256]{2,1,0:T(8,128)S(1)}, u32[]{:S(2)}, u32[]{:S(2)}) collective-permute-start(f32[4,64,256]{2,1,0:T(8,128)} %get-tuple-element.40), channel_id=1, source_target_pairs={{1,0},{2,1},{3,2},{4,3},{5,4},{6,5},{7,6},{0,7},{9,8},{10,9},{11,1... | collective-permute-start | bytes 786440 | tf_op jit(solution)/shard_map/ppermute | solution.py:35
  61.1 26.6 %collective-permute-start.4 = (f32[4,64,256]{2,1,0:T(8,128)}, f32[4,64,256]{2,1,0:T(8,128)S(1)}, u32[]{:S(2)}, u32[]{:S(2)}) collective-permute-start(f32[4,64,256]{2,1,0:T(8,128)} %get-tuple-element.41), channel_id=1, source_target_pairs={{0,1},{1,2},{2,3},{3,4},{4,5},{5,6},{6,7},{7,0},{8,9},{9,10},{10,1... | collective-permute-start | bytes 786440 | tf_op jit(solution)/shard_map/ppermute | solution.py:34
  81.3 9.6 %collective-permute-start.3 = (f32[8,64,128]{2,1,0:T(8,128)S(1)}, f32[8,64,128]{2,1,0:T(8,128)S(1)}, u32[]{:S(2)}, u32[]{:S(2)}) collective-permute-start(f32[8,64,128]{2,1,0:T(8,128)S(1)} %bitcast.21), channel_id=1, source_target_pairs={{0,64},{64,0},{1,65},{65,1},{2,66},{66,2},{3,67},{67,3},{4,68},{68... | collective-permute-start | bytes 786440 | tf_op jit(solution)/shard_map/ppermute | solution.py:23
  82.1 11.6 %collective-permute-start.2 = (f32[8,64,128]{2,1,0:T(8,128)S(1)}, f32[8,64,128]{2,1,0:T(8,128)S(1)}, u32[]{:S(2)}, u32[]{:S(2)}) collective-permute-start(f32[8,64,128]{2,1,0:T(8,128)S(1)} %bitcast.22), channel_id=1, source_target_pairs={{0,48},{16,0},{32,16},{48,32},{1,49},{17,1},{33,17},{49,33},{2,50}... | collective-permute-start | bytes 786440 | tf_op jit(solution)/shard_map/ppermute | solution.py:23
  83.4 10.4 %collective-permute-start.1 = (f32[8,64,128]{2,1,0:T(8,128)S(1)}, f32[8,64,128]{2,1,0:T(8,128)S(1)}, u32[]{:S(2)}, u32[]{:S(2)}) collective-permute-start(f32[8,64,128]{2,1,0:T(8,128)S(1)} %bitcast.23), channel_id=1, source_target_pairs={{0,32},{16,48},{32,0},{48,16},{1,33},{17,49},{33,1},{49,17},{2,34}... | collective-permute-start | bytes 786440 | tf_op jit(solution)/shard_map/ppermute | solution.py:23
  84.2 13.4 %collective-permute-start = (f32[8,64,128]{2,1,0:T(8,128)S(1)}, f32[8,64,128]{2,1,0:T(8,128)S(1)}, u32[]{:S(2)}, u32[]{:S(2)}) collective-permute-start(f32[8,64,128]{2,1,0:T(8,128)S(1)} %bitcast.24), channel_id=1, source_target_pairs={{0,16},{16,32},{32,48},{48,0},{1,17},{17,33},{33,49},{49,1},{2,18}... | collective-permute-start | bytes 786440 | tf_op jit(solution)/shard_map/ppermute | solution.py:23
  84.2 1.2 %copy-start.2 = (f32[1,16,64,256]{3,2,1,0:T(8,128)S(1)}, f32[1,16,64,256]{3,2,1,0:T(8,128)}, u32[]{:S(2)}) copy-start(f32[1,16,64,256]{3,2,1,0:T(8,128)} %param.10) | copy-start | bytes 3145732
  90.1 9.0 %collective-permute-start.6 = (f32[4,64,256]{2,1,0:T(8,128)S(1)}, f32[4,64,256]{2,1,0:T(8,128)S(1)}, u32[]{:S(2)}, u32[]{:S(2)}) collective-permute-start(f32[4,64,256]{2,1,0:T(8,128)S(1)} %get-tuple-element.28), channel_id=1, source_target_pairs={{0,1},{1,2},{2,3},{3,4},{4,5},{5,6},{6,7},{7,0},{8,9},{9,10},{10,1... | collective-permute-start | bytes 786440 | tf_op jit(solution)/shard_map/ppermute | solution.py:34
  90.9 8.2 %collective-permute-start.7 = (f32[4,64,256]{2,1,0:T(8,128)S(1)}, f32[4,64,256]{2,1,0:T(8,128)S(1)}, u32[]{:S(2)}, u32[]{:S(2)}) collective-permute-start(f32[4,64,256]{2,1,0:T(8,128)S(1)} %get-tuple-element.29), channel_id=1, source_target_pairs={{1,0},{2,1},{3,2},{4,3},{5,4},{6,5},{7,6},{0,7},{9,8},{10,9},{11,1... | collective-permute-start | bytes 786440 | tf_op jit(solution)/shard_map/ppermute | solution.py:35
  97.6 13.8 %collective-permute-start.14 = (f32[8,64,128]{2,1,0:T(8,128)S(1)}, f32[8,64,128]{2,1,0:T(8,128)S(1)}, u32[]{:S(2)}, u32[]{:S(2)}) collective-permute-start(f32[8,64,128]{2,1,0:T(8,128)S(1)} %collective-permute-done.3.refs_7_), channel_id=1, source_target_pairs={{0,48},{16,0},{32,16},{48,32},{1,49},{17,1},{33,17},{49,33},{2,50}... | collective-permute-start | bytes 786440 | tf_op jit(solution)/shard_map/ppermute | solution.py:23
  97.6 13.8 %collective-permute-start.12 = (f32[8,64,128]{2,1,0:T(8,128)S(1)}, f32[8,64,128]{2,1,0:T(8,128)S(1)}, u32[]{:S(2)}, u32[]{:S(2)}) collective-permute-start(f32[8,64,128]{2,1,0:T(8,128)S(1)} %collective-permute-done.3.refs_7_), channel_id=1, source_target_pairs={{0,16},{16,32},{32,48},{48,0},{1,17},{17,33},{33,49},{49,1},{2,18}... | collective-permute-start | bytes 786440 | tf_op jit(solution)/shard_map/ppermute | solution.py:23
  99.1 9.8 %collective-permute-start.16 = (f32[8,64,128]{2,1,0:T(8,128)S(1)}, f32[8,64,128]{2,1,0:T(8,128)S(1)}, u32[]{:S(2)}, u32[]{:S(2)}) collective-permute-start(f32[8,64,128]{2,1,0:T(8,128)S(1)} %collective-permute-done.1.refs_3_), channel_id=1, source_target_pairs={{0,64},{64,0},{1,65},{65,1},{2,66},{66,2},{3,67},{67,3},{4,68},{68... | collective-permute-start | bytes 786440 | tf_op jit(solution)/shard_map/ppermute | solution.py:23
  99.1 12.8 %collective-permute-start.8 = (f32[8,64,128]{2,1,0:T(8,128)S(1)}, f32[8,64,128]{2,1,0:T(8,128)S(1)}, u32[]{:S(2)}, u32[]{:S(2)}) collective-permute-start(f32[8,64,128]{2,1,0:T(8,128)S(1)} %collective-permute-done.refs_1_), channel_id=1, source_target_pairs={{0,8},{8,0},{1,9},{9,1},{2,10},{10,2},{3,11},{11,3},{4,12},{12,4},... | collective-permute-start | bytes 786440 | tf_op jit(solution)/shard_map/ppermute | solution.py:23
  104.3 7.8 %collective-permute-start.9 = (f32[8,64,128]{2,1,0:T(8,128)S(1)}, f32[8,64,128]{2,1,0:T(8,128)S(1)}, u32[]{:S(2)}, u32[]{:S(2)}) collective-permute-start(f32[8,64,128]{2,1,0:T(8,128)S(1)} %collective-permute-done.1.refs_3_), channel_id=1, source_target_pairs={{0,8},{8,0},{1,9},{9,1},{2,10},{10,2},{3,11},{11,3},{4,12},{12,4},... | collective-permute-start | bytes 786440 | tf_op jit(solution)/shard_map/ppermute | solution.py:23
  108.9 3.7 %collective-permute-start.10 = (f32[8,64,128]{2,1,0:T(8,128)S(1)}, f32[8,64,128]{2,1,0:T(8,128)S(1)}, u32[]{:S(2)}, u32[]{:S(2)}) collective-permute-start(f32[8,64,128]{2,1,0:T(8,128)S(1)} %collective-permute-done.2.refs_5_), channel_id=1, source_target_pairs={{0,8},{8,0},{1,9},{9,1},{2,10},{10,2},{3,11},{11,3},{4,12},{12,4},... | collective-permute-start | bytes 786440 | tf_op jit(solution)/shard_map/ppermute | solution.py:23
  111.4 1.5 %collective-permute-start.11 = (f32[8,64,128]{2,1,0:T(8,128)S(1)}, f32[8,64,128]{2,1,0:T(8,128)S(1)}, u32[]{:S(2)}, u32[]{:S(2)}) collective-permute-start(f32[8,64,128]{2,1,0:T(8,128)S(1)} %collective-permute-done.3.refs_7_), channel_id=1, source_target_pairs={{0,8},{8,0},{1,9},{9,1},{2,10},{10,2},{3,11},{11,3},{4,12},{12,4},... | collective-permute-start | bytes 786440 | tf_op jit(solution)/shard_map/ppermute | solution.py:23
  111.4 1.9 %collective-permute-start.17 = (f32[8,64,128]{2,1,0:T(8,128)S(1)}, f32[8,64,128]{2,1,0:T(8,128)S(1)}, u32[]{:S(2)}, u32[]{:S(2)}) collective-permute-start(f32[8,64,128]{2,1,0:T(8,128)S(1)} %collective-permute-done.16.refs_13_), channel_id=1, source_target_pairs={{0,8},{8,0},{1,9},{9,1},{2,10},{10,2},{3,11},{11,3},{4,12},{12,4},... | collective-permute-start | bytes 786440 | tf_op jit(solution)/shard_map/ppermute | solution.py:23
  112.0 1.8 %collective-permute-start.15 = (f32[8,64,128]{2,1,0:T(8,128)S(1)}, f32[8,64,128]{2,1,0:T(8,128)S(1)}, u32[]{:S(2)}, u32[]{:S(2)}) collective-permute-start(f32[8,64,128]{2,1,0:T(8,128)S(1)} %collective-permute-done.14.refs_11_), channel_id=1, source_target_pairs={{0,8},{8,0},{1,9},{9,1},{2,10},{10,2},{3,11},{11,3},{4,12},{12,4},... | collective-permute-start | bytes 786440 | tf_op jit(solution)/shard_map/ppermute | solution.py:23
  112.0 2.1 %collective-permute-start.13 = (f32[8,64,128]{2,1,0:T(8,128)S(1)}, f32[8,64,128]{2,1,0:T(8,128)S(1)}, u32[]{:S(2)}, u32[]{:S(2)}) collective-permute-start(f32[8,64,128]{2,1,0:T(8,128)S(1)} %collective-permute-done.12.refs_9_), channel_id=1, source_target_pairs={{0,8},{8,0},{1,9},{9,1},{2,10},{10,2},{3,11},{11,3},{4,12},{12,4},... | collective-permute-start | bytes 786440 | tf_op jit(solution)/shard_map/ppermute | solution.py:23
